TPU v7x, 32 devices: a whole 2x2x4 slice. The times are simulated.
32 devices in a mesh: tm: 4 (over y, x), space: 8 (over z, core).
Axes of the slice: x: 2, y: 2, z: 4, core: 2. Of those that a mesh axis runs over, the one named last changes fastest.
Arguments:
- iterate: float32 [64, 5, 16384], P('tm', None, 'space'), may hold values from -6 to 6
- right_side: float32 [64, 5, 16384], P('tm', None, 'space'), may hold values from -6 to 6
- jacobian: float32 [6, 5, 5, 16384], P(None, None, None, 'space'), may hold values from -0.24 to 0.24
- self_block: float32 [5, 5, 16384], P(None, None, 'space'), may hold values from -0.48 to 0.48
- cell_diag: float32 [5, 16384], P(None, 'space'), may hold values from 2.5 to 5
- neighbours: int32 [128, 6], P('space'), may hold values from 0 to 31, as said below
- face_list: int32 [64], P('space'), may hold values from 0 to 15, as said below
Outputs:
- updated: float32 [64, 5, 16384], P('tm', None, 'space')
- residual: float32 [64, 5, 16384], P('tm', None, 'space')
Inputs may be any that keep to these rules, and one draw needn't show every extreme that they name: `neighbours`: row b of slab s names 6 blocks in slab s's extended numbering: 0 to 15 its own blocks, 16 + h the h-th face block of slab s-1, 24 + h the h-th face block of slab s+1. Entry 0 always names a face block of the lower slab, entry 1 one of the upper slab, entries 2 to 5 own blocks. `face_list`: each slab's 8 entries are distinct local blocks of that slab; the last entry is always the slab's last block.
All inputs are finite; a program needn't handle non-finite values.
Results may differ from a plain program's by a relative error of at most 0.0001.
Values sent between devices are 32-bit elements; how exact they have to be, the bound alone decides.
No kernel may reach another device: no remote copies, remote signals or barrier semaphores. Data moves between devices by JAX's collectives and lax.ppermute only.
A program may use at most 64 MiB of HBM per device.

v0:
```python
import functools

import jax
import jax.numpy as jnp
from jax import lax
from jax.experimental import pallas as pl
from jax.experimental.pallas import tpu as pltpu
from jax.sharding import PartitionSpec as P

NV = 5
BLK = 128
K = 6
NU1 = 2
NU2 = 2
NUC = 4
GROUP = 4

time_weight = 0.5
coarse_weight = time_weight / GROUP
damping = 0.7

UNROLL = 2
SCRATCH_BYTES = 4 << 20
IN_VMEM = pl.BlockSpec(memory_space=pltpu.VMEM)
IN_SMEM = pl.BlockSpec(memory_space=pltpu.SMEM)


def call(kernel, name, tables, arrays, outs, flops=0, scratch=(), out_specs=None):
    arrays = [pltpu.with_memory_space_constraint(a, pltpu.VMEM) for a in arrays]
    size = 4 * (sum(a.size for a in arrays) + sum(o.size for o in outs))
    return pl.pallas_call(
        kernel,
        out_shape=outs if out_specs else [pltpu.VMEM(o.shape, o.dtype) for o in outs],
        in_specs=[IN_SMEM] * len(tables) + [IN_VMEM] * len(arrays),
        out_specs=out_specs or [IN_VMEM] * len(outs),
        scratch_shapes=scratch,
        cost_estimate=pl.CostEstimate(flops=flops, bytes_accessed=size, transcendentals=0),
        compiler_params=pltpu.CompilerParams(vmem_limit_bytes=SCRATCH_BYTES),
        name=name,
    )(*tables, *arrays)


def shape(*dims):
    return jax.ShapeDtypeStruct(dims, jnp.float32)


def lanes_of(b):
    return pl.ds(pl.multiple_of(b * BLK, BLK), BLK)


def cross_slot():
    return lax.rem(lax.axis_index("space"), 2)


def each_block(count, step):
    unroll = UNROLL if count % UNROLL == 0 else 1

    def steps(i, carry):
        for u in range(unroll):
            step(i * unroll + u, u)
        return carry

    lax.fori_loop(0, count // unroll, steps, 0)


def table_kernel(neighbours, face_list, table, listed):
    slot = cross_slot()
    slots, blocks = neighbours.shape
    faces = face_list.shape[0]

    def step(b, carry):
        table[0, b] = neighbours[slot, b] - (blocks + faces * slot)
        table[1, b] = neighbours[1 - slot, b] - (blocks + faces * (1 - slot))
        for k in range(2, slots):
            table[k, b] = neighbours[k, b]
        return carry

    lax.fori_loop(0, blocks, step, 0)
    for h in range(faces):
        listed[h] = face_list[h]


def points_kernel(cell_diag, fine_out, coarse_out):
    fine_out[...] = damping / (3.0 * time_weight + cell_diag[...])
    coarse_out[...] = damping / (3.0 * coarse_weight + cell_diag[...])


def rim_jacobian_kernel(jacobian, out):
    lower_crosses = cross_slot() == 0
    for a in range(NV):
        for j in range(NV):
            lower, upper = jacobian[a, j, pl.ds(0, 1), :], jacobian[a, j, pl.ds(1, 1), :]
            out[0, a, pl.ds(j, 1), :] = jnp.where(lower_crosses, lower, upper)
            out[1, a, pl.ds(j, 1), :] = jnp.where(lower_crosses, upper, lower)


def coupled(total, coupling, values):
    for j in range(NV):
        for a in range(NV):
            total[a] = total[a] - coupling(a, j) * values[j]
    return total


def earlier(v, steps):
    if v.shape[0] <= steps:
        return jnp.zeros_like(v)
    return jnp.concatenate([jnp.zeros((steps, BLK), jnp.float32), v[: v.shape[0] - steps]], axis=0)


def own_part(total, b, field, rim, table, jacobian, rim_jacobian, self_block):
    lanes = lanes_of(b)
    v = [field[j, :, lanes] for j in range(NV)]
    for a in range(NV):
        for j in range(NV):
            if j != a:
                total[a] = total[a] - self_block[a, pl.ds(j, 1), lanes] * v[j]
    for slot in range(2, K):
        there = lanes_of(table[slot, b])
        row = pl.ds(slot, 1)
        total = coupled(total, lambda a, j: jacobian[a, j, row, lanes], [field[j, :, there] for j in range(NV)])
    return rim_part(1, total, b, rim, table, rim_jacobian)


def rim_part(side, total, b, rim, table, rim_jacobian):
    block, lanes = table[side, b], lanes_of(b)
    coupling = lambda a, j: rim_jacobian[side, a, pl.ds(j, 1), lanes]
    return coupled(total, coupling, [rim[block, j] for j in range(NV)])


def faces_kernel(listed, field, faces_out):
    for h in range(faces_out.shape[0]):
        lanes = lanes_of(listed[h])
        for a in range(NV):
            faces_out[h, a] = field[a, :, lanes]


def tail_kernel(weight, field, tail_out):
    steps = field.shape[1]
    for a in range(NV):
        last = field[a, pl.ds(steps - 1, 1), :]
        tail_out[a, pl.ds(0, 1), :] = weight * (field[a, pl.ds(steps - 2, 1), :] - 4.0 * last)
        tail_out[a, pl.ds(1, 1), :] = weight * last


def own_kernel(weight, table, field, goal, rim, jacobian, rim_jacobian, self_block, cell_diag, out):
    def step(b, u):
        lanes = lanes_of(b)
        total = []
        for a in range(NV):
            v = field[a, :, lanes]
            point = 3.0 * weight + cell_diag[pl.ds(a, 1), lanes]
            timed = weight * (earlier(v, 2) - 4.0 * earlier(v, 1))
            total.append(goal[a, :, lanes] - point * v - timed)
        total = own_part(total, b, field, rim, table, jacobian, rim_jacobian, self_block)
        for a in range(NV):
            out[a, :, lanes] = total[a]

    each_block(table.shape[1], step)


def mean_rows(v, scratch, steps):
    scratch[...] = v
    return sum(scratch[pl.ds(i, steps, stride=GROUP), :] for i in range(GROUP)) * (1.0 / GROUP)


def means_kernel(weight, table, field, goal, means, rim, jacobian, rim_jacobian, self_block, cell_diag, out, scratch):
    steps = means.shape[1]

    def step(b, u):
        lanes = lanes_of(b)
        total = []
        for a in range(NV):
            v = field[a, :, lanes]
            fine = goal[a, :, lanes] - weight * (3.0 * v - 4.0 * earlier(v, 1) + earlier(v, 2))
            total.append(mean_rows(fine, scratch.at[u, a], steps) - cell_diag[pl.ds(a, 1), lanes] * means[a, :, lanes])
        total = own_part(total, b, means, rim, table, jacobian, rim_jacobian, self_block)
        for a in range(NV):
            out[a, :, lanes] = total[a]

    each_block(table.shape[1], step)


def less_rows(total, rows):
    pad = total.shape[0] - rows.shape[0]
    if pad:
        rows = jnp.concatenate([rows, jnp.zeros((pad, BLK), jnp.float32)], axis=0)
    return total - rows


def rest_part(b, part, rim, tail, table, rim_jacobian):
    lanes = lanes_of(b)
    total = [less_rows(part[a, :, lanes], tail[a, :, lanes]) for a in range(NV)]
    return rim_part(0, total, b, rim, table, rim_jacobian)


def sweep_kernel(table, listed, field, part, rim, tail, rim_jacobian, points, out, faces_out):
    def step(b, u):
        lanes = lanes_of(b)
        total = rest_part(b, part, rim, tail, table, rim_jacobian)
        for a in range(NV):
            out[a, :, lanes] = field[a, :, lanes] + points[pl.ds(a, 1), lanes] * total[a]

    each_block(table.shape[1], step)
    faces_kernel(listed, out, faces_out)


def smoothed_kernel(table, listed, field, part, rim, tail, rim_jacobian, points, out, means_out, faces_out, scratch):
    steps = means_out.shape[1]

    def step(b, u):
        lanes = lanes_of(b)
        total = rest_part(b, part, rim, tail, table, rim_jacobian)
        for a in range(NV):
            v = field[a, :, lanes] + points[pl.ds(a, 1), lanes] * total[a]
            out[a, :, lanes] = v
            means_out[a, :, lanes] = mean_rows(v, scratch.at[u, a], steps)

    each_block(table.shape[1], step)
    faces_kernel(listed, means_out, faces_out)


def first_correction_kernel(table, listed, part, rim, tail, rim_jacobian, points, defect_out, out, faces_out):
    def step(b, u):
        lanes = lanes_of(b)
        total = []
        for a in range(NV):
            rows = tail[a, :, lanes]
            total.append(less_rows(part[a, :, lanes], (rows[:1] + rows[1:]) * (1.0 / GROUP)))
        total = rim_part(0, total, b, rim, table, rim_jacobian)
        for a in range(NV):
            defect_out[a, :, lanes] = total[a]
            out[a, :, lanes] = points[pl.ds(a, 1), lanes] * total[a]

    each_block(table.shape[1], step)
    faces_kernel(listed, out, faces_out)


def corrected_kernel(table, listed, field, part, rim, tail, fine, rim_jacobian, points, out, faces_out, scratch):
    steps = field.shape[1]

    def step(b, u):
        lanes = lanes_of(b)
        total = rest_part(b, part, rim, tail, table, rim_jacobian)
        for a in range(NV):
            v = field[a, :, lanes] + points[pl.ds(a, 1), lanes] * total[a]
            for i in range(GROUP):
                scratch[u, a, pl.ds(i, steps, stride=GROUP), :] = v
            out[a, :, lanes] = fine[a, :, lanes] + scratch[u, a]

    each_block(table.shape[1], step)
    faces_kernel(listed, out, faces_out)


def residual_kernel(table, part, rim, tail, rim_jacobian, out, scratch, sems):
    blocks = table.shape[1]

    def send(b):
        lanes = lanes_of(b)
        return pltpu.make_async_copy(scratch.at[:, :, lanes], out.at[:, :, lanes], sems.at[b])

    def step(b, u):
        lanes = lanes_of(b)
        total = rest_part(b, part, rim, tail, table, rim_jacobian)
        for a in range(NV):
            scratch[a, :, lanes] = total[a]
        send(b).start()

    each_block(blocks, step)
    each_block(blocks, lambda b, u: send(b).wait())


def exchange(faces, tail):
    slabs, periods = lax.axis_size("space"), lax.axis_size("tm")
    across = [(i, i + 1) for i in range(1, slabs - 1, 2)]
    beside = [(i, i + 1) for i in range(0, slabs - 1, 2)]
    both_ways = lambda pairs: pairs + [(j, i) for i, j in pairs]
    rim_x = lax.ppermute(faces, "space", both_ways(across))
    rim_on = lax.ppermute(faces, "space", both_ways(beside))
    tail = lax.ppermute(tail, "tm", [(i, (i + 1) % periods) for i in range(periods)])
    return rim_x, rim_on, tail


def body(iterate, right_side, jacobian, self_block, cell_diag, neighbours, face_list):
    steps, cells = iterate.shape[0], iterate.shape[2]
    blocks, faces = cells // BLK, face_list.shape[0]
    coarse = steps // GROUP
    per_slot = 2 * blocks * NV * NV * BLK

    whole = lambda n: shape(NV, n, cells)
    face = lambda n: shape(faces, NV, n, BLK)
    rows_scratch = [pltpu.VMEM((UNROLL, NV, steps, BLK), jnp.float32)]

    table, listed = pl.pallas_call(
        table_kernel,
        out_shape=[pltpu.SMEM((K, blocks), jnp.int32), pltpu.SMEM((faces,), jnp.int32)],
        in_specs=[IN_SMEM] * 2,
        out_specs=[IN_SMEM] * 2,
        name="block_tables",
    )(jnp.transpose(neighbours), face_list)

    state = jnp.transpose(iterate, (1, 0, 2))
    goal = jnp.transpose(right_side, (1, 0, 2))
    jacobian = jnp.transpose(jacobian, (1, 2, 0, 3))
    fine_points, coarse_points = call(points_kernel, "point_diagonals", [], [cell_diag], [shape(NV, cells)] * 2)
    rim_jacobian = call(rim_jacobian_kernel, "rim_jacobian", [], [jacobian], [shape(2, NV, NV, cells)])[0]
    sent = call(faces_kernel, "faces_of_iterate", [listed], [state], [face(steps)])[0]

    def swap(sent, field, weight):
        tail = call(functools.partial(tail_kernel, weight), "tail", [], [field], [whole(2)])[0]
        return exchange(sent, tail)

    def own(weight, n, field, target, rim_on):
        return call(
            functools.partial(own_kernel, weight), "own_part", [table],
            [field, target, rim_on, jacobian, rim_jacobian, self_block, cell_diag], [whole(n)], 6 * per_slot * n,
        )[0]

    for sweep_no in range(NU1):
        rim_x, rim_on, tail = swap(sent, state, time_weight)
        part = own(time_weight, steps, state, goal, rim_on)
        arrays = [state, part, rim_x, tail, rim_jacobian, fine_points]
        if sweep_no < NU1 - 1:
            state, sent = call(
                sweep_kernel, "sweep", [table, listed], arrays, [whole(steps), face(steps)], per_slot * steps
            )
        else:
            state, means, sent = call(
                smoothed_kernel, "sweep_and_means", [table, listed], arrays,
                [whole(steps), whole(coarse), face(coarse)], per_slot * steps, rows_scratch,
            )

    rim_x, rim_on, tail = swap(sent, state, time_weight)
    part = call(
        functools.partial(means_kernel, time_weight), "own_part_of_means", [table],
        [state, goal, means, rim_on, jacobian, rim_jacobian, self_block, cell_diag], [whole(coarse)], 6 * per_slot * coarse,
        rows_scratch,
    )[0]
    defect, correction, sent = call(
        first_correction_kernel, "first_correction", [table, listed],
        [part, rim_x, tail, rim_jacobian, coarse_points], [whole(coarse), whole(coarse), face(coarse)], per_slot * coarse,
    )
    for sweep_no in range(NUC - 1):
        rim_x, rim_on, tail = swap(sent, correction, coarse_weight)
        part = own(coarse_weight, coarse, correction, defect, rim_on)
        if sweep_no < NUC - 2:
            correction, sent = call(
                sweep_kernel, "coarse_sweep", [table, listed],
                [correction, part, rim_x, tail, rim_jacobian, coarse_points],
                [whole(coarse), face(coarse)], per_slot * coarse,
            )
        else:
            state, sent = call(
                corrected_kernel, "corrected", [table, listed],
                [correction, part, rim_x, tail, state, rim_jacobian, coarse_points],
                [whole(steps), face(steps)], per_slot * coarse, rows_scratch,
            )

    for sweep_no in range(NU2):
        rim_x, rim_on, tail = swap(sent, state, time_weight)
        part = own(time_weight, steps, state, goal, rim_on)
        state, sent = call(
            sweep_kernel, "sweep", [table, listed],
            [state, part, rim_x, tail, rim_jacobian, fine_points], [whole(steps), face(steps)], per_slot * steps,
        )
    rim_x, rim_on, tail = swap(sent, state, time_weight)
    part = own(time_weight, steps, state, goal, rim_on)
    residual = call(
        residual_kernel, "residual", [table], [part, rim_x, tail, rim_jacobian], [whole(steps)], per_slot * steps,
        [pltpu.VMEM((NV, steps, cells), jnp.float32), pltpu.SemaphoreType.DMA((blocks,))],
        [pl.BlockSpec(memory_space=pl.ANY)],
    )[0]
    return jnp.transpose(state, (1, 0, 2)), jnp.transpose(residual, (1, 0, 2))


def solution(mesh):
    in_specs = (
        P("tm", None, "space"),
        P("tm", None, "space"),
        P(None, None, None, "space"),
        P(None, None, "space"),
        P(None, "space"),
        P("space", None),
        P("space"),
    )
    out_specs = (P("tm", None, "space"), P("tm", None, "space"))
    return jax.shard_map(body, mesh=mesh, in_specs=in_specs, out_specs=out_specs, check_vma=False)
```

profile of v0, /device:TPU:1, one launch (start us, length us, event | category | flops | bytes accessed | tf_op | source)
XLA Modules:
  0.0 80.8 jit_solution(17981838263241899612)
XLA Ops:
  0.6 1.1 %block_tables.1 = (s32[6,16]{1,0:T(8,128)S(4)}, s32[8]{0:T(128)S(4)}) custom-call(s32[6,16]{1,0:T(8,128)} %bitcast.28, s32[8]{0:T(128)} %face_list.1), custom_call_target="tpu_custom_call" | custom-call | tf_op jit(solution)/shard_map/block_tables/pallas_call | solution.py:293
  1.8 1.1 %copy-done.3 = f32[16,5,2048]{2,0,1:T(8,128)S(1)} copy-done((f32[16,5,2048]{2,0,1:T(8,128)S(1)}, f32[16,5,2048]{2,0,1:T(8,128)}, u32[]{:S(2)}) %copy-start.3) | copy-done | bytes 655384
  3.1 4.7 %collective-permute-start.1 = (f32[8,5,16,128]{3,2,1,0:T(8,128)S(1)}, f32[8,5,16,128]{3,2,1,0:T(8,128)S(1)}, u32[]{:S(2)}, u32[]{:S(2)}) collective-permute-start(f32[8,5,16,128]{3,2,1,0:T(8,128)S(1)} %faces_of_iterate.1), channel_id=1, source_target_pairs={{1,2},{3,4},{5,6},{2,1},{4,3},{6,5},{9,10},{11,12},{13,14},{10,9},... | collective-permute-start | bytes 983048 | tf_op jit(solution)/shard_map/ppermute | solution.py:277
  7.8 1.3 %collective-permute-start.2 = (f32[5,2,2048]{2,1,0:T(2,128)S(1)}, f32[5,2,2048]{2,1,0:T(2,128)S(1)}, u32[]{:S(2)}, u32[]{:S(2)}) collective-permute-start(f32[5,2,2048]{2,1,0:T(2,128)S(1)} %tail.9), channel_id=1, source_target_pairs={{0,8},{8,16},{16,24},{24,0},{1,9},{9,17},{17,25},{25,1},{2,10},{10... | collective-permute-start | bytes 245768 | tf_op jit(solution)/shard_map/ppermute | solution.py:279
  9.3 2.1 %own_part.8.part = f32[5,16,2048]{2,1,0:T(8,128)S(1)} custom-call(s32[6,16]{1,0:T(8,128)S(4)} %get-tuple-element.24.table, f32[5,16,2048]{2,1,0:T(8,128)S(1)} %bitcast.25, f32[5,16,2048]{2,1,0:T(8,128)S(1)} %bitcast.17, f32[8,5,16,128]{3,2,1,0:T(8,128)S(1)} %collective-permute-done.rim, f32[5,5,6,2048]{3,2,1,0:T(8,128)S(1)} %bitcast.8, ...), custom_call_target="tpu_custom_call" | custom-call | flops 9830400 | bytes 4177920 | tf_op jit(solution)/shard_map/own_part/pallas_call | solution.py:31
  13.1 4.0 %collective-permute-start.4 = (f32[8,5,16,128]{3,2,1,0:T(8,128)S(1)}, f32[8,5,16,128]{3,2,1,0:T(8,128)S(1)}, u32[]{:S(2)}, u32[]{:S(2)}) collective-permute-start(f32[8,5,16,128]{3,2,1,0:T(8,128)S(1)} %get-tuple-element.28), channel_id=1, source_target_pairs={{1,2},{3,4},{5,6},{2,1},{4,3},{6,5},{9,10},{11,12},{13,14},{10,9},... | collective-permute-start | bytes 983048 | tf_op jit(solution)/shard_map/ppermute | solution.py:277
  17.1 1.3 %collective-permute-start.5 = (f32[5,2,2048]{2,1,0:T(2,128)S(1)}, f32[5,2,2048]{2,1,0:T(2,128)S(1)}, u32[]{:S(2)}, u32[]{:S(2)}) collective-permute-start(f32[5,2,2048]{2,1,0:T(2,128)S(1)} %tail.10), channel_id=1, source_target_pairs={{0,8},{8,16},{16,24},{24,0},{1,9},{9,17},{17,25},{25,1},{2,10},{10... | collective-permute-start | bytes 245768 | tf_op jit(solution)/shard_map/ppermute | solution.py:279
  18.3 2.1 %own_part.9.part = f32[5,16,2048]{2,1,0:T(8,128)S(1)} custom-call(s32[6,16]{1,0:T(8,128)S(4)} %get-tuple-element.24.table, f32[5,16,2048]{2,1,0:T(8,128)S(1)} %get-tuple-element.27.field, f32[5,16,2048]{2,1,0:T(8,128)S(1)} %bitcast.18, f32[8,5,16,128]{3,2,1,0:T(8,128)S(1)} %collective-permute-done.3.rim, f32[5,5,6,2048]{3,2,1,0:T(8,128)S(1)} %bitcast.9, ...), custom_call_target="tpu_custom_call" | custom-call | flops 9830400 | bytes 4177920 | tf_op jit(solution)/shard_map/own_part/pallas_call | solution.py:31
  22.5 1.3 %collective-permute-start.8 = (f32[5,2,2048]{2,1,0:T(2,128)S(1)}, f32[5,2,2048]{2,1,0:T(2,128)S(1)}, u32[]{:S(2)}, u32[]{:S(2)}) collective-permute-start(f32[5,2,2048]{2,1,0:T(2,128)S(1)} %tail.11), channel_id=1, source_target_pairs={{0,8},{8,16},{16,24},{24,0},{1,9},{9,17},{17,25},{25,1},{2,10},{10... | collective-permute-start | bytes 245768 | tf_op jit(solution)/shard_map/ppermute | solution.py:279
  23.8 4.0 %collective-permute-start.7 = (f32[8,5,4,128]{3,2,1,0:T(4,128)S(1)}, f32[8,5,4,128]{3,2,1,0:T(4,128)S(1)}, u32[]{:S(2)}, u32[]{:S(2)}) collective-permute-start(f32[8,5,4,128]{3,2,1,0:T(4,128)S(1)} %get-tuple-element.31), channel_id=1, source_target_pairs={{1,2},{3,4},{5,6},{2,1},{4,3},{6,5},{9,10},{11,12},{13,14},{10,9},... | collective-permute-start | bytes 245768 | tf_op jit(solution)/shard_map/ppermute | solution.py:277
  27.8 1.2 %own_part_of_means.1.part = f32[5,4,2048]{2,1,0:T(4,128)S(1)} custom-call(s32[6,16]{1,0:T(8,128)S(4)} %get-tuple-element.24.table, f32[5,16,2048]{2,1,0:T(8,128)S(1)} %get-tuple-element.29.field.fine, f32[5,16,2048]{2,1,0:T(8,128)S(1)} %bitcast.19, f32[5,4,2048]{2,1,0:T(4,128)S(1)} %get-tuple-element.30.means, ...), custom_call_target="tpu_custom_call" | custom-call | flops 2457600 | bytes 3604480 | tf_op jit(solution)/shard_map/own_part_of_means/pallas_call | solution.py:31
  30.3 1.3 %collective-permute-start.11 = (f32[5,2,2048]{2,1,0:T(2,128)S(1)}, f32[5,2,2048]{2,1,0:T(2,128)S(1)}, u32[]{:S(2)}, u32[]{:S(2)}) collective-permute-start(f32[5,2,2048]{2,1,0:T(2,128)S(1)} %tail.12), channel_id=1, source_target_pairs={{0,8},{8,16},{16,24},{24,0},{1,9},{9,17},{17,25},{25,1},{2,10},{10... | collective-permute-start | bytes 245768 | tf_op jit(solution)/shard_map/ppermute | solution.py:279
  31.5 4.0 %collective-permute-start.10 = (f32[8,5,4,128]{3,2,1,0:T(4,128)S(1)}, f32[8,5,4,128]{3,2,1,0:T(4,128)S(1)}, u32[]{:S(2)}, u32[]{:S(2)}) collective-permute-start(f32[8,5,4,128]{3,2,1,0:T(4,128)S(1)} %get-tuple-element.35), channel_id=1, source_target_pairs={{1,2},{3,4},{5,6},{2,1},{4,3},{6,5},{9,10},{11,12},{13,14},{10,9},... | collective-permute-start | bytes 245768 | tf_op jit(solution)/shard_map/ppermute | solution.py:277
  35.6 1.0 %own_part.10.part = f32[5,4,2048]{2,1,0:T(4,128)S(1)} custom-call(s32[6,16]{1,0:T(8,128)S(4)} %get-tuple-element.24.table, f32[5,4,2048]{2,1,0:T(4,128)S(1)} %get-tuple-element.33.field, f32[5,4,2048]{2,1,0:T(4,128)S(1)} %get-tuple-element.34.goal, f32[8,5,4,128]{3,2,1,0:T(4,128)S(1)} %collective-permute-done.9.rim, f32[5,5,6,2048]{3,2,1,0:T(8,128)S(1)} %bitcast.11, ...), custom_call_target="tpu_custom_call" | custom-call | flops 2457600 | bytes 2457600 | tf_op jit(solution)/shard_map/own_part/pallas_call | solution.py:31
  36.6 1.1 %collective-permute-done.10.rim = f32[8,5,4,128]{3,2,1,0:T(4,128)S(1)} collective-permute-done((f32[8,5,4,128]{3,2,1,0:T(4,128)S(1)}, f32[8,5,4,128]{3,2,1,0:T(4,128)S(1)}, u32[]{:S(2)}, u32[]{:S(2)}) %collective-permute-start.10) | collective-permute-done | bytes 81952 | tf_op jit(solution)/shard_map/ppermute | solution.py:277
  38.1 1.3 %collective-permute-start.14 = (f32[5,2,2048]{2,1,0:T(2,128)S(1)}, f32[5,2,2048]{2,1,0:T(2,128)S(1)}, u32[]{:S(2)}, u32[]{:S(2)}) collective-permute-start(f32[5,2,2048]{2,1,0:T(2,128)S(1)} %tail.13), channel_id=1, source_target_pairs={{0,8},{8,16},{16,24},{24,0},{1,9},{9,17},{17,25},{25,1},{2,10},{10... | collective-permute-start | bytes 245768 | tf_op jit(solution)/shard_map/ppermute | solution.py:279
  39.4 4.0 %collective-permute-start.13 = (f32[8,5,4,128]{3,2,1,0:T(4,128)S(1)}, f32[8,5,4,128]{3,2,1,0:T(4,128)S(1)}, u32[]{:S(2)}, u32[]{:S(2)}) collective-permute-start(f32[8,5,4,128]{3,2,1,0:T(4,128)S(1)} %get-tuple-element.37), channel_id=1, source_target_pairs={{1,2},{3,4},{5,6},{2,1},{4,3},{6,5},{9,10},{11,12},{13,14},{10,9},... | collective-permute-start | bytes 245768 | tf_op jit(solution)/shard_map/ppermute | solution.py:277
  43.4 1.0 %own_part.11.part = f32[5,4,2048]{2,1,0:T(4,128)S(1)} custom-call(s32[6,16]{1,0:T(8,128)S(4)} %get-tuple-element.24.table, f32[5,4,2048]{2,1,0:T(4,128)S(1)} %get-tuple-element.36.field, f32[5,4,2048]{2,1,0:T(4,128)S(1)} %get-tuple-element.34.goal, f32[8,5,4,128]{3,2,1,0:T(4,128)S(1)} %collective-permute-done.12.rim, f32[5,5,6,2048]{3,2,1,0:T(8,128)S(1)} %bitcast.12, ...), custom_call_target="tpu_custom_call" | custom-call | flops 2457600 | bytes 2457600 | tf_op jit(solution)/shard_map/own_part/pallas_call | solution.py:31
  44.4 1.1 %collective-permute-done.13.rim = f32[8,5,4,128]{3,2,1,0:T(4,128)S(1)} collective-permute-done((f32[8,5,4,128]{3,2,1,0:T(4,128)S(1)}, f32[8,5,4,128]{3,2,1,0:T(4,128)S(1)}, u32[]{:S(2)}, u32[]{:S(2)}) %collective-permute-start.13) | collective-permute-done | bytes 81952 | tf_op jit(solution)/shard_map/ppermute | solution.py:277
  46.2 4.0 %collective-permute-start.16 = (f32[8,5,4,128]{3,2,1,0:T(4,128)S(1)}, f32[8,5,4,128]{3,2,1,0:T(4,128)S(1)}, u32[]{:S(2)}, u32[]{:S(2)}) collective-permute-start(f32[8,5,4,128]{3,2,1,0:T(4,128)S(1)} %get-tuple-element.39), channel_id=1, source_target_pairs={{1,2},{3,4},{5,6},{2,1},{4,3},{6,5},{9,10},{11,12},{13,14},{10,9},... | collective-permute-start | bytes 245768 | tf_op jit(solution)/shard_map/ppermute | solution.py:277
  50.2 1.0 %own_part.12.part = f32[5,4,2048]{2,1,0:T(4,128)S(1)} custom-call(s32[6,16]{1,0:T(8,128)S(4)} %get-tuple-element.24.table, f32[5,4,2048]{2,1,0:T(4,128)S(1)} %get-tuple-element.38.field, f32[5,4,2048]{2,1,0:T(4,128)S(1)} %get-tuple-element.34.goal, f32[8,5,4,128]{3,2,1,0:T(4,128)S(1)} %collective-permute-done.15.rim, f32[5,5,6,2048]{3,2,1,0:T(8,128)S(1)} %bitcast.13, ...), custom_call_target="tpu_custom_call" | custom-call | flops 2457600 | bytes 2457600 | tf_op jit(solution)/shard_map/own_part/pallas_call | solution.py:31
  51.2 1.1 %collective-permute-done.16.rim = f32[8,5,4,128]{3,2,1,0:T(4,128)S(1)} collective-permute-done((f32[8,5,4,128]{3,2,1,0:T(4,128)S(1)}, f32[8,5,4,128]{3,2,1,0:T(4,128)S(1)}, u32[]{:S(2)}, u32[]{:S(2)}) %collective-permute-start.16) | collective-permute-done | bytes 81952 | tf_op jit(solution)/shard_map/ppermute | solution.py:277
  52.9 3.7 %collective-permute-start.19 = (f32[8,5,16,128]{3,2,1,0:T(8,128)S(1)}, f32[8,5,16,128]{3,2,1,0:T(8,128)S(1)}, u32[]{:S(2)}, u32[]{:S(2)}) collective-permute-start(f32[8,5,16,128]{3,2,1,0:T(8,128)S(1)} %get-tuple-element.41), channel_id=1, source_target_pairs={{1,2},{3,4},{5,6},{2,1},{4,3},{6,5},{9,10},{11,12},{13,14},{10,9},... | collective-permute-start | bytes 983048 | tf_op jit(solution)/shard_map/ppermute | solution.py:277
  56.7 1.3 %collective-permute-start.20 = (f32[5,2,2048]{2,1,0:T(2,128)S(1)}, f32[5,2,2048]{2,1,0:T(2,128)S(1)}, u32[]{:S(2)}, u32[]{:S(2)}) collective-permute-start(f32[5,2,2048]{2,1,0:T(2,128)S(1)} %tail.15), channel_id=1, source_target_pairs={{0,8},{8,16},{16,24},{24,0},{1,9},{9,17},{17,25},{25,1},{2,10},{10... | collective-permute-start | bytes 245768 | tf_op jit(solution)/shard_map/ppermute | solution.py:279
  58.0 2.1 %own_part.13.part = f32[5,16,2048]{2,1,0:T(8,128)S(1)} custom-call(s32[6,16]{1,0:T(8,128)S(4)} %get-tuple-element.24.table, f32[5,16,2048]{2,1,0:T(8,128)S(1)} %get-tuple-element.40.field, f32[5,16,2048]{2,1,0:T(8,128)S(1)} %bitcast.20, f32[8,5,16,128]{3,2,1,0:T(8,128)S(1)} %collective-permute-done.18.rim, f32[5,5,6,2048]{3,2,1,0:T(8,128)S(1)} %bitcast.14, ...), custom_call_target="tpu_custom_call" | custom-call | flops 9830400 | bytes 4177920 | tf_op jit(solution)/shard_map/own_part/pallas_call | solution.py:31
  61.9 4.0 %collective-permute-start.22 = (f32[8,5,16,128]{3,2,1,0:T(8,128)S(1)}, f32[8,5,16,128]{3,2,1,0:T(8,128)S(1)}, u32[]{:S(2)}, u32[]{:S(2)}) collective-permute-start(f32[8,5,16,128]{3,2,1,0:T(8,128)S(1)} %get-tuple-element.43), channel_id=1, source_target_pairs={{1,2},{3,4},{5,6},{2,1},{4,3},{6,5},{9,10},{11,12},{13,14},{10,9},... | collective-permute-start | bytes 983048 | tf_op jit(solution)/shard_map/ppermute | solution.py:277
  66.0 1.3 %collective-permute-start.23 = (f32[5,2,2048]{2,1,0:T(2,128)S(1)}, f32[5,2,2048]{2,1,0:T(2,128)S(1)}, u32[]{:S(2)}, u32[]{:S(2)}) collective-permute-start(f32[5,2,2048]{2,1,0:T(2,128)S(1)} %tail.16), channel_id=1, source_target_pairs={{0,8},{8,16},{16,24},{24,0},{1,9},{9,17},{17,25},{25,1},{2,10},{10... | collective-permute-start | bytes 245768 | tf_op jit(solution)/shard_map/ppermute | solution.py:279
  67.3 2.1 %own_part.14.part = f32[5,16,2048]{2,1,0:T(8,128)S(1)} custom-call(s32[6,16]{1,0:T(8,128)S(4)} %get-tuple-element.24.table, f32[5,16,2048]{2,1,0:T(8,128)S(1)} %get-tuple-element.42.field, f32[5,16,2048]{2,1,0:T(8,128)S(1)} %bitcast.21, f32[8,5,16,128]{3,2,1,0:T(8,128)S(1)} %collective-permute-done.21.rim, f32[5,5,6,2048]{3,2,1,0:T(8,128)S(1)} %bitcast.15, ...), custom_call_target="tpu_custom_call" | custom-call | flops 9830400 | bytes 4177920 | tf_op jit(solution)/shard_map/own_part/pallas_call | solution.py:31
  71.2 3.7 %collective-permute-start.25 = (f32[8,5,16,128]{3,2,1,0:T(8,128)S(1)}, f32[8,5,16,128]{3,2,1,0:T(8,128)S(1)}, u32[]{:S(2)}, u32[]{:S(2)}) collective-permute-start(f32[8,5,16,128]{3,2,1,0:T(8,128)S(1)} %get-tuple-element.45), channel_id=1, source_target_pairs={{1,2},{3,4},{5,6},{2,1},{4,3},{6,5},{9,10},{11,12},{13,14},{10,9},... | collective-permute-start | bytes 983048 | tf_op jit(solution)/shard_map/ppermute | solution.py:277
  75.0 1.3 %collective-permute-start.26 = (f32[5,2,2048]{2,1,0:T(2,128)S(1)}, f32[5,2,2048]{2,1,0:T(2,128)S(1)}, u32[]{:S(2)}, u32[]{:S(2)}) collective-permute-start(f32[5,2,2048]{2,1,0:T(2,128)S(1)} %tail.17), channel_id=1, source_target_pairs={{0,8},{8,16},{16,24},{24,0},{1,9},{9,17},{17,25},{25,1},{2,10},{10... | collective-permute-start | bytes 245768 | tf_op jit(solution)/shard_map/ppermute | solution.py:279
  77.1 2.1 %own_part.15.part = f32[5,16,2048]{2,1,0:T(8,128)S(1)} custom-call(s32[6,16]{1,0:T(8,128)S(4)} %get-tuple-element.24.table, f32[5,16,2048]{2,1,0:T(8,128)S(1)} %get-tuple-element.44.field, f32[5,16,2048]{2,1,0:T(8,128)S(1)} %bitcast.22, f32[8,5,16,128]{3,2,1,0:T(8,128)S(1)} %collective-permute-done.24.rim, f32[5,5,6,2048]{3,2,1,0:T(8,128)S(1)} %bitcast.16, ...), custom_call_target="tpu_custom_call" | custom-call | flops 9830400 | bytes 4177920 | tf_op jit(solution)/shard_map/own_part/pallas_call | solution.py:31
  79.7 1.1 %residual.1 = f32[5,16,2048]{2,1,0:T(8,128)} custom-call(s32[6,16]{1,0:T(8,128)S(4)} %get-tuple-element.24.table, f32[5,16,2048]{2,1,0:T(8,128)S(1)} %own_part.15.part, f32[8,5,16,128]{3,2,1,0:T(8,128)S(1)} %collective-permute-done.25.rim, f32[5,2,2048]{2,1,0:T(2,128)S(1)} %collective-permute-done.26.tail, f32[2,5,5,2048]{3,2,1,0:T(8,128)S(1)} %rim_jacobian.1), custom_call_target="tpu_custom_call" | custom-call | flops 1638400 | bytes 2129920 | tf_op jit(solution)/shard_map/residual/pallas_call | solution.py:31
  (66 shorter events, 12.1 us)
Async XLA Ops:
  0.6 8.5 %copy-start = (f32[6,5,5,2048]{3,0,2,1:T(8,128)S(1)}, f32[6,5,5,2048]{3,0,2,1:T(8,128)}, u32[]{:S(2)}) copy-start(f32[6,5,5,2048]{3,0,2,1:T(8,128)} %param.9) | copy-start | bytes 3686404
  2.9 6.2 %copy-start.5 = (f32[5,2048]{1,0:T(8,128)S(1)}, f32[5,2048]{1,0:T(8,128)}, u32[]{:S(2)}) copy-start(f32[5,2048]{1,0:T(8,128)} %cell_diag.19) | copy-start | bytes 122884
  2.9 6.3 %copy-start.1 = (f32[5,5,2048]{2,1,0:T(8,128)S(1)}, f32[5,5,2048]{2,1,0:T(8,128)}, u32[]{:S(2)}) copy-start(f32[5,5,2048]{2,1,0:T(8,128)} %self_block.17) | copy-start | bytes 614404
  2.9 6.3 %copy-start.2 = (f32[16,5,2048]{2,0,1:T(8,128)S(1)}, f32[16,5,2048]{2,0,1:T(8,128)}, u32[]{:S(2)}) copy-start(f32[16,5,2048]{2,0,1:T(8,128)} %param.8) | copy-start | bytes 1966084
  2.9 6.3 %copy-start.4 = (f32[16,5,2048]{2,0,1:T(8,128)S(1)}, f32[16,5,2048]{2,0,1:T(8,128)}, u32[]{:S(2)}) copy-start(f32[16,5,2048]{2,0,1:T(8,128)} %param.7) | copy-start | bytes 1966084
  3.0 6.3 %collective-permute-start = (f32[8,5,16,128]{3,2,1,0:T(8,128)S(1)}, f32[8,5,16,128]{3,2,1,0:T(8,128)S(1)}, u32[]{:S(2)}, u32[]{:S(2)}) collective-permute-start(f32[8,5,16,128]{3,2,1,0:T(8,128)S(1)} %faces_of_iterate.1), channel_id=1, source_target_pairs={{0,1},{2,3},{4,5},{6,7},{1,0},{3,2},{5,4},{7,6},{8,9},{10,11},{12,... | collective-permute-start | bytes 983048 | tf_op jit(solution)/shard_map/ppermute | solution.py:278
  3.1 9.4 %collective-permute-start.1 = (f32[8,5,16,128]{3,2,1,0:T(8,128)S(1)}, f32[8,5,16,128]{3,2,1,0:T(8,128)S(1)}, u32[]{:S(2)}, u32[]{:S(2)}) collective-permute-start(f32[8,5,16,128]{3,2,1,0:T(8,128)S(1)} %faces_of_iterate.1), channel_id=1, source_target_pairs={{1,2},{3,4},{5,6},{2,1},{4,3},{6,5},{9,10},{11,12},{13,14},{10,9},... | collective-permute-start | bytes 983048 | tf_op jit(solution)/shard_map/ppermute | solution.py:277
  7.8 4.2 %collective-permute-start.2 = (f32[5,2,2048]{2,1,0:T(2,128)S(1)}, f32[5,2,2048]{2,1,0:T(2,128)S(1)}, u32[]{:S(2)}, u32[]{:S(2)}) collective-permute-start(f32[5,2,2048]{2,1,0:T(2,128)S(1)} %tail.9), channel_id=1, source_target_pairs={{0,8},{8,16},{16,24},{24,0},{1,9},{9,17},{17,25},{25,1},{2,10},{10... | collective-permute-start | bytes 245768 | tf_op jit(solution)/shard_map/ppermute | solution.py:279
  13.0 5.4 %collective-permute-start.3 = (f32[8,5,16,128]{3,2,1,0:T(8,128)S(1)}, f32[8,5,16,128]{3,2,1,0:T(8,128)S(1)}, u32[]{:S(2)}, u32[]{:S(2)}) collective-permute-start(f32[8,5,16,128]{3,2,1,0:T(8,128)S(1)} %get-tuple-element.28), channel_id=1, source_target_pairs={{0,1},{2,3},{4,5},{6,7},{1,0},{3,2},{5,4},{7,6},{8,9},{10,11},{12,... | collective-permute-start | bytes 983048 | tf_op jit(solution)/shard_map/ppermute | solution.py:278
  13.1 8.7 %collective-permute-start.4 = (f32[8,5,16,128]{3,2,1,0:T(8,128)S(1)}, f32[8,5,16,128]{3,2,1,0:T(8,128)S(1)}, u32[]{:S(2)}, u32[]{:S(2)}) collective-permute-start(f32[8,5,16,128]{3,2,1,0:T(8,128)S(1)} %get-tuple-element.28), channel_id=1, source_target_pairs={{1,2},{3,4},{5,6},{2,1},{4,3},{6,5},{9,10},{11,12},{13,14},{10,9},... | collective-permute-start | bytes 983048 | tf_op jit(solution)/shard_map/ppermute | solution.py:277
  17.1 4.2 %collective-permute-start.5 = (f32[5,2,2048]{2,1,0:T(2,128)S(1)}, f32[5,2,2048]{2,1,0:T(2,128)S(1)}, u32[]{:S(2)}, u32[]{:S(2)}) collective-permute-start(f32[5,2,2048]{2,1,0:T(2,128)S(1)} %tail.10), channel_id=1, source_target_pairs={{0,8},{8,16},{16,24},{24,0},{1,9},{9,17},{17,25},{25,1},{2,10},{10... | collective-permute-start | bytes 245768 | tf_op jit(solution)/shard_map/ppermute | solution.py:279
  22.4 5.4 %collective-permute-start.6 = (f32[8,5,4,128]{3,2,1,0:T(4,128)S(1)}, f32[8,5,4,128]{3,2,1,0:T(4,128)S(1)}, u32[]{:S(2)}, u32[]{:S(2)}) collective-permute-start(f32[8,5,4,128]{3,2,1,0:T(4,128)S(1)} %get-tuple-element.31), channel_id=1, source_target_pairs={{0,1},{2,3},{4,5},{6,7},{1,0},{3,2},{5,4},{7,6},{8,9},{10,11},{12,... | collective-permute-start | bytes 245768 | tf_op jit(solution)/shard_map/ppermute | solution.py:278
  22.5 6.5 %collective-permute-start.8 = (f32[5,2,2048]{2,1,0:T(2,128)S(1)}, f32[5,2,2048]{2,1,0:T(2,128)S(1)}, u32[]{:S(2)}, u32[]{:S(2)}) collective-permute-start(f32[5,2,2048]{2,1,0:T(2,128)S(1)} %tail.11), channel_id=1, source_target_pairs={{0,8},{8,16},{16,24},{24,0},{1,9},{9,17},{17,25},{25,1},{2,10},{10... | collective-permute-start | bytes 245768 | tf_op jit(solution)/shard_map/ppermute | solution.py:279
  23.8 6.1 %collective-permute-start.7 = (f32[8,5,4,128]{3,2,1,0:T(4,128)S(1)}, f32[8,5,4,128]{3,2,1,0:T(4,128)S(1)}, u32[]{:S(2)}, u32[]{:S(2)}) collective-permute-start(f32[8,5,4,128]{3,2,1,0:T(4,128)S(1)} %get-tuple-element.31), channel_id=1, source_target_pairs={{1,2},{3,4},{5,6},{2,1},{4,3},{6,5},{9,10},{11,12},{13,14},{10,9},... | collective-permute-start | bytes 245768 | tf_op jit(solution)/shard_map/ppermute | solution.py:277
  30.2 5.4 %collective-permute-start.9 = (f32[8,5,4,128]{3,2,1,0:T(4,128)S(1)}, f32[8,5,4,128]{3,2,1,0:T(4,128)S(1)}, u32[]{:S(2)}, u32[]{:S(2)}) collective-permute-start(f32[8,5,4,128]{3,2,1,0:T(4,128)S(1)} %get-tuple-element.35), channel_id=1, source_target_pairs={{0,1},{2,3},{4,5},{6,7},{1,0},{3,2},{5,4},{7,6},{8,9},{10,11},{12,... | collective-permute-start | bytes 245768 | tf_op jit(solution)/shard_map/ppermute | solution.py:278
  30.3 6.3 %collective-permute-start.11 = (f32[5,2,2048]{2,1,0:T(2,128)S(1)}, f32[5,2,2048]{2,1,0:T(2,128)S(1)}, u32[]{:S(2)}, u32[]{:S(2)}) collective-permute-start(f32[5,2,2048]{2,1,0:T(2,128)S(1)} %tail.12), channel_id=1, source_target_pairs={{0,8},{8,16},{16,24},{24,0},{1,9},{9,17},{17,25},{25,1},{2,10},{10... | collective-permute-start | bytes 245768 | tf_op jit(solution)/shard_map/ppermute | solution.py:279
  31.5 6.2 %collective-permute-start.10 = (f32[8,5,4,128]{3,2,1,0:T(4,128)S(1)}, f32[8,5,4,128]{3,2,1,0:T(4,128)S(1)}, u32[]{:S(2)}, u32[]{:S(2)}) collective-permute-start(f32[8,5,4,128]{3,2,1,0:T(4,128)S(1)} %get-tuple-element.35), channel_id=1, source_target_pairs={{1,2},{3,4},{5,6},{2,1},{4,3},{6,5},{9,10},{11,12},{13,14},{10,9},... | collective-permute-start | bytes 245768 | tf_op jit(solution)/shard_map/ppermute | solution.py:277
  38.0 5.4 %collective-permute-start.12 = (f32[8,5,4,128]{3,2,1,0:T(4,128)S(1)}, f32[8,5,4,128]{3,2,1,0:T(4,128)S(1)}, u32[]{:S(2)}, u32[]{:S(2)}) collective-permute-start(f32[8,5,4,128]{3,2,1,0:T(4,128)S(1)} %get-tuple-element.37), channel_id=1, source_target_pairs={{0,1},{2,3},{4,5},{6,7},{1,0},{3,2},{5,4},{7,6},{8,9},{10,11},{12,... | collective-permute-start | bytes 245768 | tf_op jit(solution)/shard_map/ppermute | solution.py:278
  38.1 6.3 %collective-permute-start.14 = (f32[5,2,2048]{2,1,0:T(2,128)S(1)}, f32[5,2,2048]{2,1,0:T(2,128)S(1)}, u32[]{:S(2)}, u32[]{:S(2)}) collective-permute-start(f32[5,2,2048]{2,1,0:T(2,128)S(1)} %tail.13), channel_id=1, source_target_pairs={{0,8},{8,16},{16,24},{24,0},{1,9},{9,17},{17,25},{25,1},{2,10},{10... | collective-permute-start | bytes 245768 | tf_op jit(solution)/shard_map/ppermute | solution.py:279
  39.4 6.2 %collective-permute-start.13 = (f32[8,5,4,128]{3,2,1,0:T(4,128)S(1)}, f32[8,5,4,128]{3,2,1,0:T(4,128)S(1)}, u32[]{:S(2)}, u32[]{:S(2)}) collective-permute-start(f32[8,5,4,128]{3,2,1,0:T(4,128)S(1)} %get-tuple-element.37), channel_id=1, source_target_pairs={{1,2},{3,4},{5,6},{2,1},{4,3},{6,5},{9,10},{11,12},{13,14},{10,9},... | collective-permute-start | bytes 245768 | tf_op jit(solution)/shard_map/ppermute | solution.py:277
  45.8 4.4 %collective-permute-start.15 = (f32[8,5,4,128]{3,2,1,0:T(4,128)S(1)}, f32[8,5,4,128]{3,2,1,0:T(4,128)S(1)}, u32[]{:S(2)}, u32[]{:S(2)}) collective-permute-start(f32[8,5,4,128]{3,2,1,0:T(4,128)S(1)} %get-tuple-element.39), channel_id=1, source_target_pairs={{0,1},{2,3},{4,5},{6,7},{1,0},{3,2},{5,4},{7,6},{8,9},{10,11},{12,... | collective-permute-start | bytes 245768 | tf_op jit(solution)/shard_map/ppermute | solution.py:278
  45.9 5.3 %collective-permute-start.17 = (f32[5,2,2048]{2,1,0:T(2,128)S(1)}, f32[5,2,2048]{2,1,0:T(2,128)S(1)}, u32[]{:S(2)}, u32[]{:S(2)}) collective-permute-start(f32[5,2,2048]{2,1,0:T(2,128)S(1)} %tail.14), channel_id=1, source_target_pairs={{0,8},{8,16},{16,24},{24,0},{1,9},{9,17},{17,25},{25,1},{2,10},{10... | collective-permute-start | bytes 245768 | tf_op jit(solution)/shard_map/ppermute | solution.py:279
  46.2 6.2 %collective-permute-start.16 = (f32[8,5,4,128]{3,2,1,0:T(4,128)S(1)}, f32[8,5,4,128]{3,2,1,0:T(4,128)S(1)}, u32[]{:S(2)}, u32[]{:S(2)}) collective-permute-start(f32[8,5,4,128]{3,2,1,0:T(4,128)S(1)} %get-tuple-element.39), channel_id=1, source_target_pairs={{1,2},{3,4},{5,6},{2,1},{4,3},{6,5},{9,10},{11,12},{13,14},{10,9},... | collective-permute-start | bytes 245768 | tf_op jit(solution)/shard_map/ppermute | solution.py:277
  52.8 5.1 %collective-permute-start.18 = (f32[8,5,16,128]{3,2,1,0:T(8,128)S(1)}, f32[8,5,16,128]{3,2,1,0:T(8,128)S(1)}, u32[]{:S(2)}, u32[]{:S(2)}) collective-permute-start(f32[8,5,16,128]{3,2,1,0:T(8,128)S(1)} %get-tuple-element.41), channel_id=1, source_target_pairs={{0,1},{2,3},{4,5},{6,7},{1,0},{3,2},{5,4},{7,6},{8,9},{10,11},{12,... | collective-permute-start | bytes 983048 | tf_op jit(solution)/shard_map/ppermute | solution.py:278
  52.9 8.5 %collective-permute-start.19 = (f32[8,5,16,128]{3,2,1,0:T(8,128)S(1)}, f32[8,5,16,128]{3,2,1,0:T(8,128)S(1)}, u32[]{:S(2)}, u32[]{:S(2)}) collective-permute-start(f32[8,5,16,128]{3,2,1,0:T(8,128)S(1)} %get-tuple-element.41), channel_id=1, source_target_pairs={{1,2},{3,4},{5,6},{2,1},{4,3},{6,5},{9,10},{11,12},{13,14},{10,9},... | collective-permute-start | bytes 983048 | tf_op jit(solution)/shard_map/ppermute | solution.py:277
  56.7 4.2 %collective-permute-start.20 = (f32[5,2,2048]{2,1,0:T(2,128)S(1)}, f32[5,2,2048]{2,1,0:T(2,128)S(1)}, u32[]{:S(2)}, u32[]{:S(2)}) collective-permute-start(f32[5,2,2048]{2,1,0:T(2,128)S(1)} %tail.15), channel_id=1, source_target_pairs={{0,8},{8,16},{16,24},{24,0},{1,9},{9,17},{17,25},{25,1},{2,10},{10... | collective-permute-start | bytes 245768 | tf_op jit(solution)/shard_map/ppermute | solution.py:279
  61.9 5.4 %collective-permute-start.21 = (f32[8,5,16,128]{3,2,1,0:T(8,128)S(1)}, f32[8,5,16,128]{3,2,1,0:T(8,128)S(1)}, u32[]{:S(2)}, u32[]{:S(2)}) collective-permute-start(f32[8,5,16,128]{3,2,1,0:T(8,128)S(1)} %get-tuple-element.43), channel_id=1, source_target_pairs={{0,1},{2,3},{4,5},{6,7},{1,0},{3,2},{5,4},{7,6},{8,9},{10,11},{12,... | collective-permute-start | bytes 983048 | tf_op jit(solution)/shard_map/ppermute | solution.py:278
  61.9 8.8 %collective-permute-start.22 = (f32[8,5,16,128]{3,2,1,0:T(8,128)S(1)}, f32[8,5,16,128]{3,2,1,0:T(8,128)S(1)}, u32[]{:S(2)}, u32[]{:S(2)}) collective-permute-start(f32[8,5,16,128]{3,2,1,0:T(8,128)S(1)} %get-tuple-element.43), channel_id=1, source_target_pairs={{1,2},{3,4},{5,6},{2,1},{4,3},{6,5},{9,10},{11,12},{13,14},{10,9},... | collective-permute-start | bytes 983048 | tf_op jit(solution)/shard_map/ppermute | solution.py:277
  66.0 4.2 %collective-permute-start.23 = (f32[5,2,2048]{2,1,0:T(2,128)S(1)}, f32[5,2,2048]{2,1,0:T(2,128)S(1)}, u32[]{:S(2)}, u32[]{:S(2)}) collective-permute-start(f32[5,2,2048]{2,1,0:T(2,128)S(1)} %tail.16), channel_id=1, source_target_pairs={{0,8},{8,16},{16,24},{24,0},{1,9},{9,17},{17,25},{25,1},{2,10},{10... | collective-permute-start | bytes 245768 | tf_op jit(solution)/shard_map/ppermute | solution.py:279
  71.2 6.0 %collective-permute-start.24 = (f32[8,5,16,128]{3,2,1,0:T(8,128)S(1)}, f32[8,5,16,128]{3,2,1,0:T(8,128)S(1)}, u32[]{:S(2)}, u32[]{:S(2)}) collective-permute-start(f32[8,5,16,128]{3,2,1,0:T(8,128)S(1)} %get-tuple-element.45), channel_id=1, source_target_pairs={{0,1},{2,3},{4,5},{6,7},{1,0},{3,2},{5,4},{7,6},{8,9},{10,11},{12,... | collective-permute-start | bytes 983048 | tf_op jit(solution)/shard_map/ppermute | solution.py:278
  71.2 8.5 %collective-permute-start.25 = (f32[8,5,16,128]{3,2,1,0:T(8,128)S(1)}, f32[8,5,16,128]{3,2,1,0:T(8,128)S(1)}, u32[]{:S(2)}, u32[]{:S(2)}) collective-permute-start(f32[8,5,16,128]{3,2,1,0:T(8,128)S(1)} %get-tuple-element.45), channel_id=1, source_target_pairs={{1,2},{3,4},{5,6},{2,1},{4,3},{6,5},{9,10},{11,12},{13,14},{10,9},... | collective-permute-start | bytes 983048 | tf_op jit(solution)/shard_map/ppermute | solution.py:277
  75.0 4.2 %collective-permute-start.26 = (f32[5,2,2048]{2,1,0:T(2,128)S(1)}, f32[5,2,2048]{2,1,0:T(2,128)S(1)}, u32[]{:S(2)}, u32[]{:S(2)}) collective-permute-start(f32[5,2,2048]{2,1,0:T(2,128)S(1)} %tail.17), channel_id=1, source_target_pairs={{0,8},{8,16},{16,24},{24,0},{1,9},{9,17},{17,25},{25,1},{2,10},{10... | collective-permute-start | bytes 245768 | tf_op jit(solution)/shard_map/ppermute | solution.py:279
  (1 other events, 1.1 us)
where the time goes:
time: 81.2 us; the launch traced here: 80.8 us
  starting transfers between devices  47.3 us (58%)
  Pallas kernels  20.5 us (25%)
  waiting for transfers between devices  9.93 us (12%)
  local copies, waits for them, and re-layouts  1.95 us (2%)
  between operations  1.13 us (1%)
    ppermute x9, starting transfers between devices, exchange(): rim_x = lax.ppermute(faces, 'space', both_ways(across))  36.2 us
    pallas_call x30, Pallas kernels, call(): pl.pallas_call(kernel, out_shape=outs if out_specs else [pltpu.VMEM(o.sha...  19.4 us
    ppermute x9, starting transfers between devices, exchange(): lax.ppermute(tail, 'tm', [(i, (i + 1) % periods) for i in range(periods)])  10.4 us
    ppermute x9, waiting for transfers between devices, exchange(): rim_x = lax.ppermute(faces, 'space', both_ways(across))  6.54 us
    ppermute x9, waiting for transfers between devices, exchange(): lax.ppermute(tail, 'tm', [(i, (i + 1) % periods) for i in range(periods)])  3.37 us
    unnamed x13, local copies, waits for them, and re-layouts  1.95 us
  transfers between devices with their start and end apart: 27, of which 13 were waited for; matrix products, arithmetic and copies ran while one was open for 1% of the time, Pallas kernels for 18%

commit v1 on v0

v1 whole, which is shorter than its diff:
```python
import functools

import jax
import jax.numpy as jnp
from jax import lax
from jax.experimental import pallas as pl
from jax.experimental.pallas import tpu as pltpu
from jax.sharding import PartitionSpec as P

NV = 5
BLK = 128
K = 6
NU1 = 2
NU2 = 2
NUC = 4
GROUP = 4

time_weight = 0.5
coarse_weight = time_weight / GROUP
damping = 0.7

UNROLL = 4
SCRATCH_BYTES = 4 << 20
IN_VMEM = pl.BlockSpec(memory_space=pltpu.VMEM)
NOTHING = pl.CostEstimate(flops=1, bytes_accessed=1, transcendentals=0)
LONG = pl.CostEstimate(flops=0, bytes_accessed=100 << 20, transcendentals=0)
IN_HBM = pl.BlockSpec(memory_space=pltpu.HBM)
IN_SMEM = pl.BlockSpec(memory_space=pltpu.SMEM)


def call(kernel, name, tables, arrays, outs, flops=0, scratch=(), out_specs=None):
    arrays = [pltpu.with_memory_space_constraint(a, pltpu.VMEM) for a in arrays]
    size = 4 * (sum(a.size for a in arrays) + sum(o.size for o in outs))
    return pl.pallas_call(
        kernel,
        out_shape=outs if out_specs else [pltpu.VMEM(o.shape, o.dtype) for o in outs],
        in_specs=[IN_SMEM] * len(tables) + [IN_VMEM] * len(arrays),
        out_specs=out_specs or [IN_VMEM] * len(outs),
        scratch_shapes=scratch,
        cost_estimate=LONG if name.startswith('rim') else NOTHING,
        compiler_params=pltpu.CompilerParams(vmem_limit_bytes=SCRATCH_BYTES),
        name=name,
    )(*tables, *arrays)


def in_hbm(array):
    return pltpu.with_memory_space_constraint(array, pltpu.HBM)


def shape(*dims):
    return jax.ShapeDtypeStruct(dims, jnp.float32)


def lanes_of(b):
    return pl.ds(pl.multiple_of(b * BLK, BLK), BLK)


def cross_slot():
    return lax.rem(lax.axis_index("space"), 2)


def each_block(count, step):
    unroll = UNROLL if count % UNROLL == 0 else 1

    def steps(i, carry):
        for u in range(unroll):
            step(i * unroll + u, u)
        return carry

    lax.fori_loop(0, count // unroll, steps, 0)


def first_kernel(neighbours, face_list, iterate, table, listed, field, faces_out, near, named, sems):
    copies = [
        pltpu.make_async_copy(iterate, field, sems.at[0]),
        pltpu.make_async_copy(neighbours, near, sems.at[1]),
        pltpu.make_async_copy(face_list, named, sems.at[2]),
    ]
    for copy in copies:
        copy.start()
    slot = cross_slot()
    slots, blocks = near.shape
    faces = named.shape[0]
    copies[1].wait()

    def step(b, carry):
        table[0, b] = near[slot, b] - (blocks + faces * slot)
        table[1, b] = near[1 - slot, b] - (blocks + faces * (1 - slot))
        for k in range(2, slots):
            table[k, b] = near[k, b]
        return carry

    lax.fori_loop(0, blocks, step, 0)
    copies[2].wait()
    for h in range(faces):
        listed[h] = named[h]
    copies[0].wait()
    pick_faces(listed, field, faces_out)


def arguments_kernel(listed, *refs):
    arguments, held = refs[:4], refs[4:8]
    fine_out, coarse_out, out, sems = refs[8:]
    copies = [pltpu.make_async_copy(x, y, sems.at[i]) for i, (x, y) in enumerate(zip(arguments, held))]
    for copy in copies:
        copy.start()
    for copy in copies:
        copy.wait()
    cell_diag, jacobian = held[0], held[1]
    fine_out[...] = damping / (3.0 * time_weight + cell_diag[...])
    coarse_out[...] = damping / (3.0 * coarse_weight + cell_diag[...])
    lower_crosses = cross_slot() == 0
    for a in range(NV):
        for j in range(NV):
            lower, upper = jacobian[a, j, pl.ds(0, 1), :], jacobian[a, j, pl.ds(1, 1), :]
            out[0, a, pl.ds(j, 1), :] = jnp.where(lower_crosses, lower, upper)
            out[1, a, pl.ds(j, 1), :] = jnp.where(lower_crosses, upper, lower)


def coupled(total, coupling, values):
    for j in range(NV):
        for a in range(NV):
            total[a] = total[a] - coupling(a, j) * values[j]
    return total


def earlier(v, steps):
    if v.shape[0] <= steps:
        return jnp.zeros_like(v)
    return jnp.concatenate([jnp.zeros((steps, BLK), jnp.float32), v[: v.shape[0] - steps]], axis=0)


def own_part(total, b, field, table, jacobian, self_block):
    lanes = lanes_of(b)
    v = [field[j, :, lanes] for j in range(NV)]
    for a in range(NV):
        for j in range(NV):
            if j != a:
                total[a] = total[a] - self_block[a, pl.ds(j, 1), lanes] * v[j]
    for slot in range(2, K):
        there = lanes_of(table[slot, b])
        row = pl.ds(slot, 1)
        total = coupled(total, lambda a, j: jacobian[a, j, row, lanes], [field[j, :, there] for j in range(NV)])
    return total


def rim_part(side, total, b, rim, table, rim_jacobian):
    block, lanes = table[side, b], lanes_of(b)
    coupling = lambda a, j: rim_jacobian[side, a, pl.ds(j, 1), lanes]
    return coupled(total, coupling, [rim[block, j] for j in range(NV)])


def pick_faces(listed, field, faces_out):
    for h in range(listed.shape[0]):
        lanes = lanes_of(listed[h])
        for a in range(NV):
            faces_out[h, a] = field[a, :, lanes]


def tail_rows(last_two, weight):
    last = last_two[1:]
    return weight * jnp.concatenate([last_two[:1] - 4.0 * last, last], axis=0)


def tail_kernel(weight, rim_weight, field, *refs):
    steps, cells = field.shape[1:]
    tail_out = refs[-1]
    for a in range(NV):
        last = field[a, pl.ds(steps - 1, 1), :]
        tail_out[a, pl.ds(0, 1), pl.ds(0, cells)] = weight * (field[a, pl.ds(steps - 2, 1), :] - 4.0 * last)
        tail_out[a, pl.ds(1, 1), pl.ds(0, cells)] = weight * last
    if len(refs) > 1:
        rim = refs[0]
        for h in range(rim.shape[0]):
            for a in range(NV):
                rows = tail_rows(rim[h, a, pl.ds(rim.shape[2] - 2, 2), :], rim_weight)
                tail_out[a, :, pl.ds(cells + h * BLK, BLK)] = rows


def own_kernel(weight, table, field, goal, jacobian, self_block, cell_diag, out):
    def step(b, u):
        lanes = lanes_of(b)
        total = []
        for a in range(NV):
            v = field[a, :, lanes]
            point = 3.0 * weight + cell_diag[pl.ds(a, 1), lanes]
            timed = weight * (earlier(v, 2) - 4.0 * earlier(v, 1))
            total.append(goal[a, :, lanes] - point * v - timed)
        total = own_part(total, b, field, table, jacobian, self_block)
        for a in range(NV):
            out[a, :, lanes] = total[a]

    each_block(table.shape[1], step)


def mean_rows(v, scratch, steps):
    scratch[...] = v
    return sum(scratch[pl.ds(i, steps, stride=GROUP), :] for i in range(GROUP)) * (1.0 / GROUP)


def spread_rows(v, scratch):
    for i in range(GROUP):
        scratch[pl.ds(i, v.shape[0], stride=GROUP), :] = v
    return scratch[...]


def means_kernel(weight, table, field, goal, means, jacobian, self_block, cell_diag, out, scratch):
    steps = means.shape[1]

    def step(b, u):
        lanes = lanes_of(b)
        total = []
        for a in range(NV):
            v = field[a, :, lanes]
            fine = goal[a, :, lanes] - weight * (3.0 * v - 4.0 * earlier(v, 1) + earlier(v, 2))
            total.append(mean_rows(fine, scratch.at[u, a], steps) - cell_diag[pl.ds(a, 1), lanes] * means[a, :, lanes])
        total = own_part(total, b, means, table, jacobian, self_block)
        for a in range(NV):
            out[a, :, lanes] = total[a]

    each_block(table.shape[1], step)


def beside_part(table, part, rim, rim_jacobian, out):
    def step(b, u):
        lanes = lanes_of(b)
        total = rim_part(1, [part[a, :, lanes] for a in range(NV)], b, rim, table, rim_jacobian)
        for a in range(NV):
            out[a, :, lanes] = total[a]

    each_block(table.shape[1], step)


def step_of(listed, h, a, field, part, points):
    lanes = lanes_of(listed[h])
    return field[a, :, lanes] + points[pl.ds(a, 1), lanes] * part[a, :, lanes]


def message_kernel(table, listed, field, part, rim, rim_jacobian, points, out, message):
    beside_part(table, part, rim, rim_jacobian, out)
    for h in range(listed.shape[0]):
        for a in range(NV):
            message[h, a] = step_of(listed, h, a, field, out, points)


def first_message_kernel(
    table, listed, field, part, rim, rim_jacobian, points, coarse_points, tail, out, message
):
    beside_part(table, part, rim, rim_jacobian, out)
    steps = field.shape[1]
    behind = NV * steps
    for h in range(listed.shape[0]):
        block = listed[h]
        lanes = lanes_of(block)
        for a in range(NV):
            message[h, pl.ds(a * steps, steps), :] = step_of(listed, h, a, field, out, points)
            message[h, pl.ds(behind + NV * a, NV), :] = rim_jacobian[0, a, :, lanes]
        message[h, pl.ds(behind + NV * NV, NV), :] = points[:, lanes]
        message[h, pl.ds(behind + NV * NV + NV, NV), :] = coarse_points[:, lanes]
        named = jnp.full((1, BLK), table[0, block], jnp.int32)
        message[h, pl.ds(behind + NV * NV + 2 * NV, 1), :] = named.astype(jnp.float32)


def means_message_kernel(table, listed, field, part, rim, rim_jacobian, points, out, message, scratch):
    beside_part(table, part, rim, rim_jacobian, out)
    steps = field.shape[1]
    coarse = steps // GROUP
    for h in range(listed.shape[0]):
        for a in range(NV):
            v = step_of(listed, h, a, field, out, points)
            message[h, a, pl.ds(0, coarse), :] = mean_rows(v, scratch.at[h % UNROLL, a], coarse)
            message[h, a, pl.ds(coarse, 2), :] = v[steps - 2 :]


def scaled_message_kernel(table, listed, part, rim, rim_jacobian, points, out, message):
    beside_part(table, part, rim, rim_jacobian, out)
    for h in range(listed.shape[0]):
        lanes = lanes_of(listed[h])
        for a in range(NV):
            message[h, a] = points[pl.ds(a, 1), lanes] * out[a, :, lanes]


def corrected_message_kernel(table, listed, field, part, rim, fine, rim_jacobian, points, out, message, scratch):
    beside_part(table, part, rim, rim_jacobian, out)
    for h in range(listed.shape[0]):
        for a in range(NV):
            v = step_of(listed, h, a, field, out, points)
            message[h, a] = fine[a, :, lanes_of(listed[h])] + spread_rows(v, scratch.at[h % UNROLL, a])


class Partner:
    def __init__(self, ref, steps, level):
        self.ref, self.behind, self.level = ref, NV * steps, level

    def row(self, h, r):
        return self.ref[h, pl.ds(self.behind + r, 1), :]

    def coupling(self, h):
        return lambda a, j: self.row(h, NV * a + j)

    def point(self, h, a):
        return self.row(h, NV * (NV + self.level) + a)


def index_kernel(steps, message, index):
    partner = Partner(message, steps, 0)
    for h in range(index.shape[0]):
        index[h] = jnp.max(partner.row(h, NV * (NV + 2))).astype(jnp.int32)


def own_share(index, h, faces, partner):
    block = index[h]
    zero = [jnp.zeros(faces.shape[2:], jnp.float32)] * NV
    total = coupled(zero, partner.coupling(h), [faces[block, j] for j in range(NV)])
    return [partner.point(h, a) * total[a] for a in range(NV)]


def rim_kernel(steps, level, index, faces, message, first_message, out):
    partner = Partner(first_message, steps, level)

    def step(h, u):
        share = own_share(index, h, faces, partner)
        for a in range(NV):
            if len(message.shape) == 3:
                out[h, a] = message[h, pl.ds(a * steps, steps), :] + share[a]
            else:
                out[h, a] = message[h, a] + share[a]

    each_block(index.shape[0], step)


def means_rim_kernel(steps, index, faces, message, first_message, out, last_out, scratch):
    partner = Partner(first_message, steps, 0)
    coarse = out.shape[2]

    def step(h, u):
        share = own_share(index, h, faces, partner)
        for a in range(NV):
            out[h, a] = message[h, a, pl.ds(0, coarse), :] + mean_rows(share[a], scratch.at[u, a], coarse)
            last_out[h, a] = message[h, a, pl.ds(coarse, 2), :] + share[a][steps - 2 :]

    each_block(index.shape[0], step)


def corrected_rim_kernel(steps, index, faces, message, first_message, out, scratch):
    partner = Partner(first_message, steps, 1)

    def step(h, u):
        share = own_share(index, h, faces, partner)
        for a in range(NV):
            out[h, a] = message[h, a] + spread_rows(share[a], scratch.at[u, a])

    each_block(index.shape[0], step)


def less_rows(total, rows):
    pad = total.shape[0] - rows.shape[0]
    if pad:
        rows = jnp.concatenate([rows, jnp.zeros((pad, BLK), jnp.float32)], axis=0)
    return total - rows


def mean_tail(rows):
    return (rows[:1] + rows[1:]) * (1.0 / GROUP)


def spread_tail(rows):
    return jnp.concatenate([jnp.broadcast_to(rows[i : i + 1], (GROUP, BLK)) for i in range(2)], axis=0)


def finish_rim(rim, tail, cells, partner, shape_tail, rim_out):
    def step(h, u):
        lanes = pl.ds(pl.multiple_of(cells + h * BLK, BLK), BLK)
        for a in range(NV):
            rim_out[h, a] = less_rows(rim[h, a], shape_tail(partner.point(h, a) * tail[a, :, lanes]))

    each_block(rim.shape[0], step)


def rest_part(b, part, rim, tail, table, rim_jacobian, shape_tail=lambda rows: rows):
    lanes = lanes_of(b)
    total = [less_rows(part[a, :, lanes], shape_tail(tail[a, :, lanes])) for a in range(NV)]
    return rim_part(0, total, b, rim, table, rim_jacobian)


def first_sweep_kernel(table, listed, field, part, rim, tail, rim_jacobian, points, out, faces_out):
    def step(b, u):
        lanes = lanes_of(b)
        total = rest_part(b, part, rim, tail, table, rim_jacobian)
        for a in range(NV):
            out[a, :, lanes] = field[a, :, lanes] + points[pl.ds(a, 1), lanes] * total[a]

    each_block(table.shape[1], step)
    pick_faces(listed, out, faces_out)


def sweep_kernel(
    steps, level, shape_tail, table, listed, field, part, rim, tail, first_message, rim_jacobian, points,
    out, faces_out, rim_out,
):
    finish_rim(rim, tail, field.shape[2], Partner(first_message, steps, level), shape_tail, rim_out)
    first_sweep_kernel(table, listed, field, part, rim_out, tail, rim_jacobian, points, out, faces_out)


def smoothed_kernel(
    table, listed, field, part, rim, tail, first_message, rim_jacobian, points,
    out, means_out, faces_out, rim_out, scratch,
):
    steps = means_out.shape[1]
    partner = Partner(first_message, field.shape[1], 0)
    finish_rim(rim, tail, field.shape[2], partner, lambda rows: rows, rim_out)

    def step(b, u):
        lanes = lanes_of(b)
        total = rest_part(b, part, rim_out, tail, table, rim_jacobian)
        for a in range(NV):
            v = field[a, :, lanes] + points[pl.ds(a, 1), lanes] * total[a]
            out[a, :, lanes] = v
            means_out[a, :, lanes] = mean_rows(v, scratch.at[u, a], steps)

    each_block(table.shape[1], step)
    pick_faces(listed, means_out, faces_out)


def first_correction_kernel(
    steps, table, listed, part, rim, tail, first_message, rim_jacobian, points, defect_out, out, faces_out, rim_out
):
    finish_rim(rim, tail, part.shape[2], Partner(first_message, steps, 0), mean_tail, rim_out)

    def step(b, u):
        lanes = lanes_of(b)
        total = rest_part(b, part, rim_out, tail, table, rim_jacobian, mean_tail)
        for a in range(NV):
            defect_out[a, :, lanes] = total[a]
            out[a, :, lanes] = points[pl.ds(a, 1), lanes] * total[a]

    each_block(table.shape[1], step)
    pick_faces(listed, out, faces_out)


def corrected_kernel(
    steps, table, listed, field, part, rim, tail, fine, first_message, rim_jacobian, points,
    out, faces_out, rim_out, scratch,
):
    partner = Partner(first_message, steps, 1)
    finish_rim(rim, tail, field.shape[2], partner, lambda rows: rows, rim_out)

    def step(b, u):
        lanes = lanes_of(b)
        total = rest_part(b, part, rim_out, tail, table, rim_jacobian)
        for a in range(NV):
            v = field[a, :, lanes] + points[pl.ds(a, 1), lanes] * total[a]
            out[a, :, lanes] = fine[a, :, lanes] + spread_rows(v, scratch.at[u, a])

    each_block(table.shape[1], step)
    pick_faces(listed, out, faces_out)


def residual_kernel(
    steps, table, field, part, rim, tail, first_message, rim_jacobian, updated, out, scratch, finished, sems
):
    blocks = table.shape[1]
    copy = pltpu.make_async_copy(field, updated, sems.at[blocks])
    copy.start()
    partner = Partner(first_message, steps, 0)
    finish_rim(rim, tail, part.shape[2], partner, lambda rows: rows, finished)

    def send(b):
        lanes = lanes_of(b)
        return pltpu.make_async_copy(scratch.at[:, :, lanes], out.at[:, :, lanes], sems.at[b])

    def step(b, u):
        lanes = lanes_of(b)
        total = rest_part(b, part, finished, tail, table, rim_jacobian)
        for a in range(NV):
            scratch[a, :, lanes] = total[a]
        send(b).start()

    each_block(blocks, step)
    each_block(blocks, lambda b, u: send(b).wait())
    copy.wait()


def neighbour_pairs(first):
    pairs = [(i, i + 1) for i in range(first, lax.axis_size("space") - 1, 2)]
    return pairs + [(j, i) for i, j in pairs]


def over_chips(message):
    return lax.ppermute(message, "space", neighbour_pairs(1))


def on_chip(faces):
    return lax.ppermute(faces, "space", neighbour_pairs(0))


def to_later(tail):
    periods = lax.axis_size("tm")
    return lax.ppermute(tail, "tm", [(i, (i + 1) % periods) for i in range(periods)])


def body(iterate, right_side, jacobian, self_block, cell_diag, neighbours, face_list):
    steps, cells = iterate.shape[0], iterate.shape[2]
    blocks, faces = cells // BLK, face_list.shape[0]
    coarse = steps // GROUP
    per_slot = 2 * blocks * NV * NV * BLK

    whole = lambda n: shape(NV, n, cells)
    face = lambda n: shape(faces, NV, n, BLK)
    spare = lambda more, n: shape(faces + more, NV, n, BLK)
    rows_scratch = [pltpu.VMEM((UNROLL, NV, steps, BLK), jnp.float32)]
    bind = functools.partial
    plain = lambda rows: rows

    goal = jnp.transpose(right_side, (1, 0, 2))
    jacobian = jnp.transpose(jacobian, (1, 2, 0, 3))
    table, listed, start, sent = pl.pallas_call(
        first_kernel,
        out_shape=[
            pltpu.SMEM((K, blocks), jnp.int32), pltpu.SMEM((faces,), jnp.int32),
            pltpu.VMEM((NV, steps, cells), jnp.float32), pltpu.VMEM((faces, NV, steps, BLK), jnp.float32),
        ],
        in_specs=[IN_HBM] * 3,
        out_specs=[IN_SMEM] * 2 + [IN_VMEM] * 2,
        scratch_shapes=[
            pltpu.SMEM((K, blocks), jnp.int32), pltpu.SMEM((faces,), jnp.int32), pltpu.SemaphoreType.DMA((3,)),
        ],
        compiler_params=pltpu.CompilerParams(vmem_limit_bytes=SCRATCH_BYTES),
        cost_estimate=NOTHING,
        name="iterate_and_tables",
    )(*[in_hbm(x) for x in (jnp.transpose(neighbours), face_list, jnp.transpose(iterate, (1, 0, 2)))])
    tables = [table, listed]
    rim = over_chips(sent)
    beside = on_chip(sent)
    arguments = [in_hbm(x) for x in (cell_diag, jacobian, self_block, goal)]
    outs = [shape(*x.shape) for x in arguments] + [shape(NV, cells)] * 2 + [shape(2, NV, NV, cells)]
    cell_diag, jacobian, self_block, goal, fine_points, coarse_points, rim_jacobian = pl.pallas_call(
        arguments_kernel,
        out_shape=[pltpu.VMEM(x.shape, jnp.float32) for x in outs],
        in_specs=[IN_SMEM] + [IN_HBM] * len(arguments),
        out_specs=[IN_VMEM] * len(outs),
        scratch_shapes=[pltpu.SemaphoreType.DMA((len(arguments),))],
        compiler_params=pltpu.CompilerParams(vmem_limit_bytes=SCRATCH_BYTES),
        cost_estimate=NOTHING,
        name="arguments",
    )(listed, *arguments)

    def own(weight, n, field, target):
        return call(
            bind(own_kernel, weight), "own_part", [table], [field, target, jacobian, self_block, cell_diag],
            [whole(n)], 5 * per_slot * n,
        )[0]

    def tail_of(field, weight, rim=None, rim_weight=None):
        arrays = [field] if rim is None else [field, rim]
        out = shape(NV, 2, cells + (0 if rim is None else faces * BLK))
        return to_later(call(bind(tail_kernel, weight, rim_weight), "tail", [], arrays, [out])[0])

    state = start
    tail = tail_of(state, time_weight)
    part = own(time_weight, steps, state, goal)
    part, message = call(
        first_message_kernel, "first_message", tables,
        [state, part, beside, rim_jacobian, fine_points, coarse_points, tail],
        [whole(steps), shape(faces, NV * steps + NV * (NV + 3), BLK)], per_slot * steps,
    )
    first_message = over_chips(message)
    message = first_message
    earlier_sent = sent
    state, sent = call(
        first_sweep_kernel, "first_sweep", tables, [state, part, rim, tail, rim_jacobian, fine_points],
        [whole(steps), face(steps)], per_slot * steps,
    )
    index = pl.pallas_call(
        bind(index_kernel, steps), out_shape=pltpu.SMEM((faces,), jnp.int32), in_specs=[IN_VMEM],
        out_specs=IN_SMEM, name="coupled_faces", cost_estimate=NOTHING,
        compiler_params=pltpu.CompilerParams(vmem_limit_bytes=SCRATCH_BYTES),
    )(pltpu.with_memory_space_constraint(first_message, pltpu.VMEM))

    beside = on_chip(sent)
    tail = tail_of(state, time_weight, rim, time_weight)
    part = own(time_weight, steps, state, goal)
    part, next_message = call(
        means_message_kernel, "message_of_means", tables, [state, part, beside, rim_jacobian, fine_points],
        [whole(steps), face(coarse + 2)], per_slot * steps, rows_scratch,
    )
    next_message = over_chips(next_message)
    rim = call(
        bind(rim_kernel, steps, 0), "rim", [index], [earlier_sent, message, first_message], [face(steps)],
        per_slot * steps // 2,
    )[0]
    message, earlier_sent = next_message, sent
    state, means, sent, rim = call(
        smoothed_kernel, "sweep_and_means", tables,
        [state, part, rim, tail, first_message, rim_jacobian, fine_points],
        [whole(steps), whole(coarse), face(coarse), face(steps)], per_slot * steps, rows_scratch,
    )

    beside = on_chip(sent)
    tail = tail_of(state, time_weight, rim, time_weight)
    part = call(
        bind(means_kernel, time_weight), "own_part_of_means", [table],
        [state, goal, means, jacobian, self_block, cell_diag], [whole(coarse)], 5 * per_slot * coarse, rows_scratch,
    )[0]
    part, next_message = call(
        scaled_message_kernel, "message_of_correction", tables, [part, beside, rim_jacobian, coarse_points],
        [whole(coarse), spare(faces, coarse)], per_slot * coarse,
    )
    next_message = over_chips(next_message)
    rim, last_rows = call(
        bind(means_rim_kernel, steps), "rim_of_means", [index], [earlier_sent, message, first_message],
        [face(coarse), face(2)], per_slot * steps // 2, rows_scratch,
    )
    message, earlier_sent = next_message, sent
    defect, correction, sent, rim = call(
        bind(first_correction_kernel, steps), "first_correction", tables,
        [part, rim, tail, first_message, rim_jacobian, coarse_points],
        [whole(coarse), whole(coarse), face(coarse), face(coarse)], per_slot * coarse,
    )

    rim, rim_weight, shape_tail = last_rows, time_weight, mean_tail
    for sweep_no in range(NUC - 1):
        beside = on_chip(sent)
        tail = tail_of(correction, coarse_weight, rim, rim_weight)
        part = own(coarse_weight, coarse, correction, defect)
        last = sweep_no == NUC - 2
        if last:
            part, next_message = call(
                corrected_message_kernel, "message_of_corrected", tables,
                [correction, part, beside, state, rim_jacobian, coarse_points],
                [whole(coarse), spare(1, steps)], per_slot * coarse, rows_scratch,
            )
        else:
            part, next_message = call(
                message_kernel, "message_of_coarse", tables, [correction, part, beside, rim_jacobian, coarse_points],
                [whole(coarse), spare(faces, coarse)], per_slot * coarse,
            )
        next_message = over_chips(next_message)
        rim = call(
            bind(rim_kernel, steps, 1), "rim_of_coarse", [index], [earlier_sent, message, first_message],
            [face(coarse)], per_slot * coarse // 2,
        )[0]
        message, earlier_sent = next_message, sent
        if last:
            state, sent, rim = call(
                bind(corrected_kernel, steps), "corrected", tables,
                [correction, part, rim, tail, state, first_message, rim_jacobian, coarse_points],
                [whole(steps), face(steps), face(coarse)], per_slot * coarse, rows_scratch,
            )
        else:
            correction, sent, rim = call(
                bind(sweep_kernel, steps, 1, shape_tail), "coarse_sweep", tables,
                [correction, part, rim, tail, first_message, rim_jacobian, coarse_points],
                [whole(coarse), face(coarse), face(coarse)], per_slot * coarse,
            )
        rim_weight, shape_tail = coarse_weight, plain

    for sweep_no in range(NU2 + 1):
        beside = on_chip(sent)
        tail = tail_of(state, time_weight, rim, rim_weight)
        part = own(time_weight, steps, state, goal)
        last = sweep_no == NU2
        if last:
            part = call(
                beside_part, "beside_part", [table], [part, beside, rim_jacobian], [whole(steps)], per_slot * steps
            )[0]
        else:
            part, next_message = call(
                message_kernel, "message", tables, [state, part, beside, rim_jacobian, fine_points],
                [whole(steps), spare(1, steps)], per_slot * steps,
            )
            next_message = over_chips(next_message)
        if sweep_no == 0:
            rim = call(
                bind(corrected_rim_kernel, steps), "rim_of_corrected", [index],
                [earlier_sent, message, first_message], [face(steps)], per_slot * coarse // 2, rows_scratch,
            )[0]
            level, shape_tail = 1, spread_tail
        else:
            rim = call(
                bind(rim_kernel, steps, 0), "rim", [index], [earlier_sent, message, first_message],
                [face(steps)], per_slot * steps // 2,
            )[0]
            level, shape_tail = 0, plain
        if not last:
            message, earlier_sent = next_message, sent
            state, sent, rim = call(
                bind(sweep_kernel, steps, level, shape_tail), "sweep", tables,
                [state, part, rim, tail, first_message, rim_jacobian, fine_points],
                [whole(steps), face(steps), face(steps)], per_slot * steps,
            )
        rim_weight = time_weight
    updated, residual = call(
        bind(residual_kernel, steps), "residual", [table], [state, part, rim, tail, first_message, rim_jacobian],
        [whole(steps)] * 2, per_slot * steps,
        [
            pltpu.VMEM((NV, steps, cells), jnp.float32), pltpu.VMEM((faces, NV, steps, BLK), jnp.float32),
            pltpu.SemaphoreType.DMA((blocks + 1,)),
        ],
        [IN_HBM] * 2,
    )
    return jnp.transpose(updated, (1, 0, 2)), jnp.transpose(residual, (1, 0, 2))


def solution(mesh):
    in_specs = (
        P("tm", None, "space"),
        P("tm", None, "space"),
        P(None, None, None, "space"),
        P(None, None, "space"),
        P(None, "space"),
        P("space", None),
        P("space"),
    )
    out_specs = (P("tm", None, "space"), P("tm", None, "space"))
    return jax.shard_map(body, mesh=mesh, in_specs=in_specs, out_specs=out_specs, check_vma=False)
```

time: 81.2 us -> 74.2 us (0.914)
  the two profiles are of different devices: /device:TPU:1 before, /device:TPU:0 now
where the time goes in v1:
time: 74.2 us; the launch traced here: 73.8 us
  starting transfers between devices  27.7 us (37%)
  Pallas kernels  25.4 us (34%)
  waiting for transfers between devices  19.6 us (26%)
  between operations  1.18 us (2%)
    pallas_call x44, Pallas kernels, call(): pl.pallas_call(kernel, out_shape=outs if out_specs else [pltpu.VMEM(o.sha...  22.2 us
    ppermute x9, waiting for transfers between devices, to_later(): lax.ppermute(tail, 'tm', [(i, (i + 1) % periods) for i in range(periods)])  19.5 us
    ppermute x9, starting transfers between devices, on_chip(): return lax.ppermute(faces, 'space', neighbour_pairs(0))  13.1 us
    ppermute x9, starting transfers between devices, to_later(): lax.ppermute(tail, 'tm', [(i, (i + 1) % periods) for i in range(periods)])  8.5 us
    ppermute x9, starting transfers between devices, over_chips(): return lax.ppermute(message, 'space', neighbour_pairs(1))  6.1 us
    pallas_call x1, Pallas kernels, body(): pl.pallas_call(arguments_kernel, out_shape=[pltpu.VMEM(x.shape, jnp.float...  1.88 us
  transfers between devices with their start and end apart: 27, of which 8 were waited for; matrix products, arithmetic and copies ran while one was open for 0% of the time, Pallas kernels for 31%

profile of v1, /device:TPU:0, one launch (start us, length us, event | category | flops | bytes accessed | tf_op | source)
XLA Modules:
  0.0 73.8 jit_solution(2326236618525408605)
XLA Ops:
  0.6 1.2 %iterate_and_tables.1 = (s32[6,16]{1,0:T(8,128)S(4)}, s32[8]{0:T(128)S(4)}, f32[5,16,2048]{2,1,0:T(8,128)S(1)}, f32[8,5,16,128]{3,2,1,0:T(8,128)S(1)}) custom-call(s32[6,16]{1,0:T(8,128)} %bitcast.9, s32[8]{0:T(128)} %face_list.1, f32[5,16,2048]{2,1,0:T(8,128)} %bitcast.7), custom_call_target="tpu_custom_call" | custom-call | flops 1 | bytes 1 | tf_op jit(solution)/shard_map/iterate_and_tables/pallas_call | solution.py:517
  3.0 2.6 %collective-permute-start.1 = (f32[5,2,2048]{2,1,0:T(2,128)S(1)}, f32[5,2,2048]{2,1,0:T(2,128)S(1)}, u32[]{:S(2)}, u32[]{:S(2)}) collective-permute-start(f32[5,2,2048]{2,1,0:T(2,128)S(1)} %tail.9), channel_id=1, source_target_pairs={{0,8},{8,16},{16,24},{24,0},{1,9},{9,17},{17,25},{25,1},{2,10},{10... | collective-permute-start | bytes 245768 | tf_op jit(solution)/shard_map/ppermute | solution.py:499
  5.6 1.9 %arguments.1 = (f32[5,2048]{1,0:T(8,128)S(1)}, f32[5,5,6,2048]{3,2,1,0:T(8,128)S(1)}, f32[5,5,2048]{2,1,0:T(8,128)S(1)}, f32[5,16,2048]{2,1,0:T(8,128)S(1)}, f32...) custom-call(s32[8]{0:T(128)S(4)} %get-tuple-element.58.listed, f32[5,2048]{1,0:T(8,128)} %refs_0_.1, ...), custom_call_target="tpu_custom_call" | custom-call | flops 1 | bytes 1 | tf_op jit(solution)/shard_map/arguments/pallas_call | solution.py:537
  7.5 1.7 %own_part.8.part = f32[5,16,2048]{2,1,0:T(8,128)S(1)} custom-call(s32[6,16]{1,0:T(8,128)S(4)} %get-tuple-element.57.table, f32[5,16,2048]{2,1,0:T(8,128)S(1)} %get-tuple-element.59.field, f32[5,16,2048]{2,1,0:T(8,128)S(1)} %get-tuple-element.60.goal, f32[5,5,6,2048]{3,2,1,0:T(8,128)S(1)} %get-tuple-element.61.jacobian, ...), custom_call_target="tpu_custom_call" | custom-call | flops 1 | bytes 1 | tf_op jit(solution)/shard_map/own_part/pallas_call | solution.py:34
  10.9 4.8 %collective-permute-start.3 = (f32[8,5,16,128]{3,2,1,0:T(8,128)S(1)}, f32[8,5,16,128]{3,2,1,0:T(8,128)S(1)}, u32[]{:S(2)}, u32[]{:S(2)}) collective-permute-start(f32[8,5,16,128]{3,2,1,0:T(8,128)S(1)} %get-tuple-element.70.faces), channel_id=1, source_target_pairs={{0,1},{2,3},{4,5},{6,7},{1,0},{3,2},{5,4},{7,6},{8,9},{10,11},{12,... | collective-permute-start | bytes 983048 | tf_op jit(solution)/shard_map/ppermute | solution.py:494
  15.7 1.5 %collective-permute-start.5 = (f32[5,2,3072]{2,1,0:T(2,128)S(1)}, f32[5,2,3072]{2,1,0:T(2,128)S(1)}, u32[]{:S(2)}, u32[]{:S(2)}) collective-permute-start(f32[5,2,3072]{2,1,0:T(2,128)S(1)} %tail.10), channel_id=1, source_target_pairs={{0,8},{8,16},{16,24},{24,0},{1,9},{9,17},{17,25},{25,1},{2,10},{10... | collective-permute-start | bytes 368648 | tf_op jit(solution)/shard_map/ppermute | solution.py:499
  17.2 1.7 %own_part.9.part = f32[5,16,2048]{2,1,0:T(8,128)S(1)} custom-call(s32[6,16]{1,0:T(8,128)S(4)} %get-tuple-element.57.table, f32[5,16,2048]{2,1,0:T(8,128)S(1)} %get-tuple-element.69.field, f32[5,16,2048]{2,1,0:T(8,128)S(1)} %get-tuple-element.60.goal, f32[5,5,6,2048]{3,2,1,0:T(8,128)S(1)} %get-tuple-element.61.jacobian, ...), custom_call_target="tpu_custom_call" | custom-call | flops 1 | bytes 1 | tf_op jit(solution)/shard_map/own_part/pallas_call | solution.py:34
  20.4 1.5 %collective-permute-done.5.tail = f32[5,2,3072]{2,1,0:T(2,128)S(1)} collective-permute-done((f32[5,2,3072]{2,1,0:T(2,128)S(1)}, f32[5,2,3072]{2,1,0:T(2,128)S(1)}, u32[]{:S(2)}, u32[]{:S(2)}) %collective-permute-start.5) | collective-permute-done | bytes 122912 | tf_op jit(solution)/shard_map/ppermute | solution.py:499
  22.5 1.0 %collective-permute-start.8 = (f32[5,2,3072]{2,1,0:T(2,128)S(1)}, f32[5,2,3072]{2,1,0:T(2,128)S(1)}, u32[]{:S(2)}, u32[]{:S(2)}) collective-permute-start(f32[5,2,3072]{2,1,0:T(2,128)S(1)} %tail.11), channel_id=1, source_target_pairs={{0,8},{8,16},{16,24},{24,0},{1,9},{9,17},{17,25},{25,1},{2,10},{10... | collective-permute-start | bytes 368648 | tf_op jit(solution)/shard_map/ppermute | solution.py:499
  23.5 2.6 %collective-permute-start.6 = (f32[8,5,4,128]{3,2,1,0:T(4,128)S(1)}, f32[8,5,4,128]{3,2,1,0:T(4,128)S(1)}, u32[]{:S(2)}, u32[]{:S(2)}) collective-permute-start(f32[8,5,4,128]{3,2,1,0:T(4,128)S(1)} %get-tuple-element.75.faces), channel_id=1, source_target_pairs={{0,1},{2,3},{4,5},{6,7},{1,0},{3,2},{5,4},{7,6},{8,9},{10,11},{12,... | collective-permute-start | bytes 245768 | tf_op jit(solution)/shard_map/ppermute | solution.py:494
  26.1 1.1 %own_part_of_means.1.part = f32[5,4,2048]{2,1,0:T(4,128)S(1)} custom-call(s32[6,16]{1,0:T(8,128)S(4)} %get-tuple-element.57.table, f32[5,16,2048]{2,1,0:T(8,128)S(1)} %get-tuple-element.73.field.fine, f32[5,16,2048]{2,1,0:T(8,128)S(1)} %get-tuple-element.60.goal, f32[5,4,2048]{2,1,0:T(4,128)S(1)} %get-tuple-element.74.means, ...), custom_call_target="tpu_custom_call" | custom-call | flops 1 | bytes 1 | tf_op jit(solution)/shard_map/own_part_of_means/pallas_call | solution.py:34
  28.3 0.9 %collective-permute-done.8.tail = f32[5,2,3072]{2,1,0:T(2,128)S(1)} collective-permute-done((f32[5,2,3072]{2,1,0:T(2,128)S(1)}, f32[5,2,3072]{2,1,0:T(2,128)S(1)}, u32[]{:S(2)}, u32[]{:S(2)}) %collective-permute-start.8) | collective-permute-done | bytes 122912 | tf_op jit(solution)/shard_map/ppermute | solution.py:499
  29.2 0.9 %first_correction.1 = (f32[5,4,2048]{2,1,0:T(4,128)S(1)}, f32[5,4,2048]{2,1,0:T(4,128)S(1)}, f32[8,5,4,128]{3,2,1,0:T(4,128)S(1)}, f32[8,5,4,128]{3,2,1,0:T(4,128)}) custom-call(s32[6,16]{1,0:T(8,128)S(4)} %get-tuple-element.57.table, s32[8]{0:T(128)S(4)} %get-tuple-element.58.listed, f32[5,4,2048]{2,1,0:T(4,128)S(1)} %get-tuple-element.76.part, ...), custom_call_target="tpu_custom_call" | custom-call | flops 1 | bytes 1 | tf_op jit(solution)/shard_map/first_correction/pallas_call | solution.py:34
  30.8 1.8 %collective-permute-start.9 = (f32[8,5,4,128]{3,2,1,0:T(4,128)S(1)}, f32[8,5,4,128]{3,2,1,0:T(4,128)S(1)}, u32[]{:S(2)}, u32[]{:S(2)}) collective-permute-start(f32[8,5,4,128]{3,2,1,0:T(4,128)S(1)} %get-tuple-element.82.faces), channel_id=1, source_target_pairs={{0,1},{2,3},{4,5},{6,7},{1,0},{3,2},{5,4},{7,6},{8,9},{10,11},{12,... | collective-permute-start | bytes 245768 | tf_op jit(solution)/shard_map/ppermute | solution.py:494
  32.6 0.9 %own_part.10.part = f32[5,4,2048]{2,1,0:T(4,128)S(1)} custom-call(s32[6,16]{1,0:T(8,128)S(4)} %get-tuple-element.57.table, f32[5,4,2048]{2,1,0:T(4,128)S(1)} %get-tuple-element.80.field, f32[5,4,2048]{2,1,0:T(4,128)S(1)} %get-tuple-element.81.goal, f32[5,5,6,2048]{3,2,1,0:T(8,128)S(1)} %get-tuple-element.61.jacobian, ...), custom_call_target="tpu_custom_call" | custom-call | flops 1 | bytes 1 | tf_op jit(solution)/shard_map/own_part/pallas_call | solution.py:34
  34.6 2.5 %collective-permute-done.11.tail = f32[5,2,3072]{2,1,0:T(2,128)S(1)} collective-permute-done((f32[5,2,3072]{2,1,0:T(2,128)S(1)}, f32[5,2,3072]{2,1,0:T(2,128)S(1)}, u32[]{:S(2)}, u32[]{:S(2)}) %collective-permute-start.11) | collective-permute-done | bytes 122912 | tf_op jit(solution)/shard_map/ppermute | solution.py:499
  37.5 1.9 %collective-permute-start.12 = (f32[8,5,4,128]{3,2,1,0:T(4,128)S(1)}, f32[8,5,4,128]{3,2,1,0:T(4,128)S(1)}, u32[]{:S(2)}, u32[]{:S(2)}) collective-permute-start(f32[8,5,4,128]{3,2,1,0:T(4,128)S(1)} %get-tuple-element.87.faces), channel_id=1, source_target_pairs={{0,1},{2,3},{4,5},{6,7},{1,0},{3,2},{5,4},{7,6},{8,9},{10,11},{12,... | collective-permute-start | bytes 245768 | tf_op jit(solution)/shard_map/ppermute | solution.py:494
  39.4 0.9 %own_part.11.part = f32[5,4,2048]{2,1,0:T(4,128)S(1)} custom-call(s32[6,16]{1,0:T(8,128)S(4)} %get-tuple-element.57.table, f32[5,4,2048]{2,1,0:T(4,128)S(1)} %get-tuple-element.86.field, f32[5,4,2048]{2,1,0:T(4,128)S(1)} %get-tuple-element.81.goal, f32[5,5,6,2048]{3,2,1,0:T(8,128)S(1)} %get-tuple-element.61.jacobian, ...), custom_call_target="tpu_custom_call" | custom-call | flops 1 | bytes 1 | tf_op jit(solution)/shard_map/own_part/pallas_call | solution.py:34
  41.4 2.6 %collective-permute-done.14.tail = f32[5,2,3072]{2,1,0:T(2,128)S(1)} collective-permute-done((f32[5,2,3072]{2,1,0:T(2,128)S(1)}, f32[5,2,3072]{2,1,0:T(2,128)S(1)}, u32[]{:S(2)}, u32[]{:S(2)}) %collective-permute-start.14) | collective-permute-done | bytes 122912 | tf_op jit(solution)/shard_map/ppermute | solution.py:499
  44.5 1.1 %collective-permute-start.15 = (f32[8,5,4,128]{3,2,1,0:T(4,128)S(1)}, f32[8,5,4,128]{3,2,1,0:T(4,128)S(1)}, u32[]{:S(2)}, u32[]{:S(2)}) collective-permute-start(f32[8,5,4,128]{3,2,1,0:T(4,128)S(1)} %get-tuple-element.92.faces), channel_id=1, source_target_pairs={{0,1},{2,3},{4,5},{6,7},{1,0},{3,2},{5,4},{7,6},{8,9},{10,11},{12,... | collective-permute-start | bytes 245768 | tf_op jit(solution)/shard_map/ppermute | solution.py:494
  45.6 0.9 %own_part.12.part = f32[5,4,2048]{2,1,0:T(4,128)S(1)} custom-call(s32[6,16]{1,0:T(8,128)S(4)} %get-tuple-element.57.table, f32[5,4,2048]{2,1,0:T(4,128)S(1)} %get-tuple-element.91.field, f32[5,4,2048]{2,1,0:T(4,128)S(1)} %get-tuple-element.81.goal, f32[5,5,6,2048]{3,2,1,0:T(8,128)S(1)} %get-tuple-element.61.jacobian, ...), custom_call_target="tpu_custom_call" | custom-call | flops 1 | bytes 1 | tf_op jit(solution)/shard_map/own_part/pallas_call | solution.py:34
  47.7 2.9 %collective-permute-done.17.tail = f32[5,2,3072]{2,1,0:T(2,128)S(1)} collective-permute-done((f32[5,2,3072]{2,1,0:T(2,128)S(1)}, f32[5,2,3072]{2,1,0:T(2,128)S(1)}, u32[]{:S(2)}, u32[]{:S(2)}) %collective-permute-start.17) | collective-permute-done | bytes 122912 | tf_op jit(solution)/shard_map/ppermute | solution.py:499
  51.3 1.1 %collective-permute-start.20 = (f32[5,2,3072]{2,1,0:T(2,128)S(1)}, f32[5,2,3072]{2,1,0:T(2,128)S(1)}, u32[]{:S(2)}, u32[]{:S(2)}) collective-permute-start(f32[5,2,3072]{2,1,0:T(2,128)S(1)} %tail.15), channel_id=1, source_target_pairs={{0,8},{8,16},{16,24},{24,0},{1,9},{9,17},{17,25},{25,1},{2,10},{10... | collective-permute-start | bytes 368648 | tf_op jit(solution)/shard_map/ppermute | solution.py:499
  52.4 1.7 %own_part.13.part = f32[5,16,2048]{2,1,0:T(8,128)S(1)} custom-call(s32[6,16]{1,0:T(8,128)S(4)} %get-tuple-element.57.table, f32[5,16,2048]{2,1,0:T(8,128)S(1)} %get-tuple-element.96.field, f32[5,16,2048]{2,1,0:T(8,128)S(1)} %get-tuple-element.60.goal, f32[5,5,6,2048]{3,2,1,0:T(8,128)S(1)} %get-tuple-element.61.jacobian, ...), custom_call_target="tpu_custom_call" | custom-call | flops 1 | bytes 1 | tf_op jit(solution)/shard_map/own_part/pallas_call | solution.py:34
  55.4 2.5 %collective-permute-done.20.tail = f32[5,2,3072]{2,1,0:T(2,128)S(1)} collective-permute-done((f32[5,2,3072]{2,1,0:T(2,128)S(1)}, f32[5,2,3072]{2,1,0:T(2,128)S(1)}, u32[]{:S(2)}, u32[]{:S(2)}) %collective-permute-start.20) | collective-permute-done | bytes 122912 | tf_op jit(solution)/shard_map/ppermute | solution.py:499
  58.7 0.8 %collective-permute-start.23 = (f32[5,2,3072]{2,1,0:T(2,128)S(1)}, f32[5,2,3072]{2,1,0:T(2,128)S(1)}, u32[]{:S(2)}, u32[]{:S(2)}) collective-permute-start(f32[5,2,3072]{2,1,0:T(2,128)S(1)} %tail.16), channel_id=1, source_target_pairs={{0,8},{8,16},{16,24},{24,0},{1,9},{9,17},{17,25},{25,1},{2,10},{10... | collective-permute-start | bytes 368648 | tf_op jit(solution)/shard_map/ppermute | solution.py:499
  59.5 1.7 %own_part.14.part = f32[5,16,2048]{2,1,0:T(8,128)S(1)} custom-call(s32[6,16]{1,0:T(8,128)S(4)} %get-tuple-element.57.table, f32[5,16,2048]{2,1,0:T(8,128)S(1)} %get-tuple-element.101.field, f32[5,16,2048]{2,1,0:T(8,128)S(1)} %get-tuple-element.60.goal, f32[5,5,6,2048]{3,2,1,0:T(8,128)S(1)} %get-tuple-element.61.jacobian, ...), custom_call_target="tpu_custom_call" | custom-call | flops 1 | bytes 1 | tf_op jit(solution)/shard_map/own_part/pallas_call | solution.py:34
  62.5 2.9 %collective-permute-done.23.tail = f32[5,2,3072]{2,1,0:T(2,128)S(1)} collective-permute-done((f32[5,2,3072]{2,1,0:T(2,128)S(1)}, f32[5,2,3072]{2,1,0:T(2,128)S(1)}, u32[]{:S(2)}, u32[]{:S(2)}) %collective-permute-start.23) | collective-permute-done | bytes 122912 | tf_op jit(solution)/shard_map/ppermute | solution.py:499
  66.0 0.8 %collective-permute-start.26 = (f32[5,2,3072]{2,1,0:T(2,128)S(1)}, f32[5,2,3072]{2,1,0:T(2,128)S(1)}, u32[]{:S(2)}, u32[]{:S(2)}) collective-permute-start(f32[5,2,3072]{2,1,0:T(2,128)S(1)} %tail.17), channel_id=1, source_target_pairs={{0,8},{8,16},{16,24},{24,0},{1,9},{9,17},{17,25},{25,1},{2,10},{10... | collective-permute-start | bytes 368648 | tf_op jit(solution)/shard_map/ppermute | solution.py:499
  66.8 1.7 %own_part.15.part = f32[5,16,2048]{2,1,0:T(8,128)S(1)} custom-call(s32[6,16]{1,0:T(8,128)S(4)} %get-tuple-element.57.table, f32[5,16,2048]{2,1,0:T(8,128)S(1)} %get-tuple-element.106.field, f32[5,16,2048]{2,1,0:T(8,128)S(1)} %get-tuple-element.60.goal, f32[5,5,6,2048]{3,2,1,0:T(8,128)S(1)} %get-tuple-element.61.jacobian, ...), custom_call_target="tpu_custom_call" | custom-call | flops 1 | bytes 1 | tf_op jit(solution)/shard_map/own_part/pallas_call | solution.py:34
  69.0 3.6 %collective-permute-done.26.tail = f32[5,2,3072]{2,1,0:T(2,128)S(1)} collective-permute-done((f32[5,2,3072]{2,1,0:T(2,128)S(1)}, f32[5,2,3072]{2,1,0:T(2,128)S(1)}, u32[]{:S(2)}, u32[]{:S(2)}) %collective-permute-start.26) | collective-permute-done | bytes 122912 | tf_op jit(solution)/shard_map/ppermute | solution.py:499
  72.7 1.2 %residual.1 = (f32[5,16,2048]{2,1,0:T(8,128)}, f32[5,16,2048]{2,1,0:T(8,128)}) custom-call(s32[6,16]{1,0:T(8,128)S(4)} %get-tuple-element.57.table, f32[5,16,2048]{2,1,0:T(8,128)S(1)} %get-tuple-element.106.field, f32[5,16,2048]{2,1,0:T(8,128)S(1)} %beside_part.1.part, f32[8,5,16,128]{3,2,1,0:T(8,128)S(1)} %rim.5, ...), custom_call_target="tpu_custom_call" | custom-call | flops 1 | bytes 1 | tf_op jit(solution)/shard_map/residual/pallas_call | solution.py:34
  (69 shorter events, 15.6 us)
Async XLA Ops:
  1.8 7.4 %collective-permute-start = (f32[8,5,16,128]{3,2,1,0:T(8,128)S(1)}, f32[8,5,16,128]{3,2,1,0:T(8,128)S(1)}, u32[]{:S(2)}, u32[]{:S(2)}) collective-permute-start(f32[8,5,16,128]{3,2,1,0:T(8,128)S(1)} %get-tuple-element.64.faces), channel_id=1, source_target_pairs={{0,1},{2,3},{4,5},{6,7},{1,0},{3,2},{5,4},{7,6},{8,9},{10,11},{12,... | collective-permute-start | bytes 983048 | tf_op jit(solution)/shard_map/ppermute | solution.py:494
  2.3 8.0 %collective-permute-start.2 = (f32[8,5,16,128]{3,2,1,0:T(8,128)S(1)}, f32[8,5,16,128]{3,2,1,0:T(8,128)S(1)}, u32[]{:S(2)}, u32[]{:S(2)}) collective-permute-start(f32[8,5,16,128]{3,2,1,0:T(8,128)S(1)} %get-tuple-element.64.faces), channel_id=1, source_target_pairs={{1,2},{3,4},{5,6},{2,1},{4,3},{6,5},{9,10},{11,12},{13,14},{10,9},... | collective-permute-start | bytes 983048 | tf_op jit(solution)/shard_map/ppermute | solution.py:490
  3.0 6.2 %collective-permute-start.1 = (f32[5,2,2048]{2,1,0:T(2,128)S(1)}, f32[5,2,2048]{2,1,0:T(2,128)S(1)}, u32[]{:S(2)}, u32[]{:S(2)}) collective-permute-start(f32[5,2,2048]{2,1,0:T(2,128)S(1)} %tail.9), channel_id=1, source_target_pairs={{0,8},{8,16},{16,24},{24,0},{1,9},{9,17},{17,25},{25,1},{2,10},{10... | collective-permute-start | bytes 245768 | tf_op jit(solution)/shard_map/ppermute | solution.py:499
  9.7 10.4 %collective-permute-start.4 = (f32[8,120,128]{2,1,0:T(8,128)S(1)}, f32[8,120,128]{2,1,0:T(8,128)S(1)}, u32[]{:S(2)}, u32[]{:S(2)}) collective-permute-start(f32[8,120,128]{2,1,0:T(8,128)S(1)} %get-tuple-element.72), channel_id=1, source_target_pairs={{1,2},{3,4},{5,6},{2,1},{4,3},{6,5},{9,10},{11,12},{13,14},{10,9},... | collective-permute-start | bytes 1474568 | tf_op jit(solution)/shard_map/ppermute | solution.py:490
  10.9 8.0 %collective-permute-start.3 = (f32[8,5,16,128]{3,2,1,0:T(8,128)S(1)}, f32[8,5,16,128]{3,2,1,0:T(8,128)S(1)}, u32[]{:S(2)}, u32[]{:S(2)}) collective-permute-start(f32[8,5,16,128]{3,2,1,0:T(8,128)S(1)} %get-tuple-element.70.faces), channel_id=1, source_target_pairs={{0,1},{2,3},{4,5},{6,7},{1,0},{3,2},{5,4},{7,6},{8,9},{10,11},{12,... | collective-permute-start | bytes 983048 | tf_op jit(solution)/shard_map/ppermute | solution.py:494
  15.7 6.2 %collective-permute-start.5 = (f32[5,2,3072]{2,1,0:T(2,128)S(1)}, f32[5,2,3072]{2,1,0:T(2,128)S(1)}, u32[]{:S(2)}, u32[]{:S(2)}) collective-permute-start(f32[5,2,3072]{2,1,0:T(2,128)S(1)} %tail.10), channel_id=1, source_target_pairs={{0,8},{8,16},{16,24},{24,0},{1,9},{9,17},{17,25},{25,1},{2,10},{10... | collective-permute-start | bytes 368648 | tf_op jit(solution)/shard_map/ppermute | solution.py:499
  19.4 8.7 %collective-permute-start.7 = (f32[8,5,6,128]{3,2,1,0:T(8,128)S(1)}, f32[8,5,6,128]{3,2,1,0:T(8,128)S(1)}, u32[]{:S(2)}, u32[]{:S(2)}) collective-permute-start(f32[8,5,6,128]{3,2,1,0:T(8,128)S(1)} %get-tuple-element.77), channel_id=1, source_target_pairs={{1,2},{3,4},{5,6},{2,1},{4,3},{6,5},{9,10},{11,12},{13,14},{10,9},... | collective-permute-start | bytes 368648 | tf_op jit(solution)/shard_map/ppermute | solution.py:490
  22.5 6.7 %collective-permute-start.8 = (f32[5,2,3072]{2,1,0:T(2,128)S(1)}, f32[5,2,3072]{2,1,0:T(2,128)S(1)}, u32[]{:S(2)}, u32[]{:S(2)}) collective-permute-start(f32[5,2,3072]{2,1,0:T(2,128)S(1)} %tail.11), channel_id=1, source_target_pairs={{0,8},{8,16},{16,24},{24,0},{1,9},{9,17},{17,25},{25,1},{2,10},{10... | collective-permute-start | bytes 368648 | tf_op jit(solution)/shard_map/ppermute | solution.py:499
  23.5 3.7 %collective-permute-start.6 = (f32[8,5,4,128]{3,2,1,0:T(4,128)S(1)}, f32[8,5,4,128]{3,2,1,0:T(4,128)S(1)}, u32[]{:S(2)}, u32[]{:S(2)}) collective-permute-start(f32[8,5,4,128]{3,2,1,0:T(4,128)S(1)} %get-tuple-element.75.faces), channel_id=1, source_target_pairs={{0,1},{2,3},{4,5},{6,7},{1,0},{3,2},{5,4},{7,6},{8,9},{10,11},{12,... | collective-permute-start | bytes 245768 | tf_op jit(solution)/shard_map/ppermute | solution.py:494
  27.4 7.1 %collective-permute-start.10 = (f32[16,5,4,128]{3,2,1,0:T(4,128)S(1)}, f32[16,5,4,128]{3,2,1,0:T(4,128)S(1)}, u32[]{:S(2)}, u32[]{:S(2)}) collective-permute-start(f32[16,5,4,128]{3,2,1,0:T(4,128)S(1)} %get-tuple-element.84), channel_id=1, source_target_pairs={{1,2},{3,4},{5,6},{2,1},{4,3},{6,5},{9,10},{11,12},{13,14},{10,9},... | collective-permute-start | bytes 491528 | tf_op jit(solution)/shard_map/ppermute | solution.py:490
  30.2 6.9 %collective-permute-start.11 = (f32[5,2,3072]{2,1,0:T(2,128)S(1)}, f32[5,2,3072]{2,1,0:T(2,128)S(1)}, u32[]{:S(2)}, u32[]{:S(2)}) collective-permute-start(f32[5,2,3072]{2,1,0:T(2,128)S(1)} %tail.12), channel_id=1, source_target_pairs={{0,8},{8,16},{16,24},{24,0},{1,9},{9,17},{17,25},{25,1},{2,10},{10... | collective-permute-start | bytes 368648 | tf_op jit(solution)/shard_map/ppermute | solution.py:499
  30.8 2.8 %collective-permute-start.9 = (f32[8,5,4,128]{3,2,1,0:T(4,128)S(1)}, f32[8,5,4,128]{3,2,1,0:T(4,128)S(1)}, u32[]{:S(2)}, u32[]{:S(2)}) collective-permute-start(f32[8,5,4,128]{3,2,1,0:T(4,128)S(1)} %get-tuple-element.82.faces), channel_id=1, source_target_pairs={{0,1},{2,3},{4,5},{6,7},{1,0},{3,2},{5,4},{7,6},{8,9},{10,11},{12,... | collective-permute-start | bytes 245768 | tf_op jit(solution)/shard_map/ppermute | solution.py:494
  33.8 7.5 %collective-permute-start.13 = (f32[16,5,4,128]{3,2,1,0:T(4,128)S(1)}, f32[16,5,4,128]{3,2,1,0:T(4,128)S(1)}, u32[]{:S(2)}, u32[]{:S(2)}) collective-permute-start(f32[16,5,4,128]{3,2,1,0:T(4,128)S(1)} %get-tuple-element.89), channel_id=1, source_target_pairs={{1,2},{3,4},{5,6},{2,1},{4,3},{6,5},{9,10},{11,12},{13,14},{10,9},... | collective-permute-start | bytes 491528 | tf_op jit(solution)/shard_map/ppermute | solution.py:490
  37.4 6.6 %collective-permute-start.14 = (f32[5,2,3072]{2,1,0:T(2,128)S(1)}, f32[5,2,3072]{2,1,0:T(2,128)S(1)}, u32[]{:S(2)}, u32[]{:S(2)}) collective-permute-start(f32[5,2,3072]{2,1,0:T(2,128)S(1)} %tail.13), channel_id=1, source_target_pairs={{0,8},{8,16},{16,24},{24,0},{1,9},{9,17},{17,25},{25,1},{2,10},{10... | collective-permute-start | bytes 368648 | tf_op jit(solution)/shard_map/ppermute | solution.py:499
  37.5 2.9 %collective-permute-start.12 = (f32[8,5,4,128]{3,2,1,0:T(4,128)S(1)}, f32[8,5,4,128]{3,2,1,0:T(4,128)S(1)}, u32[]{:S(2)}, u32[]{:S(2)}) collective-permute-start(f32[8,5,4,128]{3,2,1,0:T(4,128)S(1)} %get-tuple-element.87.faces), channel_id=1, source_target_pairs={{0,1},{2,3},{4,5},{6,7},{1,0},{3,2},{5,4},{7,6},{8,9},{10,11},{12,... | collective-permute-start | bytes 245768 | tf_op jit(solution)/shard_map/ppermute | solution.py:494
  40.6 7.0 %collective-permute-start.16 = (f32[16,5,4,128]{3,2,1,0:T(4,128)S(1)}, f32[16,5,4,128]{3,2,1,0:T(4,128)S(1)}, u32[]{:S(2)}, u32[]{:S(2)}) collective-permute-start(f32[16,5,4,128]{3,2,1,0:T(4,128)S(1)} %get-tuple-element.94), channel_id=1, source_target_pairs={{1,2},{3,4},{5,6},{2,1},{4,3},{6,5},{9,10},{11,12},{13,14},{10,9},... | collective-permute-start | bytes 491528 | tf_op jit(solution)/shard_map/ppermute | solution.py:490
  44.4 6.2 %collective-permute-start.17 = (f32[5,2,3072]{2,1,0:T(2,128)S(1)}, f32[5,2,3072]{2,1,0:T(2,128)S(1)}, u32[]{:S(2)}, u32[]{:S(2)}) collective-permute-start(f32[5,2,3072]{2,1,0:T(2,128)S(1)} %tail.14), channel_id=1, source_target_pairs={{0,8},{8,16},{16,24},{24,0},{1,9},{9,17},{17,25},{25,1},{2,10},{10... | collective-permute-start | bytes 368648 | tf_op jit(solution)/shard_map/ppermute | solution.py:499
  44.5 2.1 %collective-permute-start.15 = (f32[8,5,4,128]{3,2,1,0:T(4,128)S(1)}, f32[8,5,4,128]{3,2,1,0:T(4,128)S(1)}, u32[]{:S(2)}, u32[]{:S(2)}) collective-permute-start(f32[8,5,4,128]{3,2,1,0:T(4,128)S(1)} %get-tuple-element.92.faces), channel_id=1, source_target_pairs={{0,1},{2,3},{4,5},{6,7},{1,0},{3,2},{5,4},{7,6},{8,9},{10,11},{12,... | collective-permute-start | bytes 245768 | tf_op jit(solution)/shard_map/ppermute | solution.py:494
  46.9 8.3 %collective-permute-start.19 = (f32[9,5,16,128]{3,2,1,0:T(8,128)S(1)}, f32[9,5,16,128]{3,2,1,0:T(8,128)S(1)}, u32[]{:S(2)}, u32[]{:S(2)}) collective-permute-start(f32[9,5,16,128]{3,2,1,0:T(8,128)S(1)} %get-tuple-element.99), channel_id=1, source_target_pairs={{1,2},{3,4},{5,6},{2,1},{4,3},{6,5},{9,10},{11,12},{13,14},{10,9},... | collective-permute-start | bytes 1105928 | tf_op jit(solution)/shard_map/ppermute | solution.py:490
  51.1 3.0 %collective-permute-start.18 = (f32[8,5,16,128]{3,2,1,0:T(8,128)S(1)}, f32[8,5,16,128]{3,2,1,0:T(8,128)S(1)}, u32[]{:S(2)}, u32[]{:S(2)}) collective-permute-start(f32[8,5,16,128]{3,2,1,0:T(8,128)S(1)} %get-tuple-element.97.faces), channel_id=1, source_target_pairs={{0,1},{2,3},{4,5},{6,7},{1,0},{3,2},{5,4},{7,6},{8,9},{10,11},{12,... | collective-permute-start | bytes 983048 | tf_op jit(solution)/shard_map/ppermute | solution.py:494
  51.3 6.7 %collective-permute-start.20 = (f32[5,2,3072]{2,1,0:T(2,128)S(1)}, f32[5,2,3072]{2,1,0:T(2,128)S(1)}, u32[]{:S(2)}, u32[]{:S(2)}) collective-permute-start(f32[5,2,3072]{2,1,0:T(2,128)S(1)} %tail.15), channel_id=1, source_target_pairs={{0,8},{8,16},{16,24},{24,0},{1,9},{9,17},{17,25},{25,1},{2,10},{10... | collective-permute-start | bytes 368648 | tf_op jit(solution)/shard_map/ppermute | solution.py:499
  54.5 7.8 %collective-permute-start.22 = (f32[9,5,16,128]{3,2,1,0:T(8,128)S(1)}, f32[9,5,16,128]{3,2,1,0:T(8,128)S(1)}, u32[]{:S(2)}, u32[]{:S(2)}) collective-permute-start(f32[9,5,16,128]{3,2,1,0:T(8,128)S(1)} %get-tuple-element.104), channel_id=1, source_target_pairs={{1,2},{3,4},{5,6},{2,1},{4,3},{6,5},{9,10},{11,12},{13,14},{10,9},... | collective-permute-start | bytes 1105928 | tf_op jit(solution)/shard_map/ppermute | solution.py:490
  58.5 2.7 %collective-permute-start.21 = (f32[8,5,16,128]{3,2,1,0:T(8,128)S(1)}, f32[8,5,16,128]{3,2,1,0:T(8,128)S(1)}, u32[]{:S(2)}, u32[]{:S(2)}) collective-permute-start(f32[8,5,16,128]{3,2,1,0:T(8,128)S(1)} %get-tuple-element.102.faces), channel_id=1, source_target_pairs={{0,1},{2,3},{4,5},{6,7},{1,0},{3,2},{5,4},{7,6},{8,9},{10,11},{12,... | collective-permute-start | bytes 983048 | tf_op jit(solution)/shard_map/ppermute | solution.py:494
  58.7 6.6 %collective-permute-start.23 = (f32[5,2,3072]{2,1,0:T(2,128)S(1)}, f32[5,2,3072]{2,1,0:T(2,128)S(1)}, u32[]{:S(2)}, u32[]{:S(2)}) collective-permute-start(f32[5,2,3072]{2,1,0:T(2,128)S(1)} %tail.16), channel_id=1, source_target_pairs={{0,8},{8,16},{16,24},{24,0},{1,9},{9,17},{17,25},{25,1},{2,10},{10... | collective-permute-start | bytes 368648 | tf_op jit(solution)/shard_map/ppermute | solution.py:499
  61.6 7.2 %collective-permute-start.25 = (f32[9,5,16,128]{3,2,1,0:T(8,128)S(1)}, f32[9,5,16,128]{3,2,1,0:T(8,128)S(1)}, u32[]{:S(2)}, u32[]{:S(2)}) collective-permute-start(f32[9,5,16,128]{3,2,1,0:T(8,128)S(1)} %get-tuple-element.108), channel_id=1, source_target_pairs={{1,2},{3,4},{5,6},{2,1},{4,3},{6,5},{9,10},{11,12},{13,14},{10,9},... | collective-permute-start | bytes 1105928 | tf_op jit(solution)/shard_map/ppermute | solution.py:490
  65.8 2.7 %collective-permute-start.24 = (f32[8,5,16,128]{3,2,1,0:T(8,128)S(1)}, f32[8,5,16,128]{3,2,1,0:T(8,128)S(1)}, u32[]{:S(2)}, u32[]{:S(2)}) collective-permute-start(f32[8,5,16,128]{3,2,1,0:T(8,128)S(1)} %get-tuple-element.107), channel_id=1, source_target_pairs={{0,1},{2,3},{4,5},{6,7},{1,0},{3,2},{5,4},{7,6},{8,9},{10,11},{12,... | collective-permute-start | bytes 983048 | tf_op jit(solution)/shard_map/ppermute | solution.py:494
  66.0 6.7 %collective-permute-start.26 = (f32[5,2,3072]{2,1,0:T(2,128)S(1)}, f32[5,2,3072]{2,1,0:T(2,128)S(1)}, u32[]{:S(2)}, u32[]{:S(2)}) collective-permute-start(f32[5,2,3072]{2,1,0:T(2,128)S(1)} %tail.17), channel_id=1, source_target_pairs={{0,8},{8,16},{16,24},{24,0},{1,9},{9,17},{17,25},{25,1},{2,10},{10... | collective-permute-start | bytes 368648 | tf_op jit(solution)/shard_map/ppermute | solution.py:499

commit v2 on v1

--- a/solution.py
+++ b/solution.py
@@ -19,7 +19,7 @@
 coarse_weight = time_weight / GROUP
 damping = 0.7
 
-UNROLL = 4
+UNROLL = 8
 SCRATCH_BYTES = 4 << 20
 IN_VMEM = pl.BlockSpec(memory_space=pltpu.VMEM)
 NOTHING = pl.CostEstimate(flops=1, bytes_accessed=1, transcendentals=0)
@@ -28,15 +28,18 @@
 IN_SMEM = pl.BlockSpec(memory_space=pltpu.SMEM)
 
 
-def call(kernel, name, tables, arrays, outs, flops=0, scratch=(), out_specs=None):
+def call(kernel, name, tables, arrays, outs, flops=0, scratch=(), out_specs=None, in_place=0):
     arrays = [pltpu.with_memory_space_constraint(a, pltpu.VMEM) for a in arrays]
     size = 4 * (sum(a.size for a in arrays) + sum(o.size for o in outs))
     return pl.pallas_call(
         kernel,
-        out_shape=outs if out_specs else [pltpu.VMEM(o.shape, o.dtype) for o in outs],
+        out_shape=[
+            o if out_specs and out_specs[i] is IN_HBM else pltpu.VMEM(o.shape, o.dtype) for i, o in enumerate(outs)
+        ],
         in_specs=[IN_SMEM] * len(tables) + [IN_VMEM] * len(arrays),
         out_specs=out_specs or [IN_VMEM] * len(outs),
         scratch_shapes=scratch,
+        input_output_aliases={len(tables) + i: i for i in range(in_place)},
         cost_estimate=LONG if name.startswith('rim') else NOTHING,
         compiler_params=pltpu.CompilerParams(vmem_limit_bytes=SCRATCH_BYTES),
         name=name,
@@ -157,24 +160,33 @@
             faces_out[h, a] = field[a, :, lanes]
 
 
-def tail_rows(last_two, weight):
+def tail_rows(last_two, weight, mean):
     last = last_two[1:]
+    if mean:
+        return jnp.concatenate([(weight / GROUP) * (last_two[:1] - 3.0 * last), jnp.zeros_like(last)], axis=0)
     return weight * jnp.concatenate([last_two[:1] - 4.0 * last, last], axis=0)
 
 
-def tail_kernel(weight, rim_weight, field, *refs):
+def send_tail(weights, field, rim, tail_out):
     steps, cells = field.shape[1:]
-    tail_out = refs[-1]
+    weight, mean, rim_weight, rim_mean = weights
     for a in range(NV):
-        last = field[a, pl.ds(steps - 1, 1), :]
-        tail_out[a, pl.ds(0, 1), pl.ds(0, cells)] = weight * (field[a, pl.ds(steps - 2, 1), :] - 4.0 * last)
-        tail_out[a, pl.ds(1, 1), pl.ds(0, cells)] = weight * last
-    if len(refs) > 1:
-        rim = refs[0]
-        for h in range(rim.shape[0]):
+        before, last = field[a, pl.ds(steps - 2, 1), :], field[a, pl.ds(steps - 1, 1), :]
+        if mean:
+            tail_out[a, pl.ds(0, 1), pl.ds(0, cells)] = (weight / GROUP) * (before - 3.0 * last)
+            tail_out[a, pl.ds(1, 1), pl.ds(0, cells)] = jnp.zeros_like(last)
+        else:
+            tail_out[a, pl.ds(0, 1), pl.ds(0, cells)] = weight * (before - 4.0 * last)
+            tail_out[a, pl.ds(1, 1), pl.ds(0, cells)] = weight * last
+    if rim is not None:
+        for h in range((tail_out.shape[2] - cells) // BLK):
             for a in range(NV):
-                rows = tail_rows(rim[h, a, pl.ds(rim.shape[2] - 2, 2), :], rim_weight)
+                rows = tail_rows(rim[h, a, pl.ds(rim.shape[2] - 2, 2), :], rim_weight, rim_mean)
                 tail_out[a, :, pl.ds(cells + h * BLK, BLK)] = rows
+
+
+def tail_kernel(weights, field, *refs):
+    send_tail(weights, field, refs[0] if len(refs) > 1 else None, refs[-1])
 
 
 def own_kernel(weight, table, field, goal, jacobian, self_block, cell_diag, out):
@@ -302,7 +314,7 @@
         return self.row(h, NV * (NV + self.level) + a)
 
 
-def index_kernel(steps, message, index):
+def index_kernel(steps, message, next_message, index):
     partner = Partner(message, steps, 0)
     for h in range(index.shape[0]):
         index[h] = jnp.max(partner.row(h, NV * (NV + 2))).astype(jnp.int32)
@@ -353,132 +365,184 @@
     each_block(index.shape[0], step)
 
 
-def less_rows(total, rows):
-    pad = total.shape[0] - rows.shape[0]
-    if pad:
-        rows = jnp.concatenate([rows, jnp.zeros((pad, BLK), jnp.float32)], axis=0)
-    return total - rows
-
-
-def mean_tail(rows):
-    return (rows[:1] + rows[1:]) * (1.0 / GROUP)
+def padded(rows, count):
+    pad = count - rows.shape[0]
+    return jnp.concatenate([rows, jnp.zeros((pad, BLK), jnp.float32)], axis=0) if pad > 0 else rows
 
 
 def spread_tail(rows):
     return jnp.concatenate([jnp.broadcast_to(rows[i : i + 1], (GROUP, BLK)) for i in range(2)], axis=0)
 
 
-def finish_rim(rim, tail, cells, partner, shape_tail, rim_out):
+def rim_tail(h, a, tail, cells, partner, spread):
+    rows = tail[a, :, pl.ds(pl.multiple_of(cells + h * BLK, BLK), BLK)]
+    rows = partner.point(h, a) * rows
+    return spread_tail(rows) if spread else rows
+
+
+def finish_kernel(steps, level, spread, rim, tail, first_message, rim_out):
+    partner = Partner(first_message, steps, level)
+    cells = tail.shape[2] - rim.shape[0] * BLK
+
     def step(h, u):
-        lanes = pl.ds(pl.multiple_of(cells + h * BLK, BLK), BLK)
-        for a in range(NV):
-            rim_out[h, a] = less_rows(rim[h, a], shape_tail(partner.point(h, a) * tail[a, :, lanes]))
+        for a in range(NV):
+            rows = rim_tail(h, a, tail, cells, partner, spread)
+            rim_out[h, a] = rim[h, a] - padded(rows, rim.shape[2])
 
     each_block(rim.shape[0], step)
 
 
-def rest_part(b, part, rim, tail, table, rim_jacobian, shape_tail=lambda rows: rows):
+def rest_part(b, part, rim, table, rim_jacobian):
     lanes = lanes_of(b)
-    total = [less_rows(part[a, :, lanes], shape_tail(tail[a, :, lanes])) for a in range(NV)]
-    return rim_part(0, total, b, rim, table, rim_jacobian)
-
-
-def first_sweep_kernel(table, listed, field, part, rim, tail, rim_jacobian, points, out, faces_out):
-    def step(b, u):
-        lanes = lanes_of(b)
-        total = rest_part(b, part, rim, tail, table, rim_jacobian)
+    return rim_part(0, [part[a, :, lanes] for a in range(NV)], b, rim, table, rim_jacobian)
+
+
+def sweep_kernel(weights, table, field, part, rim, rim_jacobian, points, out, *tail_out):
+    def step(b, u):
+        lanes = lanes_of(b)
+        total = rest_part(b, part, rim, table, rim_jacobian)
         for a in range(NV):
             out[a, :, lanes] = field[a, :, lanes] + points[pl.ds(a, 1), lanes] * total[a]
+
+    each_block(table.shape[1], step)
+    if tail_out:
+        send_tail(weights, out, rim, tail_out[0])
+
+
+def first_correction_kernel(weights, table, part, rim, last_rows, rim_jacobian, points, out, defect_out, *tail_out):
+    def step(b, u):
+        lanes = lanes_of(b)
+        total = rest_part(b, part, rim, table, rim_jacobian)
+        for a in range(NV):
+            defect_out[a, :, lanes] = total[a]
+            out[a, :, lanes] = points[pl.ds(a, 1), lanes] * total[a]
+
+    each_block(table.shape[1], step)
+    if tail_out:
+        send_tail(weights, out, last_rows, tail_out[0])
+
+
+def corrected_kernel(weights, table, field, part, rim, fine, rim_jacobian, points, out, *refs):
+    scratch = refs[-1]
+
+    def step(b, u):
+        lanes = lanes_of(b)
+        total = rest_part(b, part, rim, table, rim_jacobian)
+        for a in range(NV):
+            v = field[a, :, lanes] + points[pl.ds(a, 1), lanes] * total[a]
+            out[a, :, lanes] = fine[a, :, lanes] + spread_rows(v, scratch.at[u, a])
+
+    each_block(table.shape[1], step)
+    if len(refs) > 1:
+        send_tail(weights, out, rim, refs[0])
+
+
+def last_own_kernel(weight, table, field, goal, jacobian, self_block, cell_diag, out, updated, sem):
+    copy = pltpu.make_async_copy(field, updated, sem)
+    copy.start()
+    own_kernel(weight, table, field, goal, jacobian, self_block, cell_diag, out)
+    copy.wait()
+
+
+def last_rim_kernel(steps, index, faces, message, tail, first_message, out):
+    rim_kernel(steps, 0, index, faces, message, first_message, out)
+    partner = Partner(first_message, steps, 0)
+    cells = tail.shape[2] - index.shape[0] * BLK
+
+    def step(h, u):
+        for a in range(NV):
+            out[h, a, pl.ds(0, 2), :] = out[h, a, pl.ds(0, 2), :] - rim_tail(h, a, tail, cells, partner, False)
+
+    each_block(index.shape[0], step)
+
+
+def residual_kernel(table, part, rim, tail, rim_jacobian, out, held, sems):
+    blocks = table.shape[1]
+
+    def send(b):
+        lanes = lanes_of(b)
+        return pltpu.make_async_copy(held.at[:, :, lanes], out.at[:, :, lanes], sems.at[b])
+
+    def step(b, u):
+        lanes = lanes_of(b)
+        total = rest_part(b, part, rim, table, rim_jacobian)
+        for a in range(NV):
+            held[a, :, lanes] = total[a]
+            add_rows(held, a, lanes, -tail[a, :, lanes])
+        send(b).start()
+
+    each_block(blocks, step)
+    each_block(blocks, lambda b, u: send(b).wait())
+
+
+def earlier_steps(b, tail, table, rim_jacobian, partner, spread):
+    lanes = lanes_of(b)
+    total = [-tail[a, :, lanes] for a in range(NV)]
+    if partner is None:
+        return total
+    if spread:
+        total = [padded(rows, 2 * GROUP) for rows in total]
+    cells = table.shape[1] * BLK
+    block = table[0, b]
+    values = [-rim_tail(block, j, tail, cells, partner, spread) for j in range(NV)]
+    return coupled(total, lambda a, j: rim_jacobian[0, a, pl.ds(j, 1), lanes], values)
+
+
+def add_rows(out, a, lanes, rows):
+    first = pl.ds(0, rows.shape[0])
+    out[a, first, lanes] = out[a, first, lanes] + rows
+
+
+def partner_of(first_message, steps, level):
+    return None if level is None else Partner(first_message, steps, level)
+
+
+def finish_sweep_kernel(
+    steps, level, spread, spread_out, table, listed, field, tail, first_message, rim_jacobian, points, out, faces_out
+):
+    partner = partner_of(first_message, steps, level)
+
+    def step(b, u):
+        lanes = lanes_of(b)
+        total = earlier_steps(b, tail, table, rim_jacobian, partner, spread)
+        for a in range(NV):
+            rows = points[pl.ds(a, 1), lanes] * total[a]
+            add_rows(out, a, lanes, spread_tail(rows) if spread_out else rows)
 
     each_block(table.shape[1], step)
     pick_faces(listed, out, faces_out)
 
 
-def sweep_kernel(
-    steps, level, shape_tail, table, listed, field, part, rim, tail, first_message, rim_jacobian, points,
-    out, faces_out, rim_out,
+def finish_smoothed_kernel(
+    steps, level, table, listed, field, tail, first_message, rim_jacobian, points, out, means_out, faces_out, scratch
 ):
-    finish_rim(rim, tail, field.shape[2], Partner(first_message, steps, level), shape_tail, rim_out)
-    first_sweep_kernel(table, listed, field, part, rim_out, tail, rim_jacobian, points, out, faces_out)
-
-
-def smoothed_kernel(
-    table, listed, field, part, rim, tail, first_message, rim_jacobian, points,
-    out, means_out, faces_out, rim_out, scratch,
-):
-    steps = means_out.shape[1]
-    partner = Partner(first_message, field.shape[1], 0)
-    finish_rim(rim, tail, field.shape[2], partner, lambda rows: rows, rim_out)
-
-    def step(b, u):
-        lanes = lanes_of(b)
-        total = rest_part(b, part, rim_out, tail, table, rim_jacobian)
-        for a in range(NV):
-            v = field[a, :, lanes] + points[pl.ds(a, 1), lanes] * total[a]
-            out[a, :, lanes] = v
-            means_out[a, :, lanes] = mean_rows(v, scratch.at[u, a], steps)
+    partner = partner_of(first_message, steps, level)
+
+    def step(b, u):
+        lanes = lanes_of(b)
+        total = earlier_steps(b, tail, table, rim_jacobian, partner, False)
+        for a in range(NV):
+            add_rows(out, a, lanes, points[pl.ds(a, 1), lanes] * total[a])
+            means_out[a, :, lanes] = mean_rows(out[a, :, lanes], scratch.at[u, a], means_out.shape[1])
 
     each_block(table.shape[1], step)
     pick_faces(listed, means_out, faces_out)
 
 
-def first_correction_kernel(
-    steps, table, listed, part, rim, tail, first_message, rim_jacobian, points, defect_out, out, faces_out, rim_out
+def finish_correction_kernel(
+    steps, level, table, listed, field, defect, tail, first_message, rim_jacobian, points, out, defect_out, faces_out
 ):
-    finish_rim(rim, tail, part.shape[2], Partner(first_message, steps, 0), mean_tail, rim_out)
-
-    def step(b, u):
-        lanes = lanes_of(b)
-        total = rest_part(b, part, rim_out, tail, table, rim_jacobian, mean_tail)
-        for a in range(NV):
-            defect_out[a, :, lanes] = total[a]
-            out[a, :, lanes] = points[pl.ds(a, 1), lanes] * total[a]
+    partner = partner_of(first_message, steps, level)
+
+    def step(b, u):
+        lanes = lanes_of(b)
+        total = earlier_steps(b, tail, table, rim_jacobian, partner, False)
+        for a in range(NV):
+            add_rows(defect_out, a, lanes, total[a])
+            add_rows(out, a, lanes, points[pl.ds(a, 1), lanes] * total[a])
 
     each_block(table.shape[1], step)
     pick_faces(listed, out, faces_out)
-
-
-def corrected_kernel(
-    steps, table, listed, field, part, rim, tail, fine, first_message, rim_jacobian, points,
-    out, faces_out, rim_out, scratch,
-):
-    partner = Partner(first_message, steps, 1)
-    finish_rim(rim, tail, field.shape[2], partner, lambda rows: rows, rim_out)
-
-    def step(b, u):
-        lanes = lanes_of(b)
-        total = rest_part(b, part, rim_out, tail, table, rim_jacobian)
-        for a in range(NV):
-            v = field[a, :, lanes] + points[pl.ds(a, 1), lanes] * total[a]
-            out[a, :, lanes] = fine[a, :, lanes] + spread_rows(v, scratch.at[u, a])
-
-    each_block(table.shape[1], step)
-    pick_faces(listed, out, faces_out)
-
-
-def residual_kernel(
-    steps, table, field, part, rim, tail, first_message, rim_jacobian, updated, out, scratch, finished, sems
-):
-    blocks = table.shape[1]
-    copy = pltpu.make_async_copy(field, updated, sems.at[blocks])
-    copy.start()
-    partner = Partner(first_message, steps, 0)
-    finish_rim(rim, tail, part.shape[2], partner, lambda rows: rows, finished)
-
-    def send(b):
-        lanes = lanes_of(b)
-        return pltpu.make_async_copy(scratch.at[:, :, lanes], out.at[:, :, lanes], sems.at[b])
-
-    def step(b, u):
-        lanes = lanes_of(b)
-        total = rest_part(b, part, finished, tail, table, rim_jacobian)
-        for a in range(NV):
-            scratch[a, :, lanes] = total[a]
-        send(b).start()
-
-    each_block(blocks, step)
-    each_block(blocks, lambda b, u: send(b).wait())
-    copy.wait()
 
 
 def neighbour_pairs(first):
@@ -518,7 +582,7 @@
         first_kernel,
         out_shape=[
             pltpu.SMEM((K, blocks), jnp.int32), pltpu.SMEM((faces,), jnp.int32),
-            pltpu.VMEM((NV, steps, cells), jnp.float32), pltpu.VMEM((faces, NV, steps, BLK), jnp.float32),
+            pltpu.VMEM((NV, steps, cells), jnp.float32), pltpu.VMEM(face(steps).shape, jnp.float32),
         ],
         in_specs=[IN_HBM] * 3,
         out_specs=[IN_SMEM] * 2 + [IN_VMEM] * 2,
@@ -551,13 +615,14 @@
             [whole(n)], 5 * per_slot * n,
         )[0]
 
-    def tail_of(field, weight, rim=None, rim_weight=None):
-        arrays = [field] if rim is None else [field, rim]
-        out = shape(NV, 2, cells + (0 if rim is None else faces * BLK))
-        return to_later(call(bind(tail_kernel, weight, rim_weight), "tail", [], arrays, [out])[0])
+    ahead = coarse >= 4
+    tail_shape = shape(NV, 2, cells + faces * BLK)
 
     state = start
-    tail = tail_of(state, time_weight)
+    first_tail = call(
+        bind(tail_kernel, (time_weight, False, None, None)), "tail", [], [state], [shape(NV, 2, cells)]
+    )[0]
+    tail = to_later(first_tail)
     part = own(time_weight, steps, state, goal)
     part, message = call(
         first_message_kernel, "first_message", tables,
@@ -567,37 +632,80 @@
     first_message = over_chips(message)
     message = first_message
     earlier_sent = sent
-    state, sent = call(
-        first_sweep_kernel, "first_sweep", tables, [state, part, rim, tail, rim_jacobian, fine_points],
-        [whole(steps), face(steps)], per_slot * steps,
+
+    def plan(weights, tail, level, spread=False):
+        def ready(rim):
+            if ahead or level is None:
+                return rim, level
+            return call(
+                bind(finish_kernel, steps, level, spread), "finish_rim", [], [rim, tail, first_message],
+                [shape(*rim.shape)],
+            )[0], None
+
+        return ready
+
+    def sweep(kernel, name, arrays, behind, outs, rim, weights, tail, level, spread, finisher, scratch=(), tail_rim=None):
+        rim, level = plan(weights, tail, level, spread)(rim)
+        sources = rim if tail_rim is None else tail_rim
+        extra = [] if tail_rim is None else [tail_rim]
+        results = call(
+            bind(kernel, weights), name, [table], arrays + [rim] + extra + behind,
+            outs + [tail_shape] * ahead, per_slot * steps, scratch,
+        )
+        if ahead:
+            next_tail = to_later(results[-1])
+            results = results[:-1]
+        finished = finisher(results, tail, level)
+        if not ahead:
+            next_tail = to_later(call(bind(tail_kernel, weights), "tail", [], [finished[0], sources], [tail_shape])[0])
+        return finished, next_tail, rim
+
+    def finish_with(points, n, spread=False, spread_out=False):
+        def finisher(results, tail, level):
+            return call(
+                bind(finish_sweep_kernel, steps, level, spread, spread_out), "finish_sweep", tables,
+                [results[0], tail, points if level is None else first_message, rim_jacobian, points],
+                [whole(n), face(n)], 0, (), None, 1,
+            )
+
+        return finisher
+
+    fine_weights = (time_weight, False, time_weight, False)
+    (state, sent), tail, rim = sweep(
+        sweep_kernel, "first_sweep", [state, part], [rim_jacobian, fine_points], [whole(steps)], rim, fine_weights,
+        tail, None, False, finish_with(fine_points, steps),
     )
-    index = pl.pallas_call(
-        bind(index_kernel, steps), out_shape=pltpu.SMEM((faces,), jnp.int32), in_specs=[IN_VMEM],
-        out_specs=IN_SMEM, name="coupled_faces", cost_estimate=NOTHING,
-        compiler_params=pltpu.CompilerParams(vmem_limit_bytes=SCRATCH_BYTES),
-    )(pltpu.with_memory_space_constraint(first_message, pltpu.VMEM))
-
     beside = on_chip(sent)
-    tail = tail_of(state, time_weight, rim, time_weight)
     part = own(time_weight, steps, state, goal)
     part, next_message = call(
         means_message_kernel, "message_of_means", tables, [state, part, beside, rim_jacobian, fine_points],
         [whole(steps), face(coarse + 2)], per_slot * steps, rows_scratch,
     )
+    index = pl.pallas_call(
+        bind(index_kernel, steps), out_shape=pltpu.SMEM((faces,), jnp.int32), in_specs=[IN_VMEM] * 2,
+        out_specs=IN_SMEM, name="coupled_faces", cost_estimate=NOTHING,
+        compiler_params=pltpu.CompilerParams(vmem_limit_bytes=SCRATCH_BYTES),
+    )(*[pltpu.with_memory_space_constraint(x, pltpu.VMEM) for x in (first_message, next_message)])
     next_message = over_chips(next_message)
     rim = call(
         bind(rim_kernel, steps, 0), "rim", [index], [earlier_sent, message, first_message], [face(steps)],
         per_slot * steps // 2,
     )[0]
     message, earlier_sent = next_message, sent
-    state, means, sent, rim = call(
-        smoothed_kernel, "sweep_and_means", tables,
-        [state, part, rim, tail, first_message, rim_jacobian, fine_points],
-        [whole(steps), whole(coarse), face(coarse), face(steps)], per_slot * steps, rows_scratch,
+
+    def finish_smoothed(results, tail, level):
+        return call(
+            bind(finish_smoothed_kernel, steps, level), "finish_and_means", tables,
+            [results[0], tail, first_message, rim_jacobian, fine_points],
+            [whole(steps), whole(coarse), face(coarse)], 0, rows_scratch, None, 1,
+        )
+
+    (state, means, sent), tail, rim = sweep(
+        sweep_kernel, "sweep", [state, part], [rim_jacobian, fine_points], [whole(steps)], rim,
+        (time_weight, True, time_weight, True), tail, 0, False, finish_smoothed,
     )
 
     beside = on_chip(sent)
-    tail = tail_of(state, time_weight, rim, time_weight)
     part = call(
         bind(means_kernel, time_weight), "own_part_of_means", [table],
         [state, goal, means, jacobian, self_block, cell_diag], [whole(coarse)], 5 * per_slot * coarse, rows_scratch,
@@ -612,16 +720,22 @@
         [face(coarse), face(2)], per_slot * steps // 2, rows_scratch,
     )
     message, earlier_sent = next_message, sent
-    defect, correction, sent, rim = call(
-        bind(first_correction_kernel, steps), "first_correction", tables,
-        [part, rim, tail, first_message, rim_jacobian, coarse_points],
-        [whole(coarse), whole(coarse), face(coarse), face(coarse)], per_slot * coarse,
+
+    def finish_correction(results, tail, level):
+        return call(
+            bind(finish_correction_kernel, steps, level), "finish_correction", tables,
+            [*results, tail, first_message, rim_jacobian, coarse_points],
+            [whole(coarse), whole(coarse), face(coarse)], 0, (), None, 2,
+        )
+
+    (correction, defect, sent), tail, rim = sweep(
+        first_correction_kernel, "first_correction", [part], [rim_jacobian, coarse_points],
+        [whole(coarse), whole(coarse)], rim, (coarse_weight, False, time_weight, True), tail, 0, False,
+        finish_correction, (), last_rows,
     )
 
-    rim, rim_weight, shape_tail = last_rows, time_weight, mean_tail
     for sweep_no in range(NUC - 1):
         beside = on_chip(sent)
-        tail = tail_of(correction, coarse_weight, rim, rim_weight)
         part = own(coarse_weight, coarse, correction, defect)
         last = sweep_no == NUC - 2
         if last:
@@ -642,63 +756,57 @@
         )[0]
         message, earlier_sent = next_message, sent
         if last:
-            state, sent, rim = call(
-                bind(corrected_kernel, steps), "corrected", tables,
-                [correction, part, rim, tail, state, first_message, rim_jacobian, coarse_points],
-                [whole(steps), face(steps), face(coarse)], per_slot * coarse, rows_scratch,
+            (state, sent), tail, rim = sweep(
+                corrected_kernel, "corrected", [correction, part], [state, rim_jacobian, coarse_points],
+                [whole(steps)], rim, (time_weight, False, coarse_weight, False), tail, 1, False,
+                finish_with(coarse_points, steps, False, True), rows_scratch,
             )
         else:
-            correction, sent, rim = call(
-                bind(sweep_kernel, steps, 1, shape_tail), "coarse_sweep", tables,
-                [correction, part, rim, tail, first_message, rim_jacobian, coarse_points],
-                [whole(coarse), face(coarse), face(coarse)], per_slot * coarse,
+            (correction, sent), tail, rim = sweep(
+                sweep_kernel, "coarse_sweep", [correction, part], [rim_jacobian, coarse_points], [whole(coarse)],
+                rim, (coarse_weight, False, coarse_weight, False), tail, 1, False, finish_with(coarse_points, coarse),
             )
-        rim_weight, shape_tail = coarse_weight, plain
 
     for sweep_no in range(NU2 + 1):
         beside = on_chip(sent)
-        tail = tail_of(state, time_weight, rim, rim_weight)
+        if sweep_no == NU2:
+            break
         part = own(time_weight, steps, state, goal)
-        last = sweep_no == NU2
-        if last:
-            part = call(
-                beside_part, "beside_part", [table], [part, beside, rim_jacobian], [whole(steps)], per_slot * steps
-            )[0]
-        else:
-            part, next_message = call(
-                message_kernel, "message", tables, [state, part, beside, rim_jacobian, fine_points],
-                [whole(steps), spare(1, steps)], per_slot * steps,
-            )
-            next_message = over_chips(next_message)
+        part, next_message = call(
+            message_kernel, "message", tables, [state, part, beside, rim_jacobian, fine_points],
+            [whole(steps), spare(1, steps)], per_slot * steps,
+        )
+        next_message = over_chips(next_message)
         if sweep_no == 0:
             rim = call(
                 bind(corrected_rim_kernel, steps), "rim_of_corrected", [index],
                 [earlier_sent, message, first_message], [face(steps)], per_slot * coarse // 2, rows_scratch,
             )[0]
-            level, shape_tail = 1, spread_tail
         else:
             rim = call(
                 bind(rim_kernel, steps, 0), "rim", [index], [earlier_sent, message, first_message],
                 [face(steps)], per_slot * steps // 2,
             )[0]
-            level, shape_tail = 0, plain
-        if not last:
-            message, earlier_sent = next_message, sent
-            state, sent, rim = call(
-                bind(sweep_kernel, steps, level, shape_tail), "sweep", tables,
-                [state, part, rim, tail, first_message, rim_jacobian, fine_points],
-                [whole(steps), face(steps), face(steps)], per_slot * steps,
-            )
-        rim_weight = time_weight
-    updated, residual = call(
-        bind(residual_kernel, steps), "residual", [table], [state, part, rim, tail, first_message, rim_jacobian],
-        [whole(steps)] * 2, per_slot * steps,
-        [
-            pltpu.VMEM((NV, steps, cells), jnp.float32), pltpu.VMEM((faces, NV, steps, BLK), jnp.float32),
-            pltpu.SemaphoreType.DMA((blocks + 1,)),
-        ],
-        [IN_HBM] * 2,
+        message, earlier_sent = next_message, sent
+        spread = sweep_no == 0
+        (state, sent), tail, rim = sweep(
+            sweep_kernel, "sweep", [state, part], [rim_jacobian, fine_points], [whole(steps)], rim, fine_weights,
+            tail, 1 if spread else 0, spread, finish_with(fine_points, steps, spread),
+        )
+    part, updated = call(
+        bind(last_own_kernel, time_weight), "last_own_part", [table],
+        [state, goal, jacobian, self_block, cell_diag], [whole(steps)] * 2, 5 * per_slot * steps,
+        [pltpu.SemaphoreType.DMA], [IN_VMEM, IN_HBM],
     )
+    part = call(beside_part, "beside_part", [table], [part, beside, rim_jacobian], [whole(steps)], per_slot * steps)[0]
+    rim = call(
+        bind(last_rim_kernel, steps), "rim", [index], [earlier_sent, message, tail, first_message], [face(steps)],
+        per_slot * steps // 2,
+    )[0]
+    residual = call(
+        residual_kernel, "residual", [table], [part, rim, tail, rim_jacobian], [whole(steps)], per_slot * steps,
+        [pltpu.VMEM((NV, steps, cells), jnp.float32), pltpu.SemaphoreType.DMA((blocks,))], [IN_HBM],
+    )[0]
     return jnp.transpose(updated, (1, 0, 2)), jnp.transpose(residual, (1, 0, 2))
 
 

time: 74.2 us -> 72.5 us (0.977)
  waiting for transfers between devices: 19.6 us -> 11.8 us
  starting transfers between devices: 27.7 us -> 34.7 us
  Pallas kernels: 25.4 us -> 24.3 us
    ppermute x9, waiting for transfers between devices: 19.5 us -> 11.6 us  [to_later(): lax.ppermute(tail, 'tm', [(i, (i + 1) % periods) for i in range(periods)])]
    ppermute x9, starting transfers between devices: 8.5 us -> 12.2 us  [to_later(): lax.ppermute(tail, 'tm', [(i, (i + 1) % periods) for i in range(periods)])]
    ppermute x9, starting transfers between devices: 13.1 us -> 16.4 us  [on_chip(): return lax.ppermute(faces, 'space', neighbour_pairs(0))]
    pallas_call x44, Pallas kernels: 22.2 us -> 21.1 us  [call(): pl.pallas_call(kernel, out_shape=[o if out_specs and out_specs[i] is IN_H...]
  transfers between devices with their start and end apart: 27 -> 27, of which waited for: 8 -> 8; matrix products, arithmetic and copies ran while one was open for 0% -> 0% of each run, Pallas kernels for 31% -> 30%
where the time goes in v2:
time: 72.5 us; the launch traced here: 72.1 us
  starting transfers between devices  34.7 us (48%)
  Pallas kernels  24.3 us (34%)
  waiting for transfers between devices  11.8 us (16%)
  between operations  1.28 us (2%)
    pallas_call x44, Pallas kernels, call(): pl.pallas_call(kernel, out_shape=[o if out_specs and out_specs[i] is IN_H...  21.1 us
    ppermute x9, starting transfers between devices, on_chip(): return lax.ppermute(faces, 'space', neighbour_pairs(0))  16.4 us
    ppermute x9, starting transfers between devices, to_later(): lax.ppermute(tail, 'tm', [(i, (i + 1) % periods) for i in range(periods)])  12.2 us
    ppermute x9, waiting for transfers between devices, to_later(): lax.ppermute(tail, 'tm', [(i, (i + 1) % periods) for i in range(periods)])  11.6 us
    ppermute x9, starting transfers between devices, over_chips(): return lax.ppermute(message, 'space', neighbour_pairs(1))  6.1 us
    pallas_call x1, Pallas kernels, body(): pl.pallas_call(arguments_kernel, out_shape=[pltpu.VMEM(x.shape, jnp.float...  1.88 us
  transfers between devices with their start and end apart: 27, of which 8 were waited for; matrix products, arithmetic and copies ran while one was open for 0% of the time, Pallas kernels for 30%

profile of v2, /device:TPU:0, one launch (start us, length us, event | category | flops | bytes accessed | tf_op | source)
XLA Modules:
  0.0 72.1 jit_solution(383942572500996814)
XLA Ops:
  0.6 1.2 %iterate_and_tables.1 = (s32[6,16]{1,0:T(8,128)S(4)}, s32[8]{0:T(128)S(4)}, f32[5,16,2048]{2,1,0:T(8,128)S(1)}, f32[8,5,16,128]{3,2,1,0:T(8,128)S(1)}) custom-call(s32[6,16]{1,0:T(8,128)} %bitcast.10, s32[8]{0:T(128)} %face_list.1, f32[5,16,2048]{2,1,0:T(8,128)} %bitcast.7), custom_call_target="tpu_custom_call" | custom-call | flops 1 | bytes 1 | tf_op jit(solution)/shard_map/iterate_and_tables/pallas_call | solution.py:581
  3.0 2.6 %collective-permute-start.1 = (f32[5,2,2048]{2,1,0:T(2,128)S(1)}, f32[5,2,2048]{2,1,0:T(2,128)S(1)}, u32[]{:S(2)}, u32[]{:S(2)}) collective-permute-start(f32[5,2,2048]{2,1,0:T(2,128)S(1)} %tail.1), channel_id=1, source_target_pairs={{0,8},{8,16},{16,24},{24,0},{1,9},{9,17},{17,25},{25,1},{2,10},{10... | collective-permute-start | bytes 245768 | tf_op jit(solution)/shard_map/ppermute | solution.py:563
  5.6 1.9 %arguments.1 = (f32[5,2048]{1,0:T(8,128)S(1)}, f32[5,5,6,2048]{3,2,1,0:T(8,128)S(1)}, f32[5,5,2048]{2,1,0:T(8,128)S(1)}, f32[5,16,2048]{2,1,0:T(8,128)S(1)}, f32...) custom-call(s32[8]{0:T(128)S(4)} %get-tuple-element.69.listed, f32[5,2048]{1,0:T(8,128)} %refs_0_.1, ...), custom_call_target="tpu_custom_call" | custom-call | flops 1 | bytes 1 | tf_op jit(solution)/shard_map/arguments/pallas_call | solution.py:601
  7.5 1.5 %own_part.7.part = f32[5,16,2048]{2,1,0:T(8,128)S(1)} custom-call(s32[6,16]{1,0:T(8,128)S(4)} %get-tuple-element.68.table, f32[5,16,2048]{2,1,0:T(8,128)S(1)} %get-tuple-element.70.field, f32[5,16,2048]{2,1,0:T(8,128)S(1)} %get-tuple-element.71.goal, f32[5,5,6,2048]{3,2,1,0:T(8,128)S(1)} %get-tuple-element.72.jacobian, ...), custom_call_target="tpu_custom_call" | custom-call | flops 1 | bytes 1 | tf_op jit(solution)/shard_map/own_part/pallas_call | solution.py:34
  10.7 5.0 %collective-permute-start.3 = (f32[8,5,16,128]{3,2,1,0:T(8,128)S(1)}, f32[8,5,16,128]{3,2,1,0:T(8,128)S(1)}, u32[]{:S(2)}, u32[]{:S(2)}) collective-permute-start(f32[8,5,16,128]{3,2,1,0:T(8,128)S(1)} %get-tuple-element.82.faces), channel_id=1, source_target_pairs={{0,1},{2,3},{4,5},{6,7},{1,0},{3,2},{5,4},{7,6},{8,9},{10,11},{12,... | collective-permute-start | bytes 983048 | tf_op jit(solution)/shard_map/ppermute | solution.py:558
  15.7 1.5 %collective-permute-start.5 = (f32[5,2,3072]{2,1,0:T(2,128)S(1)}, f32[5,2,3072]{2,1,0:T(2,128)S(1)}, u32[]{:S(2)}, u32[]{:S(2)}) collective-permute-start(f32[5,2,3072]{2,1,0:T(2,128)S(1)} %get-tuple-element.87), channel_id=1, source_target_pairs={{0,8},{8,16},{16,24},{24,0},{1,9},{9,17},{17,25},{25,1},{2,10},{10... | collective-permute-start | bytes 368648 | tf_op jit(solution)/shard_map/ppermute | solution.py:563
  17.2 1.5 %own_part.8.part = f32[5,16,2048]{2,1,0:T(8,128)S(1)} custom-call(s32[6,16]{1,0:T(8,128)S(4)} %get-tuple-element.68.table, f32[5,16,2048]{2,1,0:T(8,128)S(1)} %get-tuple-element.81.field, f32[5,16,2048]{2,1,0:T(8,128)S(1)} %get-tuple-element.71.goal, f32[5,5,6,2048]{3,2,1,0:T(8,128)S(1)} %get-tuple-element.72.jacobian, ...), custom_call_target="tpu_custom_call" | custom-call | flops 1 | bytes 1 | tf_op jit(solution)/shard_map/own_part/pallas_call | solution.py:34
  20.6 1.3 %collective-permute-done.5.tail = f32[5,2,3072]{2,1,0:T(2,128)S(1)} collective-permute-done((f32[5,2,3072]{2,1,0:T(2,128)S(1)}, f32[5,2,3072]{2,1,0:T(2,128)S(1)}, u32[]{:S(2)}, u32[]{:S(2)}) %collective-permute-start.5) | collective-permute-done | bytes 122912 | tf_op jit(solution)/shard_map/ppermute | solution.py:563
  22.4 1.7 %collective-permute-start.6 = (f32[8,5,4,128]{3,2,1,0:T(4,128)S(1)}, f32[8,5,4,128]{3,2,1,0:T(4,128)S(1)}, u32[]{:S(2)}, u32[]{:S(2)}) collective-permute-start(f32[8,5,4,128]{3,2,1,0:T(4,128)S(1)} %get-tuple-element.90.faces), channel_id=1, source_target_pairs={{0,1},{2,3},{4,5},{6,7},{1,0},{3,2},{5,4},{7,6},{8,9},{10,11},{12,... | collective-permute-start | bytes 245768 | tf_op jit(solution)/shard_map/ppermute | solution.py:558
  24.1 2.4 %collective-permute-start.8 = (f32[5,2,3072]{2,1,0:T(2,128)S(1)}, f32[5,2,3072]{2,1,0:T(2,128)S(1)}, u32[]{:S(2)}, u32[]{:S(2)}) collective-permute-start(f32[5,2,3072]{2,1,0:T(2,128)S(1)} %get-tuple-element.96), channel_id=1, source_target_pairs={{0,8},{8,16},{16,24},{24,0},{1,9},{9,17},{17,25},{25,1},{2,10},{10... | collective-permute-start | bytes 368648 | tf_op jit(solution)/shard_map/ppermute | solution.py:563
  26.5 1.1 %own_part_of_means.1.part = f32[5,4,2048]{2,1,0:T(4,128)S(1)} custom-call(s32[6,16]{1,0:T(8,128)S(4)} %get-tuple-element.68.table, f32[5,16,2048]{2,1,0:T(8,128)S(1)} %get-tuple-element.88.field.fine, f32[5,16,2048]{2,1,0:T(8,128)S(1)} %get-tuple-element.71.goal, f32[5,4,2048]{2,1,0:T(4,128)S(1)} %get-tuple-element.89.means, ...), custom_call_target="tpu_custom_call" | custom-call | flops 1 | bytes 1 | tf_op jit(solution)/shard_map/own_part_of_means/pallas_call | solution.py:34
  29.5 0.7 %collective-permute-done.8.tail = f32[5,2,3072]{2,1,0:T(2,128)S(1)} collective-permute-done((f32[5,2,3072]{2,1,0:T(2,128)S(1)}, f32[5,2,3072]{2,1,0:T(2,128)S(1)}, u32[]{:S(2)}, u32[]{:S(2)}) %collective-permute-start.8) | collective-permute-done | bytes 122912 | tf_op jit(solution)/shard_map/ppermute | solution.py:563
  30.5 2.1 %collective-permute-start.9 = (f32[8,5,4,128]{3,2,1,0:T(4,128)S(1)}, f32[8,5,4,128]{3,2,1,0:T(4,128)S(1)}, u32[]{:S(2)}, u32[]{:S(2)}) collective-permute-start(f32[8,5,4,128]{3,2,1,0:T(4,128)S(1)} %get-tuple-element.99.faces), channel_id=1, source_target_pairs={{0,1},{2,3},{4,5},{6,7},{1,0},{3,2},{5,4},{7,6},{8,9},{10,11},{12,... | collective-permute-start | bytes 245768 | tf_op jit(solution)/shard_map/ppermute | solution.py:558
  32.6 0.8 %own_part.9.part = f32[5,4,2048]{2,1,0:T(4,128)S(1)} custom-call(s32[6,16]{1,0:T(8,128)S(4)} %get-tuple-element.68.table, f32[5,4,2048]{2,1,0:T(4,128)S(1)} %get-tuple-element.97.field, f32[5,4,2048]{2,1,0:T(4,128)S(1)} %get-tuple-element.98.goal, f32[5,5,6,2048]{3,2,1,0:T(8,128)S(1)} %get-tuple-element.72.jacobian, ...), custom_call_target="tpu_custom_call" | custom-call | flops 1 | bytes 1 | tf_op jit(solution)/shard_map/own_part/pallas_call | solution.py:34
  35.1 2.7 %collective-permute-start.12 = (f32[8,5,4,128]{3,2,1,0:T(4,128)S(1)}, f32[8,5,4,128]{3,2,1,0:T(4,128)S(1)}, u32[]{:S(2)}, u32[]{:S(2)}) collective-permute-start(f32[8,5,4,128]{3,2,1,0:T(4,128)S(1)} %get-tuple-element.105.faces), channel_id=1, source_target_pairs={{0,1},{2,3},{4,5},{6,7},{1,0},{3,2},{5,4},{7,6},{8,9},{10,11},{12,... | collective-permute-start | bytes 245768 | tf_op jit(solution)/shard_map/ppermute | solution.py:558
  37.8 0.7 %collective-permute-start.14 = (f32[5,2,3072]{2,1,0:T(2,128)S(1)}, f32[5,2,3072]{2,1,0:T(2,128)S(1)}, u32[]{:S(2)}, u32[]{:S(2)}) collective-permute-start(f32[5,2,3072]{2,1,0:T(2,128)S(1)} %get-tuple-element.109), channel_id=1, source_target_pairs={{0,8},{8,16},{16,24},{24,0},{1,9},{9,17},{17,25},{25,1},{2,10},{10... | collective-permute-start | bytes 368648 | tf_op jit(solution)/shard_map/ppermute | solution.py:563
  38.5 0.8 %own_part.10.part = f32[5,4,2048]{2,1,0:T(4,128)S(1)} custom-call(s32[6,16]{1,0:T(8,128)S(4)} %get-tuple-element.68.table, f32[5,4,2048]{2,1,0:T(4,128)S(1)} %get-tuple-element.104.field, f32[5,4,2048]{2,1,0:T(4,128)S(1)} %get-tuple-element.98.goal, f32[5,5,6,2048]{3,2,1,0:T(8,128)S(1)} %get-tuple-element.72.jacobian, ...), custom_call_target="tpu_custom_call" | custom-call | flops 1 | bytes 1 | tf_op jit(solution)/shard_map/own_part/pallas_call | solution.py:34
  40.7 1.3 %collective-permute-start.17 = (f32[5,2,3072]{2,1,0:T(2,128)S(1)}, f32[5,2,3072]{2,1,0:T(2,128)S(1)}, u32[]{:S(2)}, u32[]{:S(2)}) collective-permute-start(f32[5,2,3072]{2,1,0:T(2,128)S(1)} %get-tuple-element.115), channel_id=1, source_target_pairs={{0,8},{8,16},{16,24},{24,0},{1,9},{9,17},{17,25},{25,1},{2,10},{10... | collective-permute-start | bytes 368648 | tf_op jit(solution)/shard_map/ppermute | solution.py:563
  41.9 2.0 %collective-permute-done.14.tail = f32[5,2,3072]{2,1,0:T(2,128)S(1)} collective-permute-done((f32[5,2,3072]{2,1,0:T(2,128)S(1)}, f32[5,2,3072]{2,1,0:T(2,128)S(1)}, u32[]{:S(2)}, u32[]{:S(2)}) %collective-permute-start.14) | collective-permute-done | bytes 122912 | tf_op jit(solution)/shard_map/ppermute | solution.py:563
  44.6 0.8 %own_part.11.part = f32[5,4,2048]{2,1,0:T(4,128)S(1)} custom-call(s32[6,16]{1,0:T(8,128)S(4)} %get-tuple-element.68.table, f32[5,4,2048]{2,1,0:T(4,128)S(1)} %get-tuple-element.110.field, f32[5,4,2048]{2,1,0:T(4,128)S(1)} %get-tuple-element.98.goal, f32[5,5,6,2048]{3,2,1,0:T(8,128)S(1)} %get-tuple-element.72.jacobian, ...), custom_call_target="tpu_custom_call" | custom-call | flops 1 | bytes 1 | tf_op jit(solution)/shard_map/own_part/pallas_call | solution.py:34
  47.5 2.5 %collective-permute-start.18 = (f32[8,5,16,128]{3,2,1,0:T(8,128)S(1)}, f32[8,5,16,128]{3,2,1,0:T(8,128)S(1)}, u32[]{:S(2)}, u32[]{:S(2)}) collective-permute-start(f32[8,5,16,128]{3,2,1,0:T(8,128)S(1)} %get-tuple-element.117.faces), channel_id=1, source_target_pairs={{0,1},{2,3},{4,5},{6,7},{1,0},{3,2},{5,4},{7,6},{8,9},{10,11},{12,... | collective-permute-start | bytes 983048 | tf_op jit(solution)/shard_map/ppermute | solution.py:558
  49.9 0.9 %collective-permute-start.20 = (f32[5,2,3072]{2,1,0:T(2,128)S(1)}, f32[5,2,3072]{2,1,0:T(2,128)S(1)}, u32[]{:S(2)}, u32[]{:S(2)}) collective-permute-start(f32[5,2,3072]{2,1,0:T(2,128)S(1)} %get-tuple-element.121), channel_id=1, source_target_pairs={{0,8},{8,16},{16,24},{24,0},{1,9},{9,17},{17,25},{25,1},{2,10},{10... | collective-permute-start | bytes 368648 | tf_op jit(solution)/shard_map/ppermute | solution.py:563
  50.8 1.5 %own_part.12.part = f32[5,16,2048]{2,1,0:T(8,128)S(1)} custom-call(s32[6,16]{1,0:T(8,128)S(4)} %get-tuple-element.68.table, f32[5,16,2048]{2,1,0:T(8,128)S(1)} %get-tuple-element.116.field, f32[5,16,2048]{2,1,0:T(8,128)S(1)} %get-tuple-element.71.goal, f32[5,5,6,2048]{3,2,1,0:T(8,128)S(1)} %get-tuple-element.72.jacobian, ...), custom_call_target="tpu_custom_call" | custom-call | flops 1 | bytes 1 | tf_op jit(solution)/shard_map/own_part/pallas_call | solution.py:34
  54.0 2.1 %collective-permute-done.20.tail = f32[5,2,3072]{2,1,0:T(2,128)S(1)} collective-permute-done((f32[5,2,3072]{2,1,0:T(2,128)S(1)}, f32[5,2,3072]{2,1,0:T(2,128)S(1)}, u32[]{:S(2)}, u32[]{:S(2)}) %collective-permute-start.20) | collective-permute-done | bytes 122912 | tf_op jit(solution)/shard_map/ppermute | solution.py:563
  57.0 1.5 %collective-permute-start.23 = (f32[5,2,3072]{2,1,0:T(2,128)S(1)}, f32[5,2,3072]{2,1,0:T(2,128)S(1)}, u32[]{:S(2)}, u32[]{:S(2)}) collective-permute-start(f32[5,2,3072]{2,1,0:T(2,128)S(1)} %get-tuple-element.127), channel_id=1, source_target_pairs={{0,8},{8,16},{16,24},{24,0},{1,9},{9,17},{17,25},{25,1},{2,10},{10... | collective-permute-start | bytes 368648 | tf_op jit(solution)/shard_map/ppermute | solution.py:563
  58.4 1.5 %own_part.13.part = f32[5,16,2048]{2,1,0:T(8,128)S(1)} custom-call(s32[6,16]{1,0:T(8,128)S(4)} %get-tuple-element.68.table, f32[5,16,2048]{2,1,0:T(8,128)S(1)} %get-tuple-element.122.field, f32[5,16,2048]{2,1,0:T(8,128)S(1)} %get-tuple-element.71.goal, f32[5,5,6,2048]{3,2,1,0:T(8,128)S(1)} %get-tuple-element.72.jacobian, ...), custom_call_target="tpu_custom_call" | custom-call | flops 1 | bytes 1 | tf_op jit(solution)/shard_map/own_part/pallas_call | solution.py:34
  61.6 1.7 %collective-permute-done.23.tail = f32[5,2,3072]{2,1,0:T(2,128)S(1)} collective-permute-done((f32[5,2,3072]{2,1,0:T(2,128)S(1)}, f32[5,2,3072]{2,1,0:T(2,128)S(1)}, u32[]{:S(2)}, u32[]{:S(2)}) %collective-permute-start.23) | collective-permute-done | bytes 122912 | tf_op jit(solution)/shard_map/ppermute | solution.py:563
  63.6 0.9 %collective-permute-start.24 = (f32[8,5,16,128]{3,2,1,0:T(8,128)S(1)}, f32[8,5,16,128]{3,2,1,0:T(8,128)S(1)}, u32[]{:S(2)}, u32[]{:S(2)}) collective-permute-start(f32[8,5,16,128]{3,2,1,0:T(8,128)S(1)} %get-tuple-element.131), channel_id=1, source_target_pairs={{0,1},{2,3},{4,5},{6,7},{1,0},{3,2},{5,4},{7,6},{8,9},{10,11},{12,... | collective-permute-start | bytes 983048 | tf_op jit(solution)/shard_map/ppermute | solution.py:558
  64.5 0.8 %collective-permute-start.26 = (f32[5,2,3072]{2,1,0:T(2,128)S(1)}, f32[5,2,3072]{2,1,0:T(2,128)S(1)}, u32[]{:S(2)}, u32[]{:S(2)}) collective-permute-start(f32[5,2,3072]{2,1,0:T(2,128)S(1)} %get-tuple-element.133), channel_id=1, source_target_pairs={{0,8},{8,16},{16,24},{24,0},{1,9},{9,17},{17,25},{25,1},{2,10},{10... | collective-permute-start | bytes 368648 | tf_op jit(solution)/shard_map/ppermute | solution.py:563
  65.3 1.5 %last_own_part.1 = (f32[5,16,2048]{2,1,0:T(8,128)S(1)}, f32[5,16,2048]{2,1,0:T(8,128)}) custom-call(s32[6,16]{1,0:T(8,128)S(4)} %get-tuple-element.68.table, f32[5,16,2048]{2,1,0:T(8,128)S(1)} %get-tuple-element.128.field, f32[5,16,2048]{2,1,0:T(8,128)S(1)} %get-tuple-element.71.goal, f32[5,5,6,2048]{3,2,1,0:T(8,128)S(1)} %get-tuple-element.72.jacobian, ...), custom_call_target="tpu_custom_call" | custom-call | flops 1 | bytes 1 | tf_op jit(solution)/shard_map/last_own_part/pallas_call | solution.py:34
  67.1 3.6 %collective-permute-done.26.tail = f32[5,2,3072]{2,1,0:T(2,128)S(1)} collective-permute-done((f32[5,2,3072]{2,1,0:T(2,128)S(1)}, f32[5,2,3072]{2,1,0:T(2,128)S(1)}, u32[]{:S(2)}, u32[]{:S(2)}) %collective-permute-start.26) | collective-permute-done | bytes 122912 | tf_op jit(solution)/shard_map/ppermute | solution.py:563
  70.9 1.1 %residual.1 = f32[5,16,2048]{2,1,0:T(8,128)} custom-call(s32[6,16]{1,0:T(8,128)S(4)} %get-tuple-element.68.table, f32[5,16,2048]{2,1,0:T(8,128)S(1)} %beside_part.1.part, f32[8,5,16,128]{3,2,1,0:T(8,128)S(1)} %rim.5, f32[5,2,3072]{2,1,0:T(2,128)S(1)} %collective-permute-done.26.tail, f32[2,5,5,2048]{3,2,1,0:T(8,128)S(1)} %get-tuple-element.76.rim_jacobian), custom_call_target="tpu_custom_call" | custom-call | flops 1 | bytes 1 | tf_op jit(solution)/shard_map/residual/pallas_call | solution.py:34
  (69 shorter events, 17.8 us)
Async XLA Ops:
  1.8 7.2 %collective-permute-start = (f32[8,5,16,128]{3,2,1,0:T(8,128)S(1)}, f32[8,5,16,128]{3,2,1,0:T(8,128)S(1)}, u32[]{:S(2)}, u32[]{:S(2)}) collective-permute-start(f32[8,5,16,128]{3,2,1,0:T(8,128)S(1)} %get-tuple-element.75.faces), channel_id=1, source_target_pairs={{0,1},{2,3},{4,5},{6,7},{1,0},{3,2},{5,4},{7,6},{8,9},{10,11},{12,... | collective-permute-start | bytes 983048 | tf_op jit(solution)/shard_map/ppermute | solution.py:558
  2.3 7.8 %collective-permute-start.2 = (f32[8,5,16,128]{3,2,1,0:T(8,128)S(1)}, f32[8,5,16,128]{3,2,1,0:T(8,128)S(1)}, u32[]{:S(2)}, u32[]{:S(2)}) collective-permute-start(f32[8,5,16,128]{3,2,1,0:T(8,128)S(1)} %get-tuple-element.75.faces), channel_id=1, source_target_pairs={{1,2},{3,4},{5,6},{2,1},{4,3},{6,5},{9,10},{11,12},{13,14},{10,9},... | collective-permute-start | bytes 983048 | tf_op jit(solution)/shard_map/ppermute | solution.py:554
  3.0 5.9 %collective-permute-start.1 = (f32[5,2,2048]{2,1,0:T(2,128)S(1)}, f32[5,2,2048]{2,1,0:T(2,128)S(1)}, u32[]{:S(2)}, u32[]{:S(2)}) collective-permute-start(f32[5,2,2048]{2,1,0:T(2,128)S(1)} %tail.1), channel_id=1, source_target_pairs={{0,8},{8,16},{16,24},{24,0},{1,9},{9,17},{17,25},{25,1},{2,10},{10... | collective-permute-start | bytes 245768 | tf_op jit(solution)/shard_map/ppermute | solution.py:563
  9.4 10.4 %collective-permute-start.4 = (f32[8,120,128]{2,1,0:T(8,128)S(1)}, f32[8,120,128]{2,1,0:T(8,128)S(1)}, u32[]{:S(2)}, u32[]{:S(2)}) collective-permute-start(f32[8,120,128]{2,1,0:T(8,128)S(1)} %get-tuple-element.84), channel_id=1, source_target_pairs={{1,2},{3,4},{5,6},{2,1},{4,3},{6,5},{9,10},{11,12},{13,14},{10,9},... | collective-permute-start | bytes 1474568 | tf_op jit(solution)/shard_map/ppermute | solution.py:554
  10.7 8.0 %collective-permute-start.3 = (f32[8,5,16,128]{3,2,1,0:T(8,128)S(1)}, f32[8,5,16,128]{3,2,1,0:T(8,128)S(1)}, u32[]{:S(2)}, u32[]{:S(2)}) collective-permute-start(f32[8,5,16,128]{3,2,1,0:T(8,128)S(1)} %get-tuple-element.82.faces), channel_id=1, source_target_pairs={{0,1},{2,3},{4,5},{6,7},{1,0},{3,2},{5,4},{7,6},{8,9},{10,11},{12,... | collective-permute-start | bytes 983048 | tf_op jit(solution)/shard_map/ppermute | solution.py:558
  15.7 6.2 %collective-permute-start.5 = (f32[5,2,3072]{2,1,0:T(2,128)S(1)}, f32[5,2,3072]{2,1,0:T(2,128)S(1)}, u32[]{:S(2)}, u32[]{:S(2)}) collective-permute-start(f32[5,2,3072]{2,1,0:T(2,128)S(1)} %get-tuple-element.87), channel_id=1, source_target_pairs={{0,8},{8,16},{16,24},{24,0},{1,9},{9,17},{17,25},{25,1},{2,10},{10... | collective-permute-start | bytes 368648 | tf_op jit(solution)/shard_map/ppermute | solution.py:563
  19.2 9.3 %collective-permute-start.7 = (f32[8,5,6,128]{3,2,1,0:T(8,128)S(1)}, f32[8,5,6,128]{3,2,1,0:T(8,128)S(1)}, u32[]{:S(2)}, u32[]{:S(2)}) collective-permute-start(f32[8,5,6,128]{3,2,1,0:T(8,128)S(1)} %get-tuple-element.85.next_message), channel_id=1, source_target_pairs={{1,2},{3,4},{5,6},{2,1},{4,3},{6,5},{9,10},{11,12},{13,14},{10,9},... | collective-permute-start | bytes 368648 | tf_op jit(solution)/shard_map/ppermute | solution.py:554
  22.4 5.1 %collective-permute-start.6 = (f32[8,5,4,128]{3,2,1,0:T(4,128)S(1)}, f32[8,5,4,128]{3,2,1,0:T(4,128)S(1)}, u32[]{:S(2)}, u32[]{:S(2)}) collective-permute-start(f32[8,5,4,128]{3,2,1,0:T(4,128)S(1)} %get-tuple-element.90.faces), channel_id=1, source_target_pairs={{0,1},{2,3},{4,5},{6,7},{1,0},{3,2},{5,4},{7,6},{8,9},{10,11},{12,... | collective-permute-start | bytes 245768 | tf_op jit(solution)/shard_map/ppermute | solution.py:558
  24.1 6.2 %collective-permute-start.8 = (f32[5,2,3072]{2,1,0:T(2,128)S(1)}, f32[5,2,3072]{2,1,0:T(2,128)S(1)}, u32[]{:S(2)}, u32[]{:S(2)}) collective-permute-start(f32[5,2,3072]{2,1,0:T(2,128)S(1)} %get-tuple-element.96), channel_id=1, source_target_pairs={{0,8},{8,16},{16,24},{24,0},{1,9},{9,17},{17,25},{25,1},{2,10},{10... | collective-permute-start | bytes 368648 | tf_op jit(solution)/shard_map/ppermute | solution.py:563
  27.8 6.7 %collective-permute-start.10 = (f32[16,5,4,128]{3,2,1,0:T(4,128)S(1)}, f32[16,5,4,128]{3,2,1,0:T(4,128)S(1)}, u32[]{:S(2)}, u32[]{:S(2)}) collective-permute-start(f32[16,5,4,128]{3,2,1,0:T(4,128)S(1)} %get-tuple-element.101), channel_id=1, source_target_pairs={{1,2},{3,4},{5,6},{2,1},{4,3},{6,5},{9,10},{11,12},{13,14},{10,9},... | collective-permute-start | bytes 491528 | tf_op jit(solution)/shard_map/ppermute | solution.py:554
  28.9 5.9 %collective-permute-start.11 = (f32[5,2,3072]{2,1,0:T(2,128)S(1)}, f32[5,2,3072]{2,1,0:T(2,128)S(1)}, u32[]{:S(2)}, u32[]{:S(2)}) collective-permute-start(f32[5,2,3072]{2,1,0:T(2,128)S(1)} %get-tuple-element.103), channel_id=1, source_target_pairs={{0,8},{8,16},{16,24},{24,0},{1,9},{9,17},{17,25},{25,1},{2,10},{10... | collective-permute-start | bytes 368648 | tf_op jit(solution)/shard_map/ppermute | solution.py:563
  30.5 3.0 %collective-permute-start.9 = (f32[8,5,4,128]{3,2,1,0:T(4,128)S(1)}, f32[8,5,4,128]{3,2,1,0:T(4,128)S(1)}, u32[]{:S(2)}, u32[]{:S(2)}) collective-permute-start(f32[8,5,4,128]{3,2,1,0:T(4,128)S(1)} %get-tuple-element.99.faces), channel_id=1, source_target_pairs={{0,1},{2,3},{4,5},{6,7},{1,0},{3,2},{5,4},{7,6},{8,9},{10,11},{12,... | collective-permute-start | bytes 245768 | tf_op jit(solution)/shard_map/ppermute | solution.py:558
  33.8 6.5 %collective-permute-start.13 = (f32[16,5,4,128]{3,2,1,0:T(4,128)S(1)}, f32[16,5,4,128]{3,2,1,0:T(4,128)S(1)}, u32[]{:S(2)}, u32[]{:S(2)}) collective-permute-start(f32[16,5,4,128]{3,2,1,0:T(4,128)S(1)} %get-tuple-element.107), channel_id=1, source_target_pairs={{1,2},{3,4},{5,6},{2,1},{4,3},{6,5},{9,10},{11,12},{13,14},{10,9},... | collective-permute-start | bytes 491528 | tf_op jit(solution)/shard_map/ppermute | solution.py:554
  35.1 4.3 %collective-permute-start.12 = (f32[8,5,4,128]{3,2,1,0:T(4,128)S(1)}, f32[8,5,4,128]{3,2,1,0:T(4,128)S(1)}, u32[]{:S(2)}, u32[]{:S(2)}) collective-permute-start(f32[8,5,4,128]{3,2,1,0:T(4,128)S(1)} %get-tuple-element.105.faces), channel_id=1, source_target_pairs={{0,1},{2,3},{4,5},{6,7},{1,0},{3,2},{5,4},{7,6},{8,9},{10,11},{12,... | collective-permute-start | bytes 245768 | tf_op jit(solution)/shard_map/ppermute | solution.py:558
  37.8 6.2 %collective-permute-start.14 = (f32[5,2,3072]{2,1,0:T(2,128)S(1)}, f32[5,2,3072]{2,1,0:T(2,128)S(1)}, u32[]{:S(2)}, u32[]{:S(2)}) collective-permute-start(f32[5,2,3072]{2,1,0:T(2,128)S(1)} %get-tuple-element.109), channel_id=1, source_target_pairs={{0,8},{8,16},{16,24},{24,0},{1,9},{9,17},{17,25},{25,1},{2,10},{10... | collective-permute-start | bytes 368648 | tf_op jit(solution)/shard_map/ppermute | solution.py:563
  39.6 7.0 %collective-permute-start.16 = (f32[16,5,4,128]{3,2,1,0:T(4,128)S(1)}, f32[16,5,4,128]{3,2,1,0:T(4,128)S(1)}, u32[]{:S(2)}, u32[]{:S(2)}) collective-permute-start(f32[16,5,4,128]{3,2,1,0:T(4,128)S(1)} %get-tuple-element.113), channel_id=1, source_target_pairs={{1,2},{3,4},{5,6},{2,1},{4,3},{6,5},{9,10},{11,12},{13,14},{10,9},... | collective-permute-start | bytes 491528 | tf_op jit(solution)/shard_map/ppermute | solution.py:554
  40.7 6.5 %collective-permute-start.17 = (f32[5,2,3072]{2,1,0:T(2,128)S(1)}, f32[5,2,3072]{2,1,0:T(2,128)S(1)}, u32[]{:S(2)}, u32[]{:S(2)}) collective-permute-start(f32[5,2,3072]{2,1,0:T(2,128)S(1)} %get-tuple-element.115), channel_id=1, source_target_pairs={{0,8},{8,16},{16,24},{24,0},{1,9},{9,17},{17,25},{25,1},{2,10},{10... | collective-permute-start | bytes 368648 | tf_op jit(solution)/shard_map/ppermute | solution.py:563
  44.2 1.4 %collective-permute-start.15 = (f32[8,5,4,128]{3,2,1,0:T(4,128)S(1)}, f32[8,5,4,128]{3,2,1,0:T(4,128)S(1)}, u32[]{:S(2)}, u32[]{:S(2)}) collective-permute-start(f32[8,5,4,128]{3,2,1,0:T(4,128)S(1)} %get-tuple-element.111.faces), channel_id=1, source_target_pairs={{0,1},{2,3},{4,5},{6,7},{1,0},{3,2},{5,4},{7,6},{8,9},{10,11},{12,... | collective-permute-start | bytes 245768 | tf_op jit(solution)/shard_map/ppermute | solution.py:558
  45.9 7.5 %collective-permute-start.19 = (f32[9,5,16,128]{3,2,1,0:T(8,128)S(1)}, f32[9,5,16,128]{3,2,1,0:T(8,128)S(1)}, u32[]{:S(2)}, u32[]{:S(2)}) collective-permute-start(f32[9,5,16,128]{3,2,1,0:T(8,128)S(1)} %get-tuple-element.119), channel_id=1, source_target_pairs={{1,2},{3,4},{5,6},{2,1},{4,3},{6,5},{9,10},{11,12},{13,14},{10,9},... | collective-permute-start | bytes 1105928 | tf_op jit(solution)/shard_map/ppermute | solution.py:554
  47.5 4.8 %collective-permute-start.18 = (f32[8,5,16,128]{3,2,1,0:T(8,128)S(1)}, f32[8,5,16,128]{3,2,1,0:T(8,128)S(1)}, u32[]{:S(2)}, u32[]{:S(2)}) collective-permute-start(f32[8,5,16,128]{3,2,1,0:T(8,128)S(1)} %get-tuple-element.117.faces), channel_id=1, source_target_pairs={{0,1},{2,3},{4,5},{6,7},{1,0},{3,2},{5,4},{7,6},{8,9},{10,11},{12,... | collective-permute-start | bytes 983048 | tf_op jit(solution)/shard_map/ppermute | solution.py:558
  49.9 6.2 %collective-permute-start.20 = (f32[5,2,3072]{2,1,0:T(2,128)S(1)}, f32[5,2,3072]{2,1,0:T(2,128)S(1)}, u32[]{:S(2)}, u32[]{:S(2)}) collective-permute-start(f32[5,2,3072]{2,1,0:T(2,128)S(1)} %get-tuple-element.121), channel_id=1, source_target_pairs={{0,8},{8,16},{16,24},{24,0},{1,9},{9,17},{17,25},{25,1},{2,10},{10... | collective-permute-start | bytes 368648 | tf_op jit(solution)/shard_map/ppermute | solution.py:563
  52.7 8.3 %collective-permute-start.22 = (f32[9,5,16,128]{3,2,1,0:T(8,128)S(1)}, f32[9,5,16,128]{3,2,1,0:T(8,128)S(1)}, u32[]{:S(2)}, u32[]{:S(2)}) collective-permute-start(f32[9,5,16,128]{3,2,1,0:T(8,128)S(1)} %get-tuple-element.125), channel_id=1, source_target_pairs={{1,2},{3,4},{5,6},{2,1},{4,3},{6,5},{9,10},{11,12},{13,14},{10,9},... | collective-permute-start | bytes 1105928 | tf_op jit(solution)/shard_map/ppermute | solution.py:554
  56.4 3.5 %collective-permute-start.21 = (f32[8,5,16,128]{3,2,1,0:T(8,128)S(1)}, f32[8,5,16,128]{3,2,1,0:T(8,128)S(1)}, u32[]{:S(2)}, u32[]{:S(2)}) collective-permute-start(f32[8,5,16,128]{3,2,1,0:T(8,128)S(1)} %get-tuple-element.123.faces), channel_id=1, source_target_pairs={{0,1},{2,3},{4,5},{6,7},{1,0},{3,2},{5,4},{7,6},{8,9},{10,11},{12,... | collective-permute-start | bytes 983048 | tf_op jit(solution)/shard_map/ppermute | solution.py:558
  57.0 6.4 %collective-permute-start.23 = (f32[5,2,3072]{2,1,0:T(2,128)S(1)}, f32[5,2,3072]{2,1,0:T(2,128)S(1)}, u32[]{:S(2)}, u32[]{:S(2)}) collective-permute-start(f32[5,2,3072]{2,1,0:T(2,128)S(1)} %get-tuple-element.127), channel_id=1, source_target_pairs={{0,8},{8,16},{16,24},{24,0},{1,9},{9,17},{17,25},{25,1},{2,10},{10... | collective-permute-start | bytes 368648 | tf_op jit(solution)/shard_map/ppermute | solution.py:563
  60.3 10.4 %collective-permute-start.25 = (f32[9,5,16,128]{3,2,1,0:T(8,128)S(1)}, f32[9,5,16,128]{3,2,1,0:T(8,128)S(1)}, u32[]{:S(2)}, u32[]{:S(2)}) collective-permute-start(f32[9,5,16,128]{3,2,1,0:T(8,128)S(1)} %get-tuple-element.132), channel_id=1, source_target_pairs={{1,2},{3,4},{5,6},{2,1},{4,3},{6,5},{9,10},{11,12},{13,14},{10,9},... | collective-permute-start | bytes 1105928 | tf_op jit(solution)/shard_map/ppermute | solution.py:554
  63.6 3.2 %collective-permute-start.24 = (f32[8,5,16,128]{3,2,1,0:T(8,128)S(1)}, f32[8,5,16,128]{3,2,1,0:T(8,128)S(1)}, u32[]{:S(2)}, u32[]{:S(2)}) collective-permute-start(f32[8,5,16,128]{3,2,1,0:T(8,128)S(1)} %get-tuple-element.131), channel_id=1, source_target_pairs={{0,1},{2,3},{4,5},{6,7},{1,0},{3,2},{5,4},{7,6},{8,9},{10,11},{12,... | collective-permute-start | bytes 983048 | tf_op jit(solution)/shard_map/ppermute | solution.py:558
  64.5 6.2 %collective-permute-start.26 = (f32[5,2,3072]{2,1,0:T(2,128)S(1)}, f32[5,2,3072]{2,1,0:T(2,128)S(1)}, u32[]{:S(2)}, u32[]{:S(2)}) collective-permute-start(f32[5,2,3072]{2,1,0:T(2,128)S(1)} %get-tuple-element.133), channel_id=1, source_target_pairs={{0,8},{8,16},{16,24},{24,0},{1,9},{9,17},{17,25},{25,1},{2,10},{10... | collective-permute-start | bytes 368648 | tf_op jit(solution)/shard_map/ppermute | solution.py:563

commit v3 on v2

--- a/solution.py
+++ b/solution.py
@@ -73,18 +73,15 @@
     lax.fori_loop(0, count // unroll, steps, 0)
 
 
-def first_kernel(neighbours, face_list, iterate, table, listed, field, faces_out, near, named, sems):
-    copies = [
-        pltpu.make_async_copy(iterate, field, sems.at[0]),
-        pltpu.make_async_copy(neighbours, near, sems.at[1]),
-        pltpu.make_async_copy(face_list, named, sems.at[2]),
-    ]
+def first_kernel(*refs):
+    sources, (table, listed, *held, faces_out, near, named, sems) = refs[:7], refs[7:]
+    copies = [pltpu.make_async_copy(x, y, sems.at[i]) for i, (x, y) in enumerate(zip(sources, [near, named, *held]))]
     for copy in copies:
         copy.start()
     slot = cross_slot()
     slots, blocks = near.shape
     faces = named.shape[0]
-    copies[1].wait()
+    copies[0].wait()
 
     def step(b, carry):
         table[0, b] = near[slot, b] - (blocks + faces * slot)
@@ -94,25 +91,19 @@
         return carry
 
     lax.fori_loop(0, blocks, step, 0)
-    copies[2].wait()
+    copies[1].wait()
     for h in range(faces):
         listed[h] = named[h]
-    copies[0].wait()
-    pick_faces(listed, field, faces_out)
-
-
-def arguments_kernel(listed, *refs):
-    arguments, held = refs[:4], refs[4:8]
-    fine_out, coarse_out, out, sems = refs[8:]
-    copies = [pltpu.make_async_copy(x, y, sems.at[i]) for i, (x, y) in enumerate(zip(arguments, held))]
-    for copy in copies:
-        copy.start()
-    for copy in copies:
+    copies[2].wait()
+    pick_faces(listed, held[0], faces_out)
+    for copy in copies[3:]:
         copy.wait()
-    cell_diag, jacobian = held[0], held[1]
+
+
+def derived_kernel(listed, cell_diag, jacobian, fine_out, coarse_out, out):
+    lower_crosses = cross_slot() == 0
     fine_out[...] = damping / (3.0 * time_weight + cell_diag[...])
     coarse_out[...] = damping / (3.0 * coarse_weight + cell_diag[...])
-    lower_crosses = cross_slot() == 0
     for a in range(NV):
         for j in range(NV):
             lower, upper = jacobian[a, j, pl.ds(0, 1), :], jacobian[a, j, pl.ds(1, 1), :]
@@ -256,7 +247,7 @@
 
 
 def first_message_kernel(
-    table, listed, field, part, rim, rim_jacobian, points, coarse_points, tail, out, message
+    table, listed, field, part, rim, rim_jacobian, points, coarse_points, out, message
 ):
     beside_part(table, part, rim, rim_jacobian, out)
     steps = field.shape[1]
@@ -395,6 +386,10 @@
 def rest_part(b, part, rim, table, rim_jacobian):
     lanes = lanes_of(b)
     return rim_part(0, [part[a, :, lanes] for a in range(NV)], b, rim, table, rim_jacobian)
+
+
+def first_sweep_kernel(weights, table, field, part, tail, rim, rim_jacobian, points, out, *tail_out):
+    sweep_kernel(weights, table, field, part, rim, rim_jacobian, points, out, *tail_out)
 
 
 def sweep_kernel(weights, table, field, part, rim, rim_jacobian, points, out, *tail_out):
@@ -578,36 +573,27 @@
 
     goal = jnp.transpose(right_side, (1, 0, 2))
     jacobian = jnp.transpose(jacobian, (1, 2, 0, 3))
-    table, listed, start, sent = pl.pallas_call(
+    operands = [jnp.transpose(neighbours), face_list, jnp.transpose(iterate, (1, 0, 2))]
+    operands = [in_hbm(x) for x in operands + [cell_diag, jacobian, self_block, goal]]
+    table, listed, state, cell_diag, jacobian, self_block, goal, sent = pl.pallas_call(
         first_kernel,
-        out_shape=[
-            pltpu.SMEM((K, blocks), jnp.int32), pltpu.SMEM((faces,), jnp.int32),
-            pltpu.VMEM((NV, steps, cells), jnp.float32), pltpu.VMEM(face(steps).shape, jnp.float32),
-        ],
-        in_specs=[IN_HBM] * 3,
-        out_specs=[IN_SMEM] * 2 + [IN_VMEM] * 2,
-        scratch_shapes=[
-            pltpu.SMEM((K, blocks), jnp.int32), pltpu.SMEM((faces,), jnp.int32), pltpu.SemaphoreType.DMA((3,)),
-        ],
+        out_shape=[pltpu.SMEM(x.shape, jnp.int32) for x in operands[:2]]
+        + [pltpu.VMEM(x.shape, jnp.float32) for x in [*operands[2:], face(steps)]],
+        in_specs=[IN_HBM] * len(operands),
+        out_specs=[IN_SMEM] * 2 + [IN_VMEM] * (len(operands) - 1),
+        scratch_shapes=[pltpu.SMEM(x.shape, jnp.int32) for x in operands[:2]]
+        + [pltpu.SemaphoreType.DMA((len(operands),))],
         compiler_params=pltpu.CompilerParams(vmem_limit_bytes=SCRATCH_BYTES),
         cost_estimate=NOTHING,
-        name="iterate_and_tables",
-    )(*[in_hbm(x) for x in (jnp.transpose(neighbours), face_list, jnp.transpose(iterate, (1, 0, 2)))])
+        name="arguments",
+    )(*operands)
     tables = [table, listed]
     rim = over_chips(sent)
     beside = on_chip(sent)
-    arguments = [in_hbm(x) for x in (cell_diag, jacobian, self_block, goal)]
-    outs = [shape(*x.shape) for x in arguments] + [shape(NV, cells)] * 2 + [shape(2, NV, NV, cells)]
-    cell_diag, jacobian, self_block, goal, fine_points, coarse_points, rim_jacobian = pl.pallas_call(
-        arguments_kernel,
-        out_shape=[pltpu.VMEM(x.shape, jnp.float32) for x in outs],
-        in_specs=[IN_SMEM] + [IN_HBM] * len(arguments),
-        out_specs=[IN_VMEM] * len(outs),
-        scratch_shapes=[pltpu.SemaphoreType.DMA((len(arguments),))],
-        compiler_params=pltpu.CompilerParams(vmem_limit_bytes=SCRATCH_BYTES),
-        cost_estimate=NOTHING,
-        name="arguments",
-    )(listed, *arguments)
+    fine_points, coarse_points, rim_jacobian = call(
+        derived_kernel, "derived", [listed], [cell_diag, jacobian],
+        [shape(NV, cells)] * 2 + [shape(2, NV, NV, cells)],
+    )
 
     def own(weight, n, field, target):
         return call(
@@ -618,15 +604,14 @@
     ahead = coarse >= 4
     tail_shape = shape(NV, 2, cells + faces * BLK)
 
-    state = start
     first_tail = call(
-        bind(tail_kernel, (time_weight, False, None, None)), "tail", [], [state], [shape(NV, 2, cells)]
+        bind(tail_kernel, (time_weight, False, None, None)), "tail", [], [state], [shape(NV, 2, 2 * cells)]
     )[0]
     tail = to_later(first_tail)
     part = own(time_weight, steps, state, goal)
     part, message = call(
         first_message_kernel, "first_message", tables,
-        [state, part, beside, rim_jacobian, fine_points, coarse_points, tail],
+        [state, part, beside, rim_jacobian, fine_points, coarse_points],
         [whole(steps), shape(faces, NV * steps + NV * (NV + 3), BLK)], per_slot * steps,
     )
     first_message = over_chips(message)
@@ -672,7 +657,7 @@
 
     fine_weights = (time_weight, False, time_weight, False)
     (state, sent), tail, rim = sweep(
-        sweep_kernel, "first_sweep", [state, part], [rim_jacobian, fine_points], [whole(steps)], rim, fine_weights,
+        first_sweep_kernel, "first_sweep", [state, part, tail], [rim_jacobian, fine_points], [whole(steps)], rim, fine_weights,
         tail, None, False, finish_with(fine_points, steps),
     )
     beside = on_chip(sent)

time: 72.5 us -> 71.4 us (0.985)
  starting transfers between devices: 34.7 us -> 32.3 us
  waiting for transfers between devices: 11.8 us -> 14.1 us
  Pallas kernels: 24.3 us -> 23.3 us
    ppermute x9, waiting for transfers between devices: 11.6 us -> 13.6 us  [to_later(): lax.ppermute(tail, 'tm', [(i, (i + 1) % periods) for i in range(periods)])]
    ppermute x9, starting transfers between devices: 16.4 us -> 14.5 us  [on_chip(): return lax.ppermute(faces, 'space', neighbour_pairs(0))]
    pallas_call x2 -> x1, Pallas kernels: 3.06 us -> 1.96 us  [body(): pl.pallas_call(first_kernel, out_shape=[pltpu.SMEM(x.shape, jnp.int32) fo...]
    pallas_call x44 -> x45, Pallas kernels: 21.1 us -> 21.2 us  [call(): pl.pallas_call(kernel, out_shape=[o if out_specs and out_specs[i] is IN_H...]
  transfers between devices with their start and end apart: 27 -> 27, of which waited for: 8 -> 9; matrix products, arithmetic and copies ran while one was open for 0% -> 0% of each run, Pallas kernels for 30% -> 28%
where the time goes in v3:
time: 71.4 us; the launch traced here: 71 us
  starting transfers between devices  32.3 us (45%)
  Pallas kernels  23.3 us (33%)
  waiting for transfers between devices  14.1 us (20%)
  between operations  1.27 us (2%)
    pallas_call x45, Pallas kernels, call(): pl.pallas_call(kernel, out_shape=[o if out_specs and out_specs[i] is IN_H...  21.2 us
    ppermute x9, starting transfers between devices, on_chip(): return lax.ppermute(faces, 'space', neighbour_pairs(0))  14.5 us
    ppermute x9, waiting for transfers between devices, to_later(): lax.ppermute(tail, 'tm', [(i, (i + 1) % periods) for i in range(periods)])  13.6 us
    ppermute x9, starting transfers between devices, to_later(): lax.ppermute(tail, 'tm', [(i, (i + 1) % periods) for i in range(periods)])  11.7 us
    ppermute x9, starting transfers between devices, over_chips(): return lax.ppermute(message, 'space', neighbour_pairs(1))  6.1 us
    pallas_call x1, Pallas kernels, body(): pl.pallas_call(first_kernel, out_shape=[pltpu.SMEM(x.shape, jnp.int32) fo...  1.96 us
  transfers between devices with their start and end apart: 27, of which 9 were waited for; matrix products, arithmetic and copies ran while one was open for 0% of the time, Pallas kernels for 28%

profile of v3, /device:TPU:0, one launch (start us, length us, event | category | flops | bytes accessed | tf_op | source)
XLA Modules:
  0.0 71.0 jit_solution(5465686532352281834)
XLA Ops:
  0.6 2.0 %arguments.1 = (s32[6,16]{1,0:T(8,128)S(4)}, s32[8]{0:T(128)S(4)}, f32[5,16,2048]{2,1,0:T(8,128)S(1)}, f32[5,2048]{1,0:T(8,128)S(1)}, f32[5,5,6,2048]{3,2,1,0:T(...) custom-call(s32[6,16]{1,0:T(8,128)} %bitcast.10, s32[8]{0:T(128)} %refs_1_.1, ...), custom_call_target="tpu_custom_call" | custom-call | flops 1 | bytes 1 | tf_op jit(solution)/shard_map/arguments/pallas_call | solution.py:578
  3.8 2.6 %collective-permute-start.1 = (f32[5,2,4096]{2,1,0:T(2,128)S(1)}, f32[5,2,4096]{2,1,0:T(2,128)S(1)}, u32[]{:S(2)}, u32[]{:S(2)}) collective-permute-start(f32[5,2,4096]{2,1,0:T(2,128)S(1)} %tail.1), channel_id=1, source_target_pairs={{0,8},{8,16},{16,24},{24,0},{1,9},{9,17},{17,25},{25,1},{2,10},{10... | collective-permute-start | bytes 491528 | tf_op jit(solution)/shard_map/ppermute | solution.py:558
  6.5 1.5 %own_part.7.part = f32[5,16,2048]{2,1,0:T(8,128)S(1)} custom-call(s32[6,16]{1,0:T(8,128)S(4)} %get-tuple-element.68.table, f32[5,16,2048]{2,1,0:T(8,128)S(1)} %get-tuple-element.70.field, f32[5,16,2048]{2,1,0:T(8,128)S(1)} %get-tuple-element.71.goal, f32[5,5,6,2048]{3,2,1,0:T(8,128)S(1)} %get-tuple-element.72.jacobian, ...), custom_call_target="tpu_custom_call" | custom-call | flops 1 | bytes 1 | tf_op jit(solution)/shard_map/own_part/pallas_call | solution.py:34
  9.1 1.5 %collective-permute-done.1.tail = f32[5,2,4096]{2,1,0:T(2,128)S(1)} collective-permute-done((f32[5,2,4096]{2,1,0:T(2,128)S(1)}, f32[5,2,4096]{2,1,0:T(2,128)S(1)}, u32[]{:S(2)}, u32[]{:S(2)}) %collective-permute-start.1) | collective-permute-done | bytes 163872 | tf_op jit(solution)/shard_map/ppermute | solution.py:558
  11.2 3.3 %collective-permute-start.3 = (f32[8,5,16,128]{3,2,1,0:T(8,128)S(1)}, f32[8,5,16,128]{3,2,1,0:T(8,128)S(1)}, u32[]{:S(2)}, u32[]{:S(2)}) collective-permute-start(f32[8,5,16,128]{3,2,1,0:T(8,128)S(1)} %get-tuple-element.82.faces), channel_id=1, source_target_pairs={{0,1},{2,3},{4,5},{6,7},{1,0},{3,2},{5,4},{7,6},{8,9},{10,11},{12,... | collective-permute-start | bytes 983048 | tf_op jit(solution)/shard_map/ppermute | solution.py:553
  14.5 1.5 %collective-permute-start.5 = (f32[5,2,3072]{2,1,0:T(2,128)S(1)}, f32[5,2,3072]{2,1,0:T(2,128)S(1)}, u32[]{:S(2)}, u32[]{:S(2)}) collective-permute-start(f32[5,2,3072]{2,1,0:T(2,128)S(1)} %get-tuple-element.87), channel_id=1, source_target_pairs={{0,8},{8,16},{16,24},{24,0},{1,9},{9,17},{17,25},{25,1},{2,10},{10... | collective-permute-start | bytes 368648 | tf_op jit(solution)/shard_map/ppermute | solution.py:558
  16.0 1.5 %own_part.8.part = f32[5,16,2048]{2,1,0:T(8,128)S(1)} custom-call(s32[6,16]{1,0:T(8,128)S(4)} %get-tuple-element.68.table, f32[5,16,2048]{2,1,0:T(8,128)S(1)} %get-tuple-element.81.field, f32[5,16,2048]{2,1,0:T(8,128)S(1)} %get-tuple-element.71.goal, f32[5,5,6,2048]{3,2,1,0:T(8,128)S(1)} %get-tuple-element.72.jacobian, ...), custom_call_target="tpu_custom_call" | custom-call | flops 1 | bytes 1 | tf_op jit(solution)/shard_map/own_part/pallas_call | solution.py:34
  19.4 1.3 %collective-permute-done.5.tail = f32[5,2,3072]{2,1,0:T(2,128)S(1)} collective-permute-done((f32[5,2,3072]{2,1,0:T(2,128)S(1)}, f32[5,2,3072]{2,1,0:T(2,128)S(1)}, u32[]{:S(2)}, u32[]{:S(2)}) %collective-permute-start.5) | collective-permute-done | bytes 122912 | tf_op jit(solution)/shard_map/ppermute | solution.py:558
  21.2 1.7 %collective-permute-start.6 = (f32[8,5,4,128]{3,2,1,0:T(4,128)S(1)}, f32[8,5,4,128]{3,2,1,0:T(4,128)S(1)}, u32[]{:S(2)}, u32[]{:S(2)}) collective-permute-start(f32[8,5,4,128]{3,2,1,0:T(4,128)S(1)} %get-tuple-element.90.faces), channel_id=1, source_target_pairs={{0,1},{2,3},{4,5},{6,7},{1,0},{3,2},{5,4},{7,6},{8,9},{10,11},{12,... | collective-permute-start | bytes 245768 | tf_op jit(solution)/shard_map/ppermute | solution.py:553
  22.9 2.2 %collective-permute-start.8 = (f32[5,2,3072]{2,1,0:T(2,128)S(1)}, f32[5,2,3072]{2,1,0:T(2,128)S(1)}, u32[]{:S(2)}, u32[]{:S(2)}) collective-permute-start(f32[5,2,3072]{2,1,0:T(2,128)S(1)} %get-tuple-element.96), channel_id=1, source_target_pairs={{0,8},{8,16},{16,24},{24,0},{1,9},{9,17},{17,25},{25,1},{2,10},{10... | collective-permute-start | bytes 368648 | tf_op jit(solution)/shard_map/ppermute | solution.py:558
  25.1 1.1 %own_part_of_means.1.part = f32[5,4,2048]{2,1,0:T(4,128)S(1)} custom-call(s32[6,16]{1,0:T(8,128)S(4)} %get-tuple-element.68.table, f32[5,16,2048]{2,1,0:T(8,128)S(1)} %get-tuple-element.88.field.fine, f32[5,16,2048]{2,1,0:T(8,128)S(1)} %get-tuple-element.71.goal, f32[5,4,2048]{2,1,0:T(4,128)S(1)} %get-tuple-element.89.means, ...), custom_call_target="tpu_custom_call" | custom-call | flops 1 | bytes 1 | tf_op jit(solution)/shard_map/own_part_of_means/pallas_call | solution.py:34
  27.5 0.8 %collective-permute-start.11 = (f32[5,2,3072]{2,1,0:T(2,128)S(1)}, f32[5,2,3072]{2,1,0:T(2,128)S(1)}, u32[]{:S(2)}, u32[]{:S(2)}) collective-permute-start(f32[5,2,3072]{2,1,0:T(2,128)S(1)} %get-tuple-element.103), channel_id=1, source_target_pairs={{0,8},{8,16},{16,24},{24,0},{1,9},{9,17},{17,25},{25,1},{2,10},{10... | collective-permute-start | bytes 368648 | tf_op jit(solution)/shard_map/ppermute | solution.py:558
  28.3 0.7 %collective-permute-done.8.tail = f32[5,2,3072]{2,1,0:T(2,128)S(1)} collective-permute-done((f32[5,2,3072]{2,1,0:T(2,128)S(1)}, f32[5,2,3072]{2,1,0:T(2,128)S(1)}, u32[]{:S(2)}, u32[]{:S(2)}) %collective-permute-start.8) | collective-permute-done | bytes 122912 | tf_op jit(solution)/shard_map/ppermute | solution.py:558
  29.3 1.9 %collective-permute-start.9 = (f32[8,5,4,128]{3,2,1,0:T(4,128)S(1)}, f32[8,5,4,128]{3,2,1,0:T(4,128)S(1)}, u32[]{:S(2)}, u32[]{:S(2)}) collective-permute-start(f32[8,5,4,128]{3,2,1,0:T(4,128)S(1)} %get-tuple-element.99.faces), channel_id=1, source_target_pairs={{0,1},{2,3},{4,5},{6,7},{1,0},{3,2},{5,4},{7,6},{8,9},{10,11},{12,... | collective-permute-start | bytes 245768 | tf_op jit(solution)/shard_map/ppermute | solution.py:553
  31.2 0.8 %own_part.9.part = f32[5,4,2048]{2,1,0:T(4,128)S(1)} custom-call(s32[6,16]{1,0:T(8,128)S(4)} %get-tuple-element.68.table, f32[5,4,2048]{2,1,0:T(4,128)S(1)} %get-tuple-element.97.field, f32[5,4,2048]{2,1,0:T(4,128)S(1)} %get-tuple-element.98.goal, f32[5,5,6,2048]{3,2,1,0:T(8,128)S(1)} %get-tuple-element.72.jacobian, ...), custom_call_target="tpu_custom_call" | custom-call | flops 1 | bytes 1 | tf_op jit(solution)/shard_map/own_part/pallas_call | solution.py:34
  33.7 3.0 %collective-permute-start.12 = (f32[8,5,4,128]{3,2,1,0:T(4,128)S(1)}, f32[8,5,4,128]{3,2,1,0:T(4,128)S(1)}, u32[]{:S(2)}, u32[]{:S(2)}) collective-permute-start(f32[8,5,4,128]{3,2,1,0:T(4,128)S(1)} %get-tuple-element.105.faces), channel_id=1, source_target_pairs={{0,1},{2,3},{4,5},{6,7},{1,0},{3,2},{5,4},{7,6},{8,9},{10,11},{12,... | collective-permute-start | bytes 245768 | tf_op jit(solution)/shard_map/ppermute | solution.py:553
  37.0 0.8 %own_part.10.part = f32[5,4,2048]{2,1,0:T(4,128)S(1)} custom-call(s32[6,16]{1,0:T(8,128)S(4)} %get-tuple-element.68.table, f32[5,4,2048]{2,1,0:T(4,128)S(1)} %get-tuple-element.104.field, f32[5,4,2048]{2,1,0:T(4,128)S(1)} %get-tuple-element.98.goal, f32[5,5,6,2048]{3,2,1,0:T(8,128)S(1)} %get-tuple-element.72.jacobian, ...), custom_call_target="tpu_custom_call" | custom-call | flops 1 | bytes 1 | tf_op jit(solution)/shard_map/own_part/pallas_call | solution.py:34
  39.1 1.7 %collective-permute-start.17 = (f32[5,2,3072]{2,1,0:T(2,128)S(1)}, f32[5,2,3072]{2,1,0:T(2,128)S(1)}, u32[]{:S(2)}, u32[]{:S(2)}) collective-permute-start(f32[5,2,3072]{2,1,0:T(2,128)S(1)} %get-tuple-element.115), channel_id=1, source_target_pairs={{0,8},{8,16},{16,24},{24,0},{1,9},{9,17},{17,25},{25,1},{2,10},{10... | collective-permute-start | bytes 368648 | tf_op jit(solution)/shard_map/ppermute | solution.py:558
  40.8 2.0 %collective-permute-done.14.tail = f32[5,2,3072]{2,1,0:T(2,128)S(1)} collective-permute-done((f32[5,2,3072]{2,1,0:T(2,128)S(1)}, f32[5,2,3072]{2,1,0:T(2,128)S(1)}, u32[]{:S(2)}, u32[]{:S(2)}) %collective-permute-start.14) | collective-permute-done | bytes 122912 | tf_op jit(solution)/shard_map/ppermute | solution.py:558
  43.2 0.8 %own_part.11.part = f32[5,4,2048]{2,1,0:T(4,128)S(1)} custom-call(s32[6,16]{1,0:T(8,128)S(4)} %get-tuple-element.68.table, f32[5,4,2048]{2,1,0:T(4,128)S(1)} %get-tuple-element.110.field, f32[5,4,2048]{2,1,0:T(4,128)S(1)} %get-tuple-element.98.goal, f32[5,5,6,2048]{3,2,1,0:T(8,128)S(1)} %get-tuple-element.72.jacobian, ...), custom_call_target="tpu_custom_call" | custom-call | flops 1 | bytes 1 | tf_op jit(solution)/shard_map/own_part/pallas_call | solution.py:34
  46.3 2.6 %collective-permute-start.18 = (f32[8,5,16,128]{3,2,1,0:T(8,128)S(1)}, f32[8,5,16,128]{3,2,1,0:T(8,128)S(1)}, u32[]{:S(2)}, u32[]{:S(2)}) collective-permute-start(f32[8,5,16,128]{3,2,1,0:T(8,128)S(1)} %get-tuple-element.117.faces), channel_id=1, source_target_pairs={{0,1},{2,3},{4,5},{6,7},{1,0},{3,2},{5,4},{7,6},{8,9},{10,11},{12,... | collective-permute-start | bytes 983048 | tf_op jit(solution)/shard_map/ppermute | solution.py:553
  48.9 0.7 %collective-permute-start.20 = (f32[5,2,3072]{2,1,0:T(2,128)S(1)}, f32[5,2,3072]{2,1,0:T(2,128)S(1)}, u32[]{:S(2)}, u32[]{:S(2)}) collective-permute-start(f32[5,2,3072]{2,1,0:T(2,128)S(1)} %get-tuple-element.121), channel_id=1, source_target_pairs={{0,8},{8,16},{16,24},{24,0},{1,9},{9,17},{17,25},{25,1},{2,10},{10... | collective-permute-start | bytes 368648 | tf_op jit(solution)/shard_map/ppermute | solution.py:558
  49.6 1.5 %own_part.12.part = f32[5,16,2048]{2,1,0:T(8,128)S(1)} custom-call(s32[6,16]{1,0:T(8,128)S(4)} %get-tuple-element.68.table, f32[5,16,2048]{2,1,0:T(8,128)S(1)} %get-tuple-element.116.field, f32[5,16,2048]{2,1,0:T(8,128)S(1)} %get-tuple-element.71.goal, f32[5,5,6,2048]{3,2,1,0:T(8,128)S(1)} %get-tuple-element.72.jacobian, ...), custom_call_target="tpu_custom_call" | custom-call | flops 1 | bytes 1 | tf_op jit(solution)/shard_map/own_part/pallas_call | solution.py:34
  52.8 2.3 %collective-permute-done.20.tail = f32[5,2,3072]{2,1,0:T(2,128)S(1)} collective-permute-done((f32[5,2,3072]{2,1,0:T(2,128)S(1)}, f32[5,2,3072]{2,1,0:T(2,128)S(1)}, u32[]{:S(2)}, u32[]{:S(2)}) %collective-permute-start.20) | collective-permute-done | bytes 122912 | tf_op jit(solution)/shard_map/ppermute | solution.py:558
  55.4 0.9 %collective-permute-start.21 = (f32[8,5,16,128]{3,2,1,0:T(8,128)S(1)}, f32[8,5,16,128]{3,2,1,0:T(8,128)S(1)}, u32[]{:S(2)}, u32[]{:S(2)}) collective-permute-start(f32[8,5,16,128]{3,2,1,0:T(8,128)S(1)} %get-tuple-element.123.faces), channel_id=1, source_target_pairs={{0,1},{2,3},{4,5},{6,7},{1,0},{3,2},{5,4},{7,6},{8,9},{10,11},{12,... | collective-permute-start | bytes 983048 | tf_op jit(solution)/shard_map/ppermute | solution.py:553
  56.3 1.1 %collective-permute-start.23 = (f32[5,2,3072]{2,1,0:T(2,128)S(1)}, f32[5,2,3072]{2,1,0:T(2,128)S(1)}, u32[]{:S(2)}, u32[]{:S(2)}) collective-permute-start(f32[5,2,3072]{2,1,0:T(2,128)S(1)} %get-tuple-element.127), channel_id=1, source_target_pairs={{0,8},{8,16},{16,24},{24,0},{1,9},{9,17},{17,25},{25,1},{2,10},{10... | collective-permute-start | bytes 368648 | tf_op jit(solution)/shard_map/ppermute | solution.py:558
  57.4 1.5 %own_part.13.part = f32[5,16,2048]{2,1,0:T(8,128)S(1)} custom-call(s32[6,16]{1,0:T(8,128)S(4)} %get-tuple-element.68.table, f32[5,16,2048]{2,1,0:T(8,128)S(1)} %get-tuple-element.122.field, f32[5,16,2048]{2,1,0:T(8,128)S(1)} %get-tuple-element.71.goal, f32[5,5,6,2048]{3,2,1,0:T(8,128)S(1)} %get-tuple-element.72.jacobian, ...), custom_call_target="tpu_custom_call" | custom-call | flops 1 | bytes 1 | tf_op jit(solution)/shard_map/own_part/pallas_call | solution.py:34
  60.6 2.1 %collective-permute-done.23.tail = f32[5,2,3072]{2,1,0:T(2,128)S(1)} collective-permute-done((f32[5,2,3072]{2,1,0:T(2,128)S(1)}, f32[5,2,3072]{2,1,0:T(2,128)S(1)}, u32[]{:S(2)}, u32[]{:S(2)}) %collective-permute-start.23) | collective-permute-done | bytes 122912 | tf_op jit(solution)/shard_map/ppermute | solution.py:558
  63.4 0.7 %collective-permute-start.26 = (f32[5,2,3072]{2,1,0:T(2,128)S(1)}, f32[5,2,3072]{2,1,0:T(2,128)S(1)}, u32[]{:S(2)}, u32[]{:S(2)}) collective-permute-start(f32[5,2,3072]{2,1,0:T(2,128)S(1)} %get-tuple-element.133), channel_id=1, source_target_pairs={{0,8},{8,16},{16,24},{24,0},{1,9},{9,17},{17,25},{25,1},{2,10},{10... | collective-permute-start | bytes 368648 | tf_op jit(solution)/shard_map/ppermute | solution.py:558
  64.1 1.5 %last_own_part.1 = (f32[5,16,2048]{2,1,0:T(8,128)S(1)}, f32[5,16,2048]{2,1,0:T(8,128)}) custom-call(s32[6,16]{1,0:T(8,128)S(4)} %get-tuple-element.68.table, f32[5,16,2048]{2,1,0:T(8,128)S(1)} %get-tuple-element.128.field, f32[5,16,2048]{2,1,0:T(8,128)S(1)} %get-tuple-element.71.goal, f32[5,5,6,2048]{3,2,1,0:T(8,128)S(1)} %get-tuple-element.72.jacobian, ...), custom_call_target="tpu_custom_call" | custom-call | flops 1 | bytes 1 | tf_op jit(solution)/shard_map/last_own_part/pallas_call | solution.py:34
  65.9 3.7 %collective-permute-done.26.tail = f32[5,2,3072]{2,1,0:T(2,128)S(1)} collective-permute-done((f32[5,2,3072]{2,1,0:T(2,128)S(1)}, f32[5,2,3072]{2,1,0:T(2,128)S(1)}, u32[]{:S(2)}, u32[]{:S(2)}) %collective-permute-start.26) | collective-permute-done | bytes 122912 | tf_op jit(solution)/shard_map/ppermute | solution.py:558
  69.8 1.1 %residual.1 = f32[5,16,2048]{2,1,0:T(8,128)} custom-call(s32[6,16]{1,0:T(8,128)S(4)} %get-tuple-element.68.table, f32[5,16,2048]{2,1,0:T(8,128)S(1)} %beside_part.1.part, f32[8,5,16,128]{3,2,1,0:T(8,128)S(1)} %rim.5, f32[5,2,3072]{2,1,0:T(2,128)S(1)} %collective-permute-done.26.tail, f32[2,5,5,2048]{3,2,1,0:T(8,128)S(1)} %get-tuple-element.76.rim_jacobian), custom_call_target="tpu_custom_call" | custom-call | flops 1 | bytes 1 | tf_op jit(solution)/shard_map/residual/pallas_call | solution.py:34
  (69 shorter events, 17.5 us)
Async XLA Ops:
  2.6 5.4 %collective-permute-start = (f32[8,5,16,128]{3,2,1,0:T(8,128)S(1)}, f32[8,5,16,128]{3,2,1,0:T(8,128)S(1)}, u32[]{:S(2)}, u32[]{:S(2)}) collective-permute-start(f32[8,5,16,128]{3,2,1,0:T(8,128)S(1)} %get-tuple-element.75.faces), channel_id=1, source_target_pairs={{0,1},{2,3},{4,5},{6,7},{1,0},{3,2},{5,4},{7,6},{8,9},{10,11},{12,... | collective-permute-start | bytes 983048 | tf_op jit(solution)/shard_map/ppermute | solution.py:553
  3.1 7.5 %collective-permute-start.2 = (f32[8,5,16,128]{3,2,1,0:T(8,128)S(1)}, f32[8,5,16,128]{3,2,1,0:T(8,128)S(1)}, u32[]{:S(2)}, u32[]{:S(2)}) collective-permute-start(f32[8,5,16,128]{3,2,1,0:T(8,128)S(1)} %get-tuple-element.75.faces), channel_id=1, source_target_pairs={{1,2},{3,4},{5,6},{2,1},{4,3},{6,5},{9,10},{11,12},{13,14},{10,9},... | collective-permute-start | bytes 983048 | tf_op jit(solution)/shard_map/ppermute | solution.py:549
  3.8 6.8 %collective-permute-start.1 = (f32[5,2,4096]{2,1,0:T(2,128)S(1)}, f32[5,2,4096]{2,1,0:T(2,128)S(1)}, u32[]{:S(2)}, u32[]{:S(2)}) collective-permute-start(f32[5,2,4096]{2,1,0:T(2,128)S(1)} %tail.1), channel_id=1, source_target_pairs={{0,8},{8,16},{16,24},{24,0},{1,9},{9,17},{17,25},{25,1},{2,10},{10... | collective-permute-start | bytes 491528 | tf_op jit(solution)/shard_map/ppermute | solution.py:558
  8.4 10.2 %collective-permute-start.4 = (f32[8,120,128]{2,1,0:T(8,128)S(1)}, f32[8,120,128]{2,1,0:T(8,128)S(1)}, u32[]{:S(2)}, u32[]{:S(2)}) collective-permute-start(f32[8,120,128]{2,1,0:T(8,128)S(1)} %get-tuple-element.84), channel_id=1, source_target_pairs={{1,2},{3,4},{5,6},{2,1},{4,3},{6,5},{9,10},{11,12},{13,14},{10,9},... | collective-permute-start | bytes 1474568 | tf_op jit(solution)/shard_map/ppermute | solution.py:549
  11.2 6.2 %collective-permute-start.3 = (f32[8,5,16,128]{3,2,1,0:T(8,128)S(1)}, f32[8,5,16,128]{3,2,1,0:T(8,128)S(1)}, u32[]{:S(2)}, u32[]{:S(2)}) collective-permute-start(f32[8,5,16,128]{3,2,1,0:T(8,128)S(1)} %get-tuple-element.82.faces), channel_id=1, source_target_pairs={{0,1},{2,3},{4,5},{6,7},{1,0},{3,2},{5,4},{7,6},{8,9},{10,11},{12,... | collective-permute-start | bytes 983048 | tf_op jit(solution)/shard_map/ppermute | solution.py:553
  14.5 6.2 %collective-permute-start.5 = (f32[5,2,3072]{2,1,0:T(2,128)S(1)}, f32[5,2,3072]{2,1,0:T(2,128)S(1)}, u32[]{:S(2)}, u32[]{:S(2)}) collective-permute-start(f32[5,2,3072]{2,1,0:T(2,128)S(1)} %get-tuple-element.87), channel_id=1, source_target_pairs={{0,8},{8,16},{16,24},{24,0},{1,9},{9,17},{17,25},{25,1},{2,10},{10... | collective-permute-start | bytes 368648 | tf_op jit(solution)/shard_map/ppermute | solution.py:558
  18.0 9.1 %collective-permute-start.7 = (f32[8,5,6,128]{3,2,1,0:T(8,128)S(1)}, f32[8,5,6,128]{3,2,1,0:T(8,128)S(1)}, u32[]{:S(2)}, u32[]{:S(2)}) collective-permute-start(f32[8,5,6,128]{3,2,1,0:T(8,128)S(1)} %get-tuple-element.85.next_message), channel_id=1, source_target_pairs={{1,2},{3,4},{5,6},{2,1},{4,3},{6,5},{9,10},{11,12},{13,14},{10,9},... | collective-permute-start | bytes 368648 | tf_op jit(solution)/shard_map/ppermute | solution.py:549
  21.2 5.0 %collective-permute-start.6 = (f32[8,5,4,128]{3,2,1,0:T(4,128)S(1)}, f32[8,5,4,128]{3,2,1,0:T(4,128)S(1)}, u32[]{:S(2)}, u32[]{:S(2)}) collective-permute-start(f32[8,5,4,128]{3,2,1,0:T(4,128)S(1)} %get-tuple-element.90.faces), channel_id=1, source_target_pairs={{0,1},{2,3},{4,5},{6,7},{1,0},{3,2},{5,4},{7,6},{8,9},{10,11},{12,... | collective-permute-start | bytes 245768 | tf_op jit(solution)/shard_map/ppermute | solution.py:553
  22.9 6.2 %collective-permute-start.8 = (f32[5,2,3072]{2,1,0:T(2,128)S(1)}, f32[5,2,3072]{2,1,0:T(2,128)S(1)}, u32[]{:S(2)}, u32[]{:S(2)}) collective-permute-start(f32[5,2,3072]{2,1,0:T(2,128)S(1)} %get-tuple-element.96), channel_id=1, source_target_pairs={{0,8},{8,16},{16,24},{24,0},{1,9},{9,17},{17,25},{25,1},{2,10},{10... | collective-permute-start | bytes 368648 | tf_op jit(solution)/shard_map/ppermute | solution.py:558
  26.4 6.7 %collective-permute-start.10 = (f32[16,5,4,128]{3,2,1,0:T(4,128)S(1)}, f32[16,5,4,128]{3,2,1,0:T(4,128)S(1)}, u32[]{:S(2)}, u32[]{:S(2)}) collective-permute-start(f32[16,5,4,128]{3,2,1,0:T(4,128)S(1)} %get-tuple-element.101), channel_id=1, source_target_pairs={{1,2},{3,4},{5,6},{2,1},{4,3},{6,5},{9,10},{11,12},{13,14},{10,9},... | collective-permute-start | bytes 491528 | tf_op jit(solution)/shard_map/ppermute | solution.py:549
  27.5 5.9 %collective-permute-start.11 = (f32[5,2,3072]{2,1,0:T(2,128)S(1)}, f32[5,2,3072]{2,1,0:T(2,128)S(1)}, u32[]{:S(2)}, u32[]{:S(2)}) collective-permute-start(f32[5,2,3072]{2,1,0:T(2,128)S(1)} %get-tuple-element.103), channel_id=1, source_target_pairs={{0,8},{8,16},{16,24},{24,0},{1,9},{9,17},{17,25},{25,1},{2,10},{10... | collective-permute-start | bytes 368648 | tf_op jit(solution)/shard_map/ppermute | solution.py:558
  29.3 2.9 %collective-permute-start.9 = (f32[8,5,4,128]{3,2,1,0:T(4,128)S(1)}, f32[8,5,4,128]{3,2,1,0:T(4,128)S(1)}, u32[]{:S(2)}, u32[]{:S(2)}) collective-permute-start(f32[8,5,4,128]{3,2,1,0:T(4,128)S(1)} %get-tuple-element.99.faces), channel_id=1, source_target_pairs={{0,1},{2,3},{4,5},{6,7},{1,0},{3,2},{5,4},{7,6},{8,9},{10,11},{12,... | collective-permute-start | bytes 245768 | tf_op jit(solution)/shard_map/ppermute | solution.py:553
  32.4 6.3 %collective-permute-start.13 = (f32[16,5,4,128]{3,2,1,0:T(4,128)S(1)}, f32[16,5,4,128]{3,2,1,0:T(4,128)S(1)}, u32[]{:S(2)}, u32[]{:S(2)}) collective-permute-start(f32[16,5,4,128]{3,2,1,0:T(4,128)S(1)} %get-tuple-element.107), channel_id=1, source_target_pairs={{1,2},{3,4},{5,6},{2,1},{4,3},{6,5},{9,10},{11,12},{13,14},{10,9},... | collective-permute-start | bytes 491528 | tf_op jit(solution)/shard_map/ppermute | solution.py:549
  33.7 4.1 %collective-permute-start.12 = (f32[8,5,4,128]{3,2,1,0:T(4,128)S(1)}, f32[8,5,4,128]{3,2,1,0:T(4,128)S(1)}, u32[]{:S(2)}, u32[]{:S(2)}) collective-permute-start(f32[8,5,4,128]{3,2,1,0:T(4,128)S(1)} %get-tuple-element.105.faces), channel_id=1, source_target_pairs={{0,1},{2,3},{4,5},{6,7},{1,0},{3,2},{5,4},{7,6},{8,9},{10,11},{12,... | collective-permute-start | bytes 245768 | tf_op jit(solution)/shard_map/ppermute | solution.py:553
  36.7 6.2 %collective-permute-start.14 = (f32[5,2,3072]{2,1,0:T(2,128)S(1)}, f32[5,2,3072]{2,1,0:T(2,128)S(1)}, u32[]{:S(2)}, u32[]{:S(2)}) collective-permute-start(f32[5,2,3072]{2,1,0:T(2,128)S(1)} %get-tuple-element.109), channel_id=1, source_target_pairs={{0,8},{8,16},{16,24},{24,0},{1,9},{9,17},{17,25},{25,1},{2,10},{10... | collective-permute-start | bytes 368648 | tf_op jit(solution)/shard_map/ppermute | solution.py:558
  38.1 7.4 %collective-permute-start.16 = (f32[16,5,4,128]{3,2,1,0:T(4,128)S(1)}, f32[16,5,4,128]{3,2,1,0:T(4,128)S(1)}, u32[]{:S(2)}, u32[]{:S(2)}) collective-permute-start(f32[16,5,4,128]{3,2,1,0:T(4,128)S(1)} %get-tuple-element.113), channel_id=1, source_target_pairs={{1,2},{3,4},{5,6},{2,1},{4,3},{6,5},{9,10},{11,12},{13,14},{10,9},... | collective-permute-start | bytes 491528 | tf_op jit(solution)/shard_map/ppermute | solution.py:549
  39.1 6.9 %collective-permute-start.17 = (f32[5,2,3072]{2,1,0:T(2,128)S(1)}, f32[5,2,3072]{2,1,0:T(2,128)S(1)}, u32[]{:S(2)}, u32[]{:S(2)}) collective-permute-start(f32[5,2,3072]{2,1,0:T(2,128)S(1)} %get-tuple-element.115), channel_id=1, source_target_pairs={{0,8},{8,16},{16,24},{24,0},{1,9},{9,17},{17,25},{25,1},{2,10},{10... | collective-permute-start | bytes 368648 | tf_op jit(solution)/shard_map/ppermute | solution.py:558
  43.1 1.3 %collective-permute-start.15 = (f32[8,5,4,128]{3,2,1,0:T(4,128)S(1)}, f32[8,5,4,128]{3,2,1,0:T(4,128)S(1)}, u32[]{:S(2)}, u32[]{:S(2)}) collective-permute-start(f32[8,5,4,128]{3,2,1,0:T(4,128)S(1)} %get-tuple-element.111.faces), channel_id=1, source_target_pairs={{0,1},{2,3},{4,5},{6,7},{1,0},{3,2},{5,4},{7,6},{8,9},{10,11},{12,... | collective-permute-start | bytes 245768 | tf_op jit(solution)/shard_map/ppermute | solution.py:553
  44.8 7.4 %collective-permute-start.19 = (f32[9,5,16,128]{3,2,1,0:T(8,128)S(1)}, f32[9,5,16,128]{3,2,1,0:T(8,128)S(1)}, u32[]{:S(2)}, u32[]{:S(2)}) collective-permute-start(f32[9,5,16,128]{3,2,1,0:T(8,128)S(1)} %get-tuple-element.119), channel_id=1, source_target_pairs={{1,2},{3,4},{5,6},{2,1},{4,3},{6,5},{9,10},{11,12},{13,14},{10,9},... | collective-permute-start | bytes 1105928 | tf_op jit(solution)/shard_map/ppermute | solution.py:549
  46.3 4.8 %collective-permute-start.18 = (f32[8,5,16,128]{3,2,1,0:T(8,128)S(1)}, f32[8,5,16,128]{3,2,1,0:T(8,128)S(1)}, u32[]{:S(2)}, u32[]{:S(2)}) collective-permute-start(f32[8,5,16,128]{3,2,1,0:T(8,128)S(1)} %get-tuple-element.117.faces), channel_id=1, source_target_pairs={{0,1},{2,3},{4,5},{6,7},{1,0},{3,2},{5,4},{7,6},{8,9},{10,11},{12,... | collective-permute-start | bytes 983048 | tf_op jit(solution)/shard_map/ppermute | solution.py:553
  48.9 6.2 %collective-permute-start.20 = (f32[5,2,3072]{2,1,0:T(2,128)S(1)}, f32[5,2,3072]{2,1,0:T(2,128)S(1)}, u32[]{:S(2)}, u32[]{:S(2)}) collective-permute-start(f32[5,2,3072]{2,1,0:T(2,128)S(1)} %get-tuple-element.121), channel_id=1, source_target_pairs={{0,8},{8,16},{16,24},{24,0},{1,9},{9,17},{17,25},{25,1},{2,10},{10... | collective-permute-start | bytes 368648 | tf_op jit(solution)/shard_map/ppermute | solution.py:558
  51.5 8.4 %collective-permute-start.22 = (f32[9,5,16,128]{3,2,1,0:T(8,128)S(1)}, f32[9,5,16,128]{3,2,1,0:T(8,128)S(1)}, u32[]{:S(2)}, u32[]{:S(2)}) collective-permute-start(f32[9,5,16,128]{3,2,1,0:T(8,128)S(1)} %get-tuple-element.125), channel_id=1, source_target_pairs={{1,2},{3,4},{5,6},{2,1},{4,3},{6,5},{9,10},{11,12},{13,14},{10,9},... | collective-permute-start | bytes 1105928 | tf_op jit(solution)/shard_map/ppermute | solution.py:549
  55.4 3.5 %collective-permute-start.21 = (f32[8,5,16,128]{3,2,1,0:T(8,128)S(1)}, f32[8,5,16,128]{3,2,1,0:T(8,128)S(1)}, u32[]{:S(2)}, u32[]{:S(2)}) collective-permute-start(f32[8,5,16,128]{3,2,1,0:T(8,128)S(1)} %get-tuple-element.123.faces), channel_id=1, source_target_pairs={{0,1},{2,3},{4,5},{6,7},{1,0},{3,2},{5,4},{7,6},{8,9},{10,11},{12,... | collective-permute-start | bytes 983048 | tf_op jit(solution)/shard_map/ppermute | solution.py:553
  56.3 6.4 %collective-permute-start.23 = (f32[5,2,3072]{2,1,0:T(2,128)S(1)}, f32[5,2,3072]{2,1,0:T(2,128)S(1)}, u32[]{:S(2)}, u32[]{:S(2)}) collective-permute-start(f32[5,2,3072]{2,1,0:T(2,128)S(1)} %get-tuple-element.127), channel_id=1, source_target_pairs={{0,8},{8,16},{16,24},{24,0},{1,9},{9,17},{17,25},{25,1},{2,10},{10... | collective-permute-start | bytes 368648 | tf_op jit(solution)/shard_map/ppermute | solution.py:558
  59.3 10.3 %collective-permute-start.25 = (f32[9,5,16,128]{3,2,1,0:T(8,128)S(1)}, f32[9,5,16,128]{3,2,1,0:T(8,128)S(1)}, u32[]{:S(2)}, u32[]{:S(2)}) collective-permute-start(f32[9,5,16,128]{3,2,1,0:T(8,128)S(1)} %get-tuple-element.132), channel_id=1, source_target_pairs={{1,2},{3,4},{5,6},{2,1},{4,3},{6,5},{9,10},{11,12},{13,14},{10,9},... | collective-permute-start | bytes 1105928 | tf_op jit(solution)/shard_map/ppermute | solution.py:549
  62.9 2.7 %collective-permute-start.24 = (f32[8,5,16,128]{3,2,1,0:T(8,128)S(1)}, f32[8,5,16,128]{3,2,1,0:T(8,128)S(1)}, u32[]{:S(2)}, u32[]{:S(2)}) collective-permute-start(f32[8,5,16,128]{3,2,1,0:T(8,128)S(1)} %get-tuple-element.131), channel_id=1, source_target_pairs={{0,1},{2,3},{4,5},{6,7},{1,0},{3,2},{5,4},{7,6},{8,9},{10,11},{12,... | collective-permute-start | bytes 983048 | tf_op jit(solution)/shard_map/ppermute | solution.py:553
  63.4 6.2 %collective-permute-start.26 = (f32[5,2,3072]{2,1,0:T(2,128)S(1)}, f32[5,2,3072]{2,1,0:T(2,128)S(1)}, u32[]{:S(2)}, u32[]{:S(2)}) collective-permute-start(f32[5,2,3072]{2,1,0:T(2,128)S(1)} %get-tuple-element.133), channel_id=1, source_target_pairs={{0,8},{8,16},{16,24},{24,0},{1,9},{9,17},{17,25},{25,1},{2,10},{10... | collective-permute-start | bytes 368648 | tf_op jit(solution)/shard_map/ppermute | solution.py:558

commit v4 on v3

--- a/solution.py
+++ b/solution.py
@@ -19,7 +19,8 @@
 coarse_weight = time_weight / GROUP
 damping = 0.7
 
-UNROLL = 8
+UNROLL = 16
+OWN_UNROLL = 8
 SCRATCH_BYTES = 4 << 20
 IN_VMEM = pl.BlockSpec(memory_space=pltpu.VMEM)
 NOTHING = pl.CostEstimate(flops=1, bytes_accessed=1, transcendentals=0)
@@ -62,8 +63,8 @@
     return lax.rem(lax.axis_index("space"), 2)
 
 
-def each_block(count, step):
-    unroll = UNROLL if count % UNROLL == 0 else 1
+def each_block(count, step, unroll=UNROLL):
+    unroll = min(unroll, count) if count % min(unroll, count) == 0 else 1
 
     def steps(i, carry):
         for u in range(unroll):
@@ -170,7 +171,7 @@
             tail_out[a, pl.ds(0, 1), pl.ds(0, cells)] = weight * (before - 4.0 * last)
             tail_out[a, pl.ds(1, 1), pl.ds(0, cells)] = weight * last
     if rim is not None:
-        for h in range((tail_out.shape[2] - cells) // BLK):
+        for h in range(rim.shape[0]):
             for a in range(NV):
                 rows = tail_rows(rim[h, a, pl.ds(rim.shape[2] - 2, 2), :], rim_weight, rim_mean)
                 tail_out[a, :, pl.ds(cells + h * BLK, BLK)] = rows
@@ -193,7 +194,7 @@
         for a in range(NV):
             out[a, :, lanes] = total[a]
 
-    each_block(table.shape[1], step)
+    each_block(table.shape[1], step, OWN_UNROLL)
 
 
 def mean_rows(v, scratch, steps):
@@ -221,7 +222,7 @@
         for a in range(NV):
             out[a, :, lanes] = total[a]
 
-    each_block(table.shape[1], step)
+    each_block(table.shape[1], step, OWN_UNROLL)
 
 
 def beside_part(table, part, rim, rim_jacobian, out):
@@ -371,9 +372,8 @@
     return spread_tail(rows) if spread else rows
 
 
-def finish_kernel(steps, level, spread, rim, tail, first_message, rim_out):
+def finish_kernel(steps, cells, level, spread, rim, tail, first_message, rim_out):
     partner = Partner(first_message, steps, level)
-    cells = tail.shape[2] - rim.shape[0] * BLK
 
     def step(h, u):
         for a in range(NV):
@@ -439,10 +439,9 @@
     copy.wait()
 
 
-def last_rim_kernel(steps, index, faces, message, tail, first_message, out):
+def last_rim_kernel(steps, cells, index, faces, message, tail, first_message, out):
     rim_kernel(steps, 0, index, faces, message, first_message, out)
     partner = Partner(first_message, steps, 0)
-    cells = tail.shape[2] - index.shape[0] * BLK
 
     def step(h, u):
         for a in range(NV):
@@ -623,7 +622,7 @@
             if ahead or level is None:
                 return rim, level
             return call(
-                bind(finish_kernel, steps, level, spread), "finish_rim", [], [rim, tail, first_message],
+                bind(finish_kernel, steps, cells, level, spread), "finish_rim", [], [rim, tail, first_message],
                 [shape(*rim.shape)],
             )[0], None
 
@@ -785,7 +784,7 @@
     )
     part = call(beside_part, "beside_part", [table], [part, beside, rim_jacobian], [whole(steps)], per_slot * steps)[0]
     rim = call(
-        bind(last_rim_kernel, steps), "rim", [index], [earlier_sent, message, tail, first_message], [face(steps)],
+        bind(last_rim_kernel, steps, cells), "rim", [index], [earlier_sent, message, tail, first_message], [face(steps)],
         per_slot * steps // 2,
     )[0]
     residual = call(

time: 71.4 us -> 70.5 us (0.987)
  Pallas kernels: 23.3 us -> 22 us
  waiting for transfers between devices: 14.1 us -> 15.1 us
    pallas_call x45, Pallas kernels: 21.2 us -> 19.9 us  [call(): pl.pallas_call(kernel, out_shape=[o if out_specs and out_specs[i] is IN_H...]
    ppermute x9, waiting for transfers between devices: 13.6 us -> 14.5 us  [to_later(): lax.ppermute(tail, 'tm', [(i, (i + 1) % periods) for i in range(periods)])]
    ppermute x9, starting transfers between devices: 14.5 us -> 13.7 us  [on_chip(): return lax.ppermute(faces, 'space', neighbour_pairs(0))]
  transfers between devices with their start and end apart: 27 -> 27, of which waited for: 9 -> 9; matrix products, arithmetic and copies ran while one was open for 0% -> 0% of each run, Pallas kernels for 28% -> 27%
where the time goes in v4:
time: 70.5 us; the launch traced here: 70.1 us
  starting transfers between devices  31.8 us (45%)
  Pallas kernels  22 us (31%)
  waiting for transfers between devices  15.1 us (21%)
  between operations  1.26 us (2%)
    pallas_call x45, Pallas kernels, call(): pl.pallas_call(kernel, out_shape=[o if out_specs and out_specs[i] is IN_H...  19.9 us
    ppermute x9, waiting for transfers between devices, to_later(): lax.ppermute(tail, 'tm', [(i, (i + 1) % periods) for i in range(periods)])  14.5 us
    ppermute x9, starting transfers between devices, on_chip(): return lax.ppermute(faces, 'space', neighbour_pairs(0))  13.7 us
    ppermute x9, starting transfers between devices, to_later(): lax.ppermute(tail, 'tm', [(i, (i + 1) % periods) for i in range(periods)])  12 us
    ppermute x9, starting transfers between devices, over_chips(): return lax.ppermute(message, 'space', neighbour_pairs(1))  6.1 us
    pallas_call x1, Pallas kernels, body(): pl.pallas_call(first_kernel, out_shape=[pltpu.SMEM(x.shape, jnp.int32) fo...  1.96 us
  transfers between devices with their start and end apart: 27, of which 9 were waited for; matrix products, arithmetic and copies ran while one was open for 0% of the time, Pallas kernels for 27%

profile of v4, /device:TPU:0, one launch (start us, length us, event | category | flops | bytes accessed | tf_op | source)
XLA Modules:
  0.0 70.1 jit_solution(4488081725398994801)
XLA Ops:
  0.6 2.0 %arguments.1 = (s32[6,16]{1,0:T(8,128)S(4)}, s32[8]{0:T(128)S(4)}, f32[5,16,2048]{2,1,0:T(8,128)S(1)}, f32[5,2048]{1,0:T(8,128)S(1)}, f32[5,5,6,2048]{3,2,1,0:T(...) custom-call(s32[6,16]{1,0:T(8,128)} %bitcast.10, s32[8]{0:T(128)} %refs_1_.1, ...), custom_call_target="tpu_custom_call" | custom-call | flops 1 | bytes 1 | tf_op jit(solution)/shard_map/arguments/pallas_call | solution.py:577
  3.8 2.6 %collective-permute-start.1 = (f32[5,2,4096]{2,1,0:T(2,128)S(1)}, f32[5,2,4096]{2,1,0:T(2,128)S(1)}, u32[]{:S(2)}, u32[]{:S(2)}) collective-permute-start(f32[5,2,4096]{2,1,0:T(2,128)S(1)} %tail.1), channel_id=1, source_target_pairs={{0,8},{8,16},{16,24},{24,0},{1,9},{9,17},{17,25},{25,1},{2,10},{10... | collective-permute-start | bytes 491528 | tf_op jit(solution)/shard_map/ppermute | solution.py:557
  6.5 1.5 %own_part.7.part = f32[5,16,2048]{2,1,0:T(8,128)S(1)} custom-call(s32[6,16]{1,0:T(8,128)S(4)} %get-tuple-element.68.table, f32[5,16,2048]{2,1,0:T(8,128)S(1)} %get-tuple-element.70.field, f32[5,16,2048]{2,1,0:T(8,128)S(1)} %get-tuple-element.71.goal, f32[5,5,6,2048]{3,2,1,0:T(8,128)S(1)} %get-tuple-element.72.jacobian, ...), custom_call_target="tpu_custom_call" | custom-call | flops 1 | bytes 1 | tf_op jit(solution)/shard_map/own_part/pallas_call | solution.py:35
  8.4 0.7 collective-permute-start.4
  9.1 1.6 %collective-permute-done.1.tail = f32[5,2,4096]{2,1,0:T(2,128)S(1)} collective-permute-done((f32[5,2,4096]{2,1,0:T(2,128)S(1)}, f32[5,2,4096]{2,1,0:T(2,128)S(1)}, u32[]{:S(2)}, u32[]{:S(2)}) %collective-permute-start.1) | collective-permute-done | bytes 163872 | tf_op jit(solution)/shard_map/ppermute | solution.py:557
  11.1 3.2 %collective-permute-start.3 = (f32[8,5,16,128]{3,2,1,0:T(8,128)S(1)}, f32[8,5,16,128]{3,2,1,0:T(8,128)S(1)}, u32[]{:S(2)}, u32[]{:S(2)}) collective-permute-start(f32[8,5,16,128]{3,2,1,0:T(8,128)S(1)} %get-tuple-element.82.faces), channel_id=1, source_target_pairs={{0,1},{2,3},{4,5},{6,7},{1,0},{3,2},{5,4},{7,6},{8,9},{10,11},{12,... | collective-permute-start | bytes 983048 | tf_op jit(solution)/shard_map/ppermute | solution.py:552
  14.3 1.5 %collective-permute-start.5 = (f32[5,2,3072]{2,1,0:T(2,128)S(1)}, f32[5,2,3072]{2,1,0:T(2,128)S(1)}, u32[]{:S(2)}, u32[]{:S(2)}) collective-permute-start(f32[5,2,3072]{2,1,0:T(2,128)S(1)} %get-tuple-element.87), channel_id=1, source_target_pairs={{0,8},{8,16},{16,24},{24,0},{1,9},{9,17},{17,25},{25,1},{2,10},{10... | collective-permute-start | bytes 368648 | tf_op jit(solution)/shard_map/ppermute | solution.py:557
  15.8 1.5 %own_part.8.part = f32[5,16,2048]{2,1,0:T(8,128)S(1)} custom-call(s32[6,16]{1,0:T(8,128)S(4)} %get-tuple-element.68.table, f32[5,16,2048]{2,1,0:T(8,128)S(1)} %get-tuple-element.81.field, f32[5,16,2048]{2,1,0:T(8,128)S(1)} %get-tuple-element.71.goal, f32[5,5,6,2048]{3,2,1,0:T(8,128)S(1)} %get-tuple-element.72.jacobian, ...), custom_call_target="tpu_custom_call" | custom-call | flops 1 | bytes 1 | tf_op jit(solution)/shard_map/own_part/pallas_call | solution.py:35
  19.0 1.5 %collective-permute-done.5.tail = f32[5,2,3072]{2,1,0:T(2,128)S(1)} collective-permute-done((f32[5,2,3072]{2,1,0:T(2,128)S(1)}, f32[5,2,3072]{2,1,0:T(2,128)S(1)}, u32[]{:S(2)}, u32[]{:S(2)}) %collective-permute-start.5) | collective-permute-done | bytes 122912 | tf_op jit(solution)/shard_map/ppermute | solution.py:557
  20.9 1.5 %collective-permute-start.6 = (f32[8,5,4,128]{3,2,1,0:T(4,128)S(1)}, f32[8,5,4,128]{3,2,1,0:T(4,128)S(1)}, u32[]{:S(2)}, u32[]{:S(2)}) collective-permute-start(f32[8,5,4,128]{3,2,1,0:T(4,128)S(1)} %get-tuple-element.90.faces), channel_id=1, source_target_pairs={{0,1},{2,3},{4,5},{6,7},{1,0},{3,2},{5,4},{7,6},{8,9},{10,11},{12,... | collective-permute-start | bytes 245768 | tf_op jit(solution)/shard_map/ppermute | solution.py:552
  22.4 2.3 %collective-permute-start.8 = (f32[5,2,3072]{2,1,0:T(2,128)S(1)}, f32[5,2,3072]{2,1,0:T(2,128)S(1)}, u32[]{:S(2)}, u32[]{:S(2)}) collective-permute-start(f32[5,2,3072]{2,1,0:T(2,128)S(1)} %get-tuple-element.96), channel_id=1, source_target_pairs={{0,8},{8,16},{16,24},{24,0},{1,9},{9,17},{17,25},{25,1},{2,10},{10... | collective-permute-start | bytes 368648 | tf_op jit(solution)/shard_map/ppermute | solution.py:557
  24.7 1.1 %own_part_of_means.1.part = f32[5,4,2048]{2,1,0:T(4,128)S(1)} custom-call(s32[6,16]{1,0:T(8,128)S(4)} %get-tuple-element.68.table, f32[5,16,2048]{2,1,0:T(8,128)S(1)} %get-tuple-element.88.field.fine, f32[5,16,2048]{2,1,0:T(8,128)S(1)} %get-tuple-element.71.goal, f32[5,4,2048]{2,1,0:T(4,128)S(1)} %get-tuple-element.89.means, ...), custom_call_target="tpu_custom_call" | custom-call | flops 1 | bytes 1 | tf_op jit(solution)/shard_map/own_part_of_means/pallas_call | solution.py:35
  27.0 0.8 %collective-permute-start.11 = (f32[5,2,3072]{2,1,0:T(2,128)S(1)}, f32[5,2,3072]{2,1,0:T(2,128)S(1)}, u32[]{:S(2)}, u32[]{:S(2)}) collective-permute-start(f32[5,2,3072]{2,1,0:T(2,128)S(1)} %get-tuple-element.103), channel_id=1, source_target_pairs={{0,8},{8,16},{16,24},{24,0},{1,9},{9,17},{17,25},{25,1},{2,10},{10... | collective-permute-start | bytes 368648 | tf_op jit(solution)/shard_map/ppermute | solution.py:557
  27.9 0.7 %collective-permute-done.8.tail = f32[5,2,3072]{2,1,0:T(2,128)S(1)} collective-permute-done((f32[5,2,3072]{2,1,0:T(2,128)S(1)}, f32[5,2,3072]{2,1,0:T(2,128)S(1)}, u32[]{:S(2)}, u32[]{:S(2)}) %collective-permute-start.8) | collective-permute-done | bytes 122912 | tf_op jit(solution)/shard_map/ppermute | solution.py:557
  28.9 2.1 %collective-permute-start.9 = (f32[8,5,4,128]{3,2,1,0:T(4,128)S(1)}, f32[8,5,4,128]{3,2,1,0:T(4,128)S(1)}, u32[]{:S(2)}, u32[]{:S(2)}) collective-permute-start(f32[8,5,4,128]{3,2,1,0:T(4,128)S(1)} %get-tuple-element.99.faces), channel_id=1, source_target_pairs={{0,1},{2,3},{4,5},{6,7},{1,0},{3,2},{5,4},{7,6},{8,9},{10,11},{12,... | collective-permute-start | bytes 245768 | tf_op jit(solution)/shard_map/ppermute | solution.py:552
  30.9 0.8 %own_part.9.part = f32[5,4,2048]{2,1,0:T(4,128)S(1)} custom-call(s32[6,16]{1,0:T(8,128)S(4)} %get-tuple-element.68.table, f32[5,4,2048]{2,1,0:T(4,128)S(1)} %get-tuple-element.97.field, f32[5,4,2048]{2,1,0:T(4,128)S(1)} %get-tuple-element.98.goal, f32[5,5,6,2048]{3,2,1,0:T(8,128)S(1)} %get-tuple-element.72.jacobian, ...), custom_call_target="tpu_custom_call" | custom-call | flops 1 | bytes 1 | tf_op jit(solution)/shard_map/own_part/pallas_call | solution.py:35
  33.3 3.0 %collective-permute-start.12 = (f32[8,5,4,128]{3,2,1,0:T(4,128)S(1)}, f32[8,5,4,128]{3,2,1,0:T(4,128)S(1)}, u32[]{:S(2)}, u32[]{:S(2)}) collective-permute-start(f32[8,5,4,128]{3,2,1,0:T(4,128)S(1)} %get-tuple-element.105.faces), channel_id=1, source_target_pairs={{0,1},{2,3},{4,5},{6,7},{1,0},{3,2},{5,4},{7,6},{8,9},{10,11},{12,... | collective-permute-start | bytes 245768 | tf_op jit(solution)/shard_map/ppermute | solution.py:552
  36.6 0.8 %own_part.10.part = f32[5,4,2048]{2,1,0:T(4,128)S(1)} custom-call(s32[6,16]{1,0:T(8,128)S(4)} %get-tuple-element.68.table, f32[5,4,2048]{2,1,0:T(4,128)S(1)} %get-tuple-element.104.field, f32[5,4,2048]{2,1,0:T(4,128)S(1)} %get-tuple-element.98.goal, f32[5,5,6,2048]{3,2,1,0:T(8,128)S(1)} %get-tuple-element.72.jacobian, ...), custom_call_target="tpu_custom_call" | custom-call | flops 1 | bytes 1 | tf_op jit(solution)/shard_map/own_part/pallas_call | solution.py:35
  38.6 1.7 %collective-permute-start.17 = (f32[5,2,3072]{2,1,0:T(2,128)S(1)}, f32[5,2,3072]{2,1,0:T(2,128)S(1)}, u32[]{:S(2)}, u32[]{:S(2)}) collective-permute-start(f32[5,2,3072]{2,1,0:T(2,128)S(1)} %get-tuple-element.115), channel_id=1, source_target_pairs={{0,8},{8,16},{16,24},{24,0},{1,9},{9,17},{17,25},{25,1},{2,10},{10... | collective-permute-start | bytes 368648 | tf_op jit(solution)/shard_map/ppermute | solution.py:557
  40.3 2.1 %collective-permute-done.14.tail = f32[5,2,3072]{2,1,0:T(2,128)S(1)} collective-permute-done((f32[5,2,3072]{2,1,0:T(2,128)S(1)}, f32[5,2,3072]{2,1,0:T(2,128)S(1)}, u32[]{:S(2)}, u32[]{:S(2)}) %collective-permute-start.14) | collective-permute-done | bytes 122912 | tf_op jit(solution)/shard_map/ppermute | solution.py:557
  42.8 0.8 %own_part.11.part = f32[5,4,2048]{2,1,0:T(4,128)S(1)} custom-call(s32[6,16]{1,0:T(8,128)S(4)} %get-tuple-element.68.table, f32[5,4,2048]{2,1,0:T(4,128)S(1)} %get-tuple-element.110.field, f32[5,4,2048]{2,1,0:T(4,128)S(1)} %get-tuple-element.98.goal, f32[5,5,6,2048]{3,2,1,0:T(8,128)S(1)} %get-tuple-element.72.jacobian, ...), custom_call_target="tpu_custom_call" | custom-call | flops 1 | bytes 1 | tf_op jit(solution)/shard_map/own_part/pallas_call | solution.py:35
  45.7 2.7 %collective-permute-start.18 = (f32[8,5,16,128]{3,2,1,0:T(8,128)S(1)}, f32[8,5,16,128]{3,2,1,0:T(8,128)S(1)}, u32[]{:S(2)}, u32[]{:S(2)}) collective-permute-start(f32[8,5,16,128]{3,2,1,0:T(8,128)S(1)} %get-tuple-element.117.faces), channel_id=1, source_target_pairs={{0,1},{2,3},{4,5},{6,7},{1,0},{3,2},{5,4},{7,6},{8,9},{10,11},{12,... | collective-permute-start | bytes 983048 | tf_op jit(solution)/shard_map/ppermute | solution.py:552
  48.9 1.5 %own_part.12.part = f32[5,16,2048]{2,1,0:T(8,128)S(1)} custom-call(s32[6,16]{1,0:T(8,128)S(4)} %get-tuple-element.68.table, f32[5,16,2048]{2,1,0:T(8,128)S(1)} %get-tuple-element.116.field, f32[5,16,2048]{2,1,0:T(8,128)S(1)} %get-tuple-element.71.goal, f32[5,5,6,2048]{3,2,1,0:T(8,128)S(1)} %get-tuple-element.72.jacobian, ...), custom_call_target="tpu_custom_call" | custom-call | flops 1 | bytes 1 | tf_op jit(solution)/shard_map/own_part/pallas_call | solution.py:35
  50.7 0.7 collective-permute-start.22
  51.9 2.9 %collective-permute-done.20.tail = f32[5,2,3072]{2,1,0:T(2,128)S(1)} collective-permute-done((f32[5,2,3072]{2,1,0:T(2,128)S(1)}, f32[5,2,3072]{2,1,0:T(2,128)S(1)}, u32[]{:S(2)}, u32[]{:S(2)}) %collective-permute-start.20) | collective-permute-done | bytes 122912 | tf_op jit(solution)/shard_map/ppermute | solution.py:557
  55.3 1.3 %collective-permute-start.23 = (f32[5,2,3072]{2,1,0:T(2,128)S(1)}, f32[5,2,3072]{2,1,0:T(2,128)S(1)}, u32[]{:S(2)}, u32[]{:S(2)}) collective-permute-start(f32[5,2,3072]{2,1,0:T(2,128)S(1)} %get-tuple-element.127), channel_id=1, source_target_pairs={{0,8},{8,16},{16,24},{24,0},{1,9},{9,17},{17,25},{25,1},{2,10},{10... | collective-permute-start | bytes 368648 | tf_op jit(solution)/shard_map/ppermute | solution.py:557
  56.6 1.5 %own_part.13.part = f32[5,16,2048]{2,1,0:T(8,128)S(1)} custom-call(s32[6,16]{1,0:T(8,128)S(4)} %get-tuple-element.68.table, f32[5,16,2048]{2,1,0:T(8,128)S(1)} %get-tuple-element.122.field, f32[5,16,2048]{2,1,0:T(8,128)S(1)} %get-tuple-element.71.goal, f32[5,5,6,2048]{3,2,1,0:T(8,128)S(1)} %get-tuple-element.72.jacobian, ...), custom_call_target="tpu_custom_call" | custom-call | flops 1 | bytes 1 | tf_op jit(solution)/shard_map/own_part/pallas_call | solution.py:35
  59.6 2.1 %collective-permute-done.23.tail = f32[5,2,3072]{2,1,0:T(2,128)S(1)} collective-permute-done((f32[5,2,3072]{2,1,0:T(2,128)S(1)}, f32[5,2,3072]{2,1,0:T(2,128)S(1)}, u32[]{:S(2)}, u32[]{:S(2)}) %collective-permute-start.23) | collective-permute-done | bytes 122912 | tf_op jit(solution)/shard_map/ppermute | solution.py:557
  62.4 1.0 %collective-permute-start.26 = (f32[5,2,3072]{2,1,0:T(2,128)S(1)}, f32[5,2,3072]{2,1,0:T(2,128)S(1)}, u32[]{:S(2)}, u32[]{:S(2)}) collective-permute-start(f32[5,2,3072]{2,1,0:T(2,128)S(1)} %get-tuple-element.133), channel_id=1, source_target_pairs={{0,8},{8,16},{16,24},{24,0},{1,9},{9,17},{17,25},{25,1},{2,10},{10... | collective-permute-start | bytes 368648 | tf_op jit(solution)/shard_map/ppermute | solution.py:557
  63.4 1.5 %last_own_part.1 = (f32[5,16,2048]{2,1,0:T(8,128)S(1)}, f32[5,16,2048]{2,1,0:T(8,128)}) custom-call(s32[6,16]{1,0:T(8,128)S(4)} %get-tuple-element.68.table, f32[5,16,2048]{2,1,0:T(8,128)S(1)} %get-tuple-element.128.field, f32[5,16,2048]{2,1,0:T(8,128)S(1)} %get-tuple-element.71.goal, f32[5,5,6,2048]{3,2,1,0:T(8,128)S(1)} %get-tuple-element.72.jacobian, ...), custom_call_target="tpu_custom_call" | custom-call | flops 1 | bytes 1 | tf_op jit(solution)/shard_map/last_own_part/pallas_call | solution.py:35
  65.1 3.6 %collective-permute-done.26.tail = f32[5,2,3072]{2,1,0:T(2,128)S(1)} collective-permute-done((f32[5,2,3072]{2,1,0:T(2,128)S(1)}, f32[5,2,3072]{2,1,0:T(2,128)S(1)}, u32[]{:S(2)}, u32[]{:S(2)}) %collective-permute-start.26) | collective-permute-done | bytes 122912 | tf_op jit(solution)/shard_map/ppermute | solution.py:557
  68.9 1.1 %residual.1 = f32[5,16,2048]{2,1,0:T(8,128)} custom-call(s32[6,16]{1,0:T(8,128)S(4)} %get-tuple-element.68.table, f32[5,16,2048]{2,1,0:T(8,128)S(1)} %beside_part.1.part, f32[8,5,16,128]{3,2,1,0:T(8,128)S(1)} %rim.5, f32[5,2,3072]{2,1,0:T(2,128)S(1)} %collective-permute-done.26.tail, f32[2,5,5,2048]{3,2,1,0:T(8,128)S(1)} %get-tuple-element.76.rim_jacobian), custom_call_target="tpu_custom_call" | custom-call | flops 1 | bytes 1 | tf_op jit(solution)/shard_map/residual/pallas_call | solution.py:35
  (69 shorter events, 15.4 us)
Async XLA Ops:
  2.6 5.4 %collective-permute-start = (f32[8,5,16,128]{3,2,1,0:T(8,128)S(1)}, f32[8,5,16,128]{3,2,1,0:T(8,128)S(1)}, u32[]{:S(2)}, u32[]{:S(2)}) collective-permute-start(f32[8,5,16,128]{3,2,1,0:T(8,128)S(1)} %get-tuple-element.75.faces), channel_id=1, source_target_pairs={{0,1},{2,3},{4,5},{6,7},{1,0},{3,2},{5,4},{7,6},{8,9},{10,11},{12,... | collective-permute-start | bytes 983048 | tf_op jit(solution)/shard_map/ppermute | solution.py:552
  3.1 7.5 %collective-permute-start.2 = (f32[8,5,16,128]{3,2,1,0:T(8,128)S(1)}, f32[8,5,16,128]{3,2,1,0:T(8,128)S(1)}, u32[]{:S(2)}, u32[]{:S(2)}) collective-permute-start(f32[8,5,16,128]{3,2,1,0:T(8,128)S(1)} %get-tuple-element.75.faces), channel_id=1, source_target_pairs={{1,2},{3,4},{5,6},{2,1},{4,3},{6,5},{9,10},{11,12},{13,14},{10,9},... | collective-permute-start | bytes 983048 | tf_op jit(solution)/shard_map/ppermute | solution.py:548
  3.8 6.8 %collective-permute-start.1 = (f32[5,2,4096]{2,1,0:T(2,128)S(1)}, f32[5,2,4096]{2,1,0:T(2,128)S(1)}, u32[]{:S(2)}, u32[]{:S(2)}) collective-permute-start(f32[5,2,4096]{2,1,0:T(2,128)S(1)} %tail.1), channel_id=1, source_target_pairs={{0,8},{8,16},{16,24},{24,0},{1,9},{9,17},{17,25},{25,1},{2,10},{10... | collective-permute-start | bytes 491528 | tf_op jit(solution)/shard_map/ppermute | solution.py:557
  8.4 10.0 %collective-permute-start.4 = (f32[8,120,128]{2,1,0:T(8,128)S(1)}, f32[8,120,128]{2,1,0:T(8,128)S(1)}, u32[]{:S(2)}, u32[]{:S(2)}) collective-permute-start(f32[8,120,128]{2,1,0:T(8,128)S(1)} %get-tuple-element.84), channel_id=1, source_target_pairs={{1,2},{3,4},{5,6},{2,1},{4,3},{6,5},{9,10},{11,12},{13,14},{10,9},... | collective-permute-start | bytes 1474568 | tf_op jit(solution)/shard_map/ppermute | solution.py:548
  11.1 6.2 %collective-permute-start.3 = (f32[8,5,16,128]{3,2,1,0:T(8,128)S(1)}, f32[8,5,16,128]{3,2,1,0:T(8,128)S(1)}, u32[]{:S(2)}, u32[]{:S(2)}) collective-permute-start(f32[8,5,16,128]{3,2,1,0:T(8,128)S(1)} %get-tuple-element.82.faces), channel_id=1, source_target_pairs={{0,1},{2,3},{4,5},{6,7},{1,0},{3,2},{5,4},{7,6},{8,9},{10,11},{12,... | collective-permute-start | bytes 983048 | tf_op jit(solution)/shard_map/ppermute | solution.py:552
  14.3 6.2 %collective-permute-start.5 = (f32[5,2,3072]{2,1,0:T(2,128)S(1)}, f32[5,2,3072]{2,1,0:T(2,128)S(1)}, u32[]{:S(2)}, u32[]{:S(2)}) collective-permute-start(f32[5,2,3072]{2,1,0:T(2,128)S(1)} %get-tuple-element.87), channel_id=1, source_target_pairs={{0,8},{8,16},{16,24},{24,0},{1,9},{9,17},{17,25},{25,1},{2,10},{10... | collective-permute-start | bytes 368648 | tf_op jit(solution)/shard_map/ppermute | solution.py:557
  17.7 8.9 %collective-permute-start.7 = (f32[8,5,6,128]{3,2,1,0:T(8,128)S(1)}, f32[8,5,6,128]{3,2,1,0:T(8,128)S(1)}, u32[]{:S(2)}, u32[]{:S(2)}) collective-permute-start(f32[8,5,6,128]{3,2,1,0:T(8,128)S(1)} %get-tuple-element.85.next_message), channel_id=1, source_target_pairs={{1,2},{3,4},{5,6},{2,1},{4,3},{6,5},{9,10},{11,12},{13,14},{10,9},... | collective-permute-start | bytes 368648 | tf_op jit(solution)/shard_map/ppermute | solution.py:548
  20.9 4.8 %collective-permute-start.6 = (f32[8,5,4,128]{3,2,1,0:T(4,128)S(1)}, f32[8,5,4,128]{3,2,1,0:T(4,128)S(1)}, u32[]{:S(2)}, u32[]{:S(2)}) collective-permute-start(f32[8,5,4,128]{3,2,1,0:T(4,128)S(1)} %get-tuple-element.90.faces), channel_id=1, source_target_pairs={{0,1},{2,3},{4,5},{6,7},{1,0},{3,2},{5,4},{7,6},{8,9},{10,11},{12,... | collective-permute-start | bytes 245768 | tf_op jit(solution)/shard_map/ppermute | solution.py:552
  22.4 6.2 %collective-permute-start.8 = (f32[5,2,3072]{2,1,0:T(2,128)S(1)}, f32[5,2,3072]{2,1,0:T(2,128)S(1)}, u32[]{:S(2)}, u32[]{:S(2)}) collective-permute-start(f32[5,2,3072]{2,1,0:T(2,128)S(1)} %get-tuple-element.96), channel_id=1, source_target_pairs={{0,8},{8,16},{16,24},{24,0},{1,9},{9,17},{17,25},{25,1},{2,10},{10... | collective-permute-start | bytes 368648 | tf_op jit(solution)/shard_map/ppermute | solution.py:557
  25.9 6.8 %collective-permute-start.10 = (f32[16,5,4,128]{3,2,1,0:T(4,128)S(1)}, f32[16,5,4,128]{3,2,1,0:T(4,128)S(1)}, u32[]{:S(2)}, u32[]{:S(2)}) collective-permute-start(f32[16,5,4,128]{3,2,1,0:T(4,128)S(1)} %get-tuple-element.101), channel_id=1, source_target_pairs={{1,2},{3,4},{5,6},{2,1},{4,3},{6,5},{9,10},{11,12},{13,14},{10,9},... | collective-permute-start | bytes 491528 | tf_op jit(solution)/shard_map/ppermute | solution.py:548
  27.0 6.0 %collective-permute-start.11 = (f32[5,2,3072]{2,1,0:T(2,128)S(1)}, f32[5,2,3072]{2,1,0:T(2,128)S(1)}, u32[]{:S(2)}, u32[]{:S(2)}) collective-permute-start(f32[5,2,3072]{2,1,0:T(2,128)S(1)} %get-tuple-element.103), channel_id=1, source_target_pairs={{0,8},{8,16},{16,24},{24,0},{1,9},{9,17},{17,25},{25,1},{2,10},{10... | collective-permute-start | bytes 368648 | tf_op jit(solution)/shard_map/ppermute | solution.py:557
  28.9 3.0 %collective-permute-start.9 = (f32[8,5,4,128]{3,2,1,0:T(4,128)S(1)}, f32[8,5,4,128]{3,2,1,0:T(4,128)S(1)}, u32[]{:S(2)}, u32[]{:S(2)}) collective-permute-start(f32[8,5,4,128]{3,2,1,0:T(4,128)S(1)} %get-tuple-element.99.faces), channel_id=1, source_target_pairs={{0,1},{2,3},{4,5},{6,7},{1,0},{3,2},{5,4},{7,6},{8,9},{10,11},{12,... | collective-permute-start | bytes 245768 | tf_op jit(solution)/shard_map/ppermute | solution.py:552
  32.1 6.2 %collective-permute-start.13 = (f32[16,5,4,128]{3,2,1,0:T(4,128)S(1)}, f32[16,5,4,128]{3,2,1,0:T(4,128)S(1)}, u32[]{:S(2)}, u32[]{:S(2)}) collective-permute-start(f32[16,5,4,128]{3,2,1,0:T(4,128)S(1)} %get-tuple-element.107), channel_id=1, source_target_pairs={{1,2},{3,4},{5,6},{2,1},{4,3},{6,5},{9,10},{11,12},{13,14},{10,9},... | collective-permute-start | bytes 491528 | tf_op jit(solution)/shard_map/ppermute | solution.py:548
  33.3 4.1 %collective-permute-start.12 = (f32[8,5,4,128]{3,2,1,0:T(4,128)S(1)}, f32[8,5,4,128]{3,2,1,0:T(4,128)S(1)}, u32[]{:S(2)}, u32[]{:S(2)}) collective-permute-start(f32[8,5,4,128]{3,2,1,0:T(4,128)S(1)} %get-tuple-element.105.faces), channel_id=1, source_target_pairs={{0,1},{2,3},{4,5},{6,7},{1,0},{3,2},{5,4},{7,6},{8,9},{10,11},{12,... | collective-permute-start | bytes 245768 | tf_op jit(solution)/shard_map/ppermute | solution.py:552
  36.3 6.2 %collective-permute-start.14 = (f32[5,2,3072]{2,1,0:T(2,128)S(1)}, f32[5,2,3072]{2,1,0:T(2,128)S(1)}, u32[]{:S(2)}, u32[]{:S(2)}) collective-permute-start(f32[5,2,3072]{2,1,0:T(2,128)S(1)} %get-tuple-element.109), channel_id=1, source_target_pairs={{0,8},{8,16},{16,24},{24,0},{1,9},{9,17},{17,25},{25,1},{2,10},{10... | collective-permute-start | bytes 368648 | tf_op jit(solution)/shard_map/ppermute | solution.py:557
  37.6 7.4 %collective-permute-start.16 = (f32[16,5,4,128]{3,2,1,0:T(4,128)S(1)}, f32[16,5,4,128]{3,2,1,0:T(4,128)S(1)}, u32[]{:S(2)}, u32[]{:S(2)}) collective-permute-start(f32[16,5,4,128]{3,2,1,0:T(4,128)S(1)} %get-tuple-element.113), channel_id=1, source_target_pairs={{1,2},{3,4},{5,6},{2,1},{4,3},{6,5},{9,10},{11,12},{13,14},{10,9},... | collective-permute-start | bytes 491528 | tf_op jit(solution)/shard_map/ppermute | solution.py:548
  38.6 6.9 %collective-permute-start.17 = (f32[5,2,3072]{2,1,0:T(2,128)S(1)}, f32[5,2,3072]{2,1,0:T(2,128)S(1)}, u32[]{:S(2)}, u32[]{:S(2)}) collective-permute-start(f32[5,2,3072]{2,1,0:T(2,128)S(1)} %get-tuple-element.115), channel_id=1, source_target_pairs={{0,8},{8,16},{16,24},{24,0},{1,9},{9,17},{17,25},{25,1},{2,10},{10... | collective-permute-start | bytes 368648 | tf_op jit(solution)/shard_map/ppermute | solution.py:557
  42.7 1.3 %collective-permute-start.15 = (f32[8,5,4,128]{3,2,1,0:T(4,128)S(1)}, f32[8,5,4,128]{3,2,1,0:T(4,128)S(1)}, u32[]{:S(2)}, u32[]{:S(2)}) collective-permute-start(f32[8,5,4,128]{3,2,1,0:T(4,128)S(1)} %get-tuple-element.111.faces), channel_id=1, source_target_pairs={{0,1},{2,3},{4,5},{6,7},{1,0},{3,2},{5,4},{7,6},{8,9},{10,11},{12,... | collective-permute-start | bytes 245768 | tf_op jit(solution)/shard_map/ppermute | solution.py:552
  44.3 7.1 %collective-permute-start.19 = (f32[9,5,16,128]{3,2,1,0:T(8,128)S(1)}, f32[9,5,16,128]{3,2,1,0:T(8,128)S(1)}, u32[]{:S(2)}, u32[]{:S(2)}) collective-permute-start(f32[9,5,16,128]{3,2,1,0:T(8,128)S(1)} %get-tuple-element.119), channel_id=1, source_target_pairs={{1,2},{3,4},{5,6},{2,1},{4,3},{6,5},{9,10},{11,12},{13,14},{10,9},... | collective-permute-start | bytes 1105928 | tf_op jit(solution)/shard_map/ppermute | solution.py:548
  45.7 4.6 %collective-permute-start.18 = (f32[8,5,16,128]{3,2,1,0:T(8,128)S(1)}, f32[8,5,16,128]{3,2,1,0:T(8,128)S(1)}, u32[]{:S(2)}, u32[]{:S(2)}) collective-permute-start(f32[8,5,16,128]{3,2,1,0:T(8,128)S(1)} %get-tuple-element.117.faces), channel_id=1, source_target_pairs={{0,1},{2,3},{4,5},{6,7},{1,0},{3,2},{5,4},{7,6},{8,9},{10,11},{12,... | collective-permute-start | bytes 983048 | tf_op jit(solution)/shard_map/ppermute | solution.py:552
  48.4 6.4 %collective-permute-start.20 = (f32[5,2,3072]{2,1,0:T(2,128)S(1)}, f32[5,2,3072]{2,1,0:T(2,128)S(1)}, u32[]{:S(2)}, u32[]{:S(2)}) collective-permute-start(f32[5,2,3072]{2,1,0:T(2,128)S(1)} %get-tuple-element.121), channel_id=1, source_target_pairs={{0,8},{8,16},{16,24},{24,0},{1,9},{9,17},{17,25},{25,1},{2,10},{10... | collective-permute-start | bytes 368648 | tf_op jit(solution)/shard_map/ppermute | solution.py:557
  50.7 8.5 %collective-permute-start.22 = (f32[9,5,16,128]{3,2,1,0:T(8,128)S(1)}, f32[9,5,16,128]{3,2,1,0:T(8,128)S(1)}, u32[]{:S(2)}, u32[]{:S(2)}) collective-permute-start(f32[9,5,16,128]{3,2,1,0:T(8,128)S(1)} %get-tuple-element.125), channel_id=1, source_target_pairs={{1,2},{3,4},{5,6},{2,1},{4,3},{6,5},{9,10},{11,12},{13,14},{10,9},... | collective-permute-start | bytes 1105928 | tf_op jit(solution)/shard_map/ppermute | solution.py:548
  55.0 3.0 %collective-permute-start.21 = (f32[8,5,16,128]{3,2,1,0:T(8,128)S(1)}, f32[8,5,16,128]{3,2,1,0:T(8,128)S(1)}, u32[]{:S(2)}, u32[]{:S(2)}) collective-permute-start(f32[8,5,16,128]{3,2,1,0:T(8,128)S(1)} %get-tuple-element.123.faces), channel_id=1, source_target_pairs={{0,1},{2,3},{4,5},{6,7},{1,0},{3,2},{5,4},{7,6},{8,9},{10,11},{12,... | collective-permute-start | bytes 983048 | tf_op jit(solution)/shard_map/ppermute | solution.py:552
  55.3 6.5 %collective-permute-start.23 = (f32[5,2,3072]{2,1,0:T(2,128)S(1)}, f32[5,2,3072]{2,1,0:T(2,128)S(1)}, u32[]{:S(2)}, u32[]{:S(2)}) collective-permute-start(f32[5,2,3072]{2,1,0:T(2,128)S(1)} %get-tuple-element.127), channel_id=1, source_target_pairs={{0,8},{8,16},{16,24},{24,0},{1,9},{9,17},{17,25},{25,1},{2,10},{10... | collective-permute-start | bytes 368648 | tf_op jit(solution)/shard_map/ppermute | solution.py:557
  58.4 10.2 %collective-permute-start.25 = (f32[9,5,16,128]{3,2,1,0:T(8,128)S(1)}, f32[9,5,16,128]{3,2,1,0:T(8,128)S(1)}, u32[]{:S(2)}, u32[]{:S(2)}) collective-permute-start(f32[9,5,16,128]{3,2,1,0:T(8,128)S(1)} %get-tuple-element.132), channel_id=1, source_target_pairs={{1,2},{3,4},{5,6},{2,1},{4,3},{6,5},{9,10},{11,12},{13,14},{10,9},... | collective-permute-start | bytes 1105928 | tf_op jit(solution)/shard_map/ppermute | solution.py:548
  62.0 2.9 %collective-permute-start.24 = (f32[8,5,16,128]{3,2,1,0:T(8,128)S(1)}, f32[8,5,16,128]{3,2,1,0:T(8,128)S(1)}, u32[]{:S(2)}, u32[]{:S(2)}) collective-permute-start(f32[8,5,16,128]{3,2,1,0:T(8,128)S(1)} %get-tuple-element.131), channel_id=1, source_target_pairs={{0,1},{2,3},{4,5},{6,7},{1,0},{3,2},{5,4},{7,6},{8,9},{10,11},{12,... | collective-permute-start | bytes 983048 | tf_op jit(solution)/shard_map/ppermute | solution.py:552
  62.4 6.3 %collective-permute-start.26 = (f32[5,2,3072]{2,1,0:T(2,128)S(1)}, f32[5,2,3072]{2,1,0:T(2,128)S(1)}, u32[]{:S(2)}, u32[]{:S(2)}) collective-permute-start(f32[5,2,3072]{2,1,0:T(2,128)S(1)} %get-tuple-element.133), channel_id=1, source_target_pairs={{0,8},{8,16},{16,24},{24,0},{1,9},{9,17},{17,25},{25,1},{2,10},{10... | collective-permute-start | bytes 368648 | tf_op jit(solution)/shard_map/ppermute | solution.py:557

commit v5 on v4

--- a/solution.py
+++ b/solution.py
@@ -215,9 +215,12 @@
         lanes = lanes_of(b)
         total = []
         for a in range(NV):
-            v = field[a, :, lanes]
-            fine = goal[a, :, lanes] - weight * (3.0 * v - 4.0 * earlier(v, 1) + earlier(v, 2))
-            total.append(mean_rows(fine, scratch.at[u, a], steps) - cell_diag[pl.ds(a, 1), lanes] * means[a, :, lanes])
+            held = scratch.at[u + OWN_UNROLL, a]
+            held[...] = field[a, :, lanes]
+            before, last = (held[pl.ds(i, steps, stride=GROUP), :] for i in (GROUP - 2, GROUP - 1))
+            timed = 3.0 * (last - earlier(last, 1)) - (before - earlier(before, 1))
+            fixed = mean_rows(goal[a, :, lanes], scratch.at[u, a], steps) - (weight / GROUP) * timed
+            total.append(fixed - cell_diag[pl.ds(a, 1), lanes] * means[a, :, lanes])
         total = own_part(total, b, means, table, jacobian, self_block)
         for a in range(NV):
             out[a, :, lanes] = total[a]

time: 70.5 us -> 70.5 us (level)
  no operation moved by 1% of the time
where the time goes in v5:
time: 70.5 us; the launch traced here: 70.1 us
  starting transfers between devices  31.8 us (45%)
  Pallas kernels  22 us (31%)
  waiting for transfers between devices  15 us (21%)
  between operations  1.26 us (2%)
    pallas_call x45, Pallas kernels, call(): pl.pallas_call(kernel, out_shape=[o if out_specs and out_specs[i] is IN_H...  19.9 us
    ppermute x9, waiting for transfers between devices, to_later(): lax.ppermute(tail, 'tm', [(i, (i + 1) % periods) for i in range(periods)])  14.5 us
    ppermute x9, starting transfers between devices, on_chip(): return lax.ppermute(faces, 'space', neighbour_pairs(0))  13.7 us
    ppermute x9, starting transfers between devices, to_later(): lax.ppermute(tail, 'tm', [(i, (i + 1) % periods) for i in range(periods)])  12 us
    ppermute x9, starting transfers between devices, over_chips(): return lax.ppermute(message, 'space', neighbour_pairs(1))  6.1 us
    pallas_call x1, Pallas kernels, body(): pl.pallas_call(first_kernel, out_shape=[pltpu.SMEM(x.shape, jnp.int32) fo...  1.96 us
  transfers between devices with their start and end apart: 27, of which 9 were waited for; matrix products, arithmetic and copies ran while one was open for 0% of the time, Pallas kernels for 27%

profile of v5, /device:TPU:0, one launch (start us, length us, event | category | flops | bytes accessed | tf_op | source)
XLA Modules:
  0.0 70.1 jit_solution(18019444087856434442)
XLA Ops:
  0.6 2.0 %arguments.1 = (s32[6,16]{1,0:T(8,128)S(4)}, s32[8]{0:T(128)S(4)}, f32[5,16,2048]{2,1,0:T(8,128)S(1)}, f32[5,2048]{1,0:T(8,128)S(1)}, f32[5,5,6,2048]{3,2,1,0:T(...) custom-call(s32[6,16]{1,0:T(8,128)} %bitcast.10, s32[8]{0:T(128)} %refs_1_.1, ...), custom_call_target="tpu_custom_call" | custom-call | flops 1 | bytes 1 | tf_op jit(solution)/shard_map/arguments/pallas_call | solution.py:580
  3.8 2.6 %collective-permute-start.1 = (f32[5,2,4096]{2,1,0:T(2,128)S(1)}, f32[5,2,4096]{2,1,0:T(2,128)S(1)}, u32[]{:S(2)}, u32[]{:S(2)}) collective-permute-start(f32[5,2,4096]{2,1,0:T(2,128)S(1)} %tail.1), channel_id=1, source_target_pairs={{0,8},{8,16},{16,24},{24,0},{1,9},{9,17},{17,25},{25,1},{2,10},{10... | collective-permute-start | bytes 491528 | tf_op jit(solution)/shard_map/ppermute | solution.py:560
  6.5 1.5 %own_part.7.part = f32[5,16,2048]{2,1,0:T(8,128)S(1)} custom-call(s32[6,16]{1,0:T(8,128)S(4)} %get-tuple-element.68.table, f32[5,16,2048]{2,1,0:T(8,128)S(1)} %get-tuple-element.70.field, f32[5,16,2048]{2,1,0:T(8,128)S(1)} %get-tuple-element.71.goal, f32[5,5,6,2048]{3,2,1,0:T(8,128)S(1)} %get-tuple-element.72.jacobian, ...), custom_call_target="tpu_custom_call" | custom-call | flops 1 | bytes 1 | tf_op jit(solution)/shard_map/own_part/pallas_call | solution.py:35
  8.4 0.7 collective-permute-start.4
  9.1 1.6 %collective-permute-done.1.tail = f32[5,2,4096]{2,1,0:T(2,128)S(1)} collective-permute-done((f32[5,2,4096]{2,1,0:T(2,128)S(1)}, f32[5,2,4096]{2,1,0:T(2,128)S(1)}, u32[]{:S(2)}, u32[]{:S(2)}) %collective-permute-start.1) | collective-permute-done | bytes 163872 | tf_op jit(solution)/shard_map/ppermute | solution.py:560
  11.1 3.2 %collective-permute-start.3 = (f32[8,5,16,128]{3,2,1,0:T(8,128)S(1)}, f32[8,5,16,128]{3,2,1,0:T(8,128)S(1)}, u32[]{:S(2)}, u32[]{:S(2)}) collective-permute-start(f32[8,5,16,128]{3,2,1,0:T(8,128)S(1)} %get-tuple-element.82.faces), channel_id=1, source_target_pairs={{0,1},{2,3},{4,5},{6,7},{1,0},{3,2},{5,4},{7,6},{8,9},{10,11},{12,... | collective-permute-start | bytes 983048 | tf_op jit(solution)/shard_map/ppermute | solution.py:555
  14.3 1.5 %collective-permute-start.5 = (f32[5,2,3072]{2,1,0:T(2,128)S(1)}, f32[5,2,3072]{2,1,0:T(2,128)S(1)}, u32[]{:S(2)}, u32[]{:S(2)}) collective-permute-start(f32[5,2,3072]{2,1,0:T(2,128)S(1)} %get-tuple-element.87), channel_id=1, source_target_pairs={{0,8},{8,16},{16,24},{24,0},{1,9},{9,17},{17,25},{25,1},{2,10},{10... | collective-permute-start | bytes 368648 | tf_op jit(solution)/shard_map/ppermute | solution.py:560
  15.8 1.5 %own_part.8.part = f32[5,16,2048]{2,1,0:T(8,128)S(1)} custom-call(s32[6,16]{1,0:T(8,128)S(4)} %get-tuple-element.68.table, f32[5,16,2048]{2,1,0:T(8,128)S(1)} %get-tuple-element.81.field, f32[5,16,2048]{2,1,0:T(8,128)S(1)} %get-tuple-element.71.goal, f32[5,5,6,2048]{3,2,1,0:T(8,128)S(1)} %get-tuple-element.72.jacobian, ...), custom_call_target="tpu_custom_call" | custom-call | flops 1 | bytes 1 | tf_op jit(solution)/shard_map/own_part/pallas_call | solution.py:35
  19.0 1.5 %collective-permute-done.5.tail = f32[5,2,3072]{2,1,0:T(2,128)S(1)} collective-permute-done((f32[5,2,3072]{2,1,0:T(2,128)S(1)}, f32[5,2,3072]{2,1,0:T(2,128)S(1)}, u32[]{:S(2)}, u32[]{:S(2)}) %collective-permute-start.5) | collective-permute-done | bytes 122912 | tf_op jit(solution)/shard_map/ppermute | solution.py:560
  20.9 1.5 %collective-permute-start.6 = (f32[8,5,4,128]{3,2,1,0:T(4,128)S(1)}, f32[8,5,4,128]{3,2,1,0:T(4,128)S(1)}, u32[]{:S(2)}, u32[]{:S(2)}) collective-permute-start(f32[8,5,4,128]{3,2,1,0:T(4,128)S(1)} %get-tuple-element.90.faces), channel_id=1, source_target_pairs={{0,1},{2,3},{4,5},{6,7},{1,0},{3,2},{5,4},{7,6},{8,9},{10,11},{12,... | collective-permute-start | bytes 245768 | tf_op jit(solution)/shard_map/ppermute | solution.py:555
  22.4 2.3 %collective-permute-start.8 = (f32[5,2,3072]{2,1,0:T(2,128)S(1)}, f32[5,2,3072]{2,1,0:T(2,128)S(1)}, u32[]{:S(2)}, u32[]{:S(2)}) collective-permute-start(f32[5,2,3072]{2,1,0:T(2,128)S(1)} %get-tuple-element.96), channel_id=1, source_target_pairs={{0,8},{8,16},{16,24},{24,0},{1,9},{9,17},{17,25},{25,1},{2,10},{10... | collective-permute-start | bytes 368648 | tf_op jit(solution)/shard_map/ppermute | solution.py:560
  24.7 1.1 %own_part_of_means.1.part = f32[5,4,2048]{2,1,0:T(4,128)S(1)} custom-call(s32[6,16]{1,0:T(8,128)S(4)} %get-tuple-element.68.table, f32[5,16,2048]{2,1,0:T(8,128)S(1)} %get-tuple-element.88.field.fine, f32[5,16,2048]{2,1,0:T(8,128)S(1)} %get-tuple-element.71.goal, f32[5,4,2048]{2,1,0:T(4,128)S(1)} %get-tuple-element.89.means, ...), custom_call_target="tpu_custom_call" | custom-call | flops 1 | bytes 1 | tf_op jit(solution)/shard_map/own_part_of_means/pallas_call | solution.py:35
  27.1 0.8 %collective-permute-start.11 = (f32[5,2,3072]{2,1,0:T(2,128)S(1)}, f32[5,2,3072]{2,1,0:T(2,128)S(1)}, u32[]{:S(2)}, u32[]{:S(2)}) collective-permute-start(f32[5,2,3072]{2,1,0:T(2,128)S(1)} %get-tuple-element.103), channel_id=1, source_target_pairs={{0,8},{8,16},{16,24},{24,0},{1,9},{9,17},{17,25},{25,1},{2,10},{10... | collective-permute-start | bytes 368648 | tf_op jit(solution)/shard_map/ppermute | solution.py:560
  27.9 0.7 %collective-permute-done.8.tail = f32[5,2,3072]{2,1,0:T(2,128)S(1)} collective-permute-done((f32[5,2,3072]{2,1,0:T(2,128)S(1)}, f32[5,2,3072]{2,1,0:T(2,128)S(1)}, u32[]{:S(2)}, u32[]{:S(2)}) %collective-permute-start.8) | collective-permute-done | bytes 122912 | tf_op jit(solution)/shard_map/ppermute | solution.py:560
  28.9 2.1 %collective-permute-start.9 = (f32[8,5,4,128]{3,2,1,0:T(4,128)S(1)}, f32[8,5,4,128]{3,2,1,0:T(4,128)S(1)}, u32[]{:S(2)}, u32[]{:S(2)}) collective-permute-start(f32[8,5,4,128]{3,2,1,0:T(4,128)S(1)} %get-tuple-element.99.faces), channel_id=1, source_target_pairs={{0,1},{2,3},{4,5},{6,7},{1,0},{3,2},{5,4},{7,6},{8,9},{10,11},{12,... | collective-permute-start | bytes 245768 | tf_op jit(solution)/shard_map/ppermute | solution.py:555
  30.9 0.8 %own_part.9.part = f32[5,4,2048]{2,1,0:T(4,128)S(1)} custom-call(s32[6,16]{1,0:T(8,128)S(4)} %get-tuple-element.68.table, f32[5,4,2048]{2,1,0:T(4,128)S(1)} %get-tuple-element.97.field, f32[5,4,2048]{2,1,0:T(4,128)S(1)} %get-tuple-element.98.goal, f32[5,5,6,2048]{3,2,1,0:T(8,128)S(1)} %get-tuple-element.72.jacobian, ...), custom_call_target="tpu_custom_call" | custom-call | flops 1 | bytes 1 | tf_op jit(solution)/shard_map/own_part/pallas_call | solution.py:35
  33.3 3.0 %collective-permute-start.12 = (f32[8,5,4,128]{3,2,1,0:T(4,128)S(1)}, f32[8,5,4,128]{3,2,1,0:T(4,128)S(1)}, u32[]{:S(2)}, u32[]{:S(2)}) collective-permute-start(f32[8,5,4,128]{3,2,1,0:T(4,128)S(1)} %get-tuple-element.105.faces), channel_id=1, source_target_pairs={{0,1},{2,3},{4,5},{6,7},{1,0},{3,2},{5,4},{7,6},{8,9},{10,11},{12,... | collective-permute-start | bytes 245768 | tf_op jit(solution)/shard_map/ppermute | solution.py:555
  36.6 0.8 %own_part.10.part = f32[5,4,2048]{2,1,0:T(4,128)S(1)} custom-call(s32[6,16]{1,0:T(8,128)S(4)} %get-tuple-element.68.table, f32[5,4,2048]{2,1,0:T(4,128)S(1)} %get-tuple-element.104.field, f32[5,4,2048]{2,1,0:T(4,128)S(1)} %get-tuple-element.98.goal, f32[5,5,6,2048]{3,2,1,0:T(8,128)S(1)} %get-tuple-element.72.jacobian, ...), custom_call_target="tpu_custom_call" | custom-call | flops 1 | bytes 1 | tf_op jit(solution)/shard_map/own_part/pallas_call | solution.py:35
  38.6 1.7 %collective-permute-start.17 = (f32[5,2,3072]{2,1,0:T(2,128)S(1)}, f32[5,2,3072]{2,1,0:T(2,128)S(1)}, u32[]{:S(2)}, u32[]{:S(2)}) collective-permute-start(f32[5,2,3072]{2,1,0:T(2,128)S(1)} %get-tuple-element.115), channel_id=1, source_target_pairs={{0,8},{8,16},{16,24},{24,0},{1,9},{9,17},{17,25},{25,1},{2,10},{10... | collective-permute-start | bytes 368648 | tf_op jit(solution)/shard_map/ppermute | solution.py:560
  40.3 2.1 %collective-permute-done.14.tail = f32[5,2,3072]{2,1,0:T(2,128)S(1)} collective-permute-done((f32[5,2,3072]{2,1,0:T(2,128)S(1)}, f32[5,2,3072]{2,1,0:T(2,128)S(1)}, u32[]{:S(2)}, u32[]{:S(2)}) %collective-permute-start.14) | collective-permute-done | bytes 122912 | tf_op jit(solution)/shard_map/ppermute | solution.py:560
  42.8 0.8 %own_part.11.part = f32[5,4,2048]{2,1,0:T(4,128)S(1)} custom-call(s32[6,16]{1,0:T(8,128)S(4)} %get-tuple-element.68.table, f32[5,4,2048]{2,1,0:T(4,128)S(1)} %get-tuple-element.110.field, f32[5,4,2048]{2,1,0:T(4,128)S(1)} %get-tuple-element.98.goal, f32[5,5,6,2048]{3,2,1,0:T(8,128)S(1)} %get-tuple-element.72.jacobian, ...), custom_call_target="tpu_custom_call" | custom-call | flops 1 | bytes 1 | tf_op jit(solution)/shard_map/own_part/pallas_call | solution.py:35
  45.7 2.7 %collective-permute-start.18 = (f32[8,5,16,128]{3,2,1,0:T(8,128)S(1)}, f32[8,5,16,128]{3,2,1,0:T(8,128)S(1)}, u32[]{:S(2)}, u32[]{:S(2)}) collective-permute-start(f32[8,5,16,128]{3,2,1,0:T(8,128)S(1)} %get-tuple-element.117.faces), channel_id=1, source_target_pairs={{0,1},{2,3},{4,5},{6,7},{1,0},{3,2},{5,4},{7,6},{8,9},{10,11},{12,... | collective-permute-start | bytes 983048 | tf_op jit(solution)/shard_map/ppermute | solution.py:555
  48.9 1.5 %own_part.12.part = f32[5,16,2048]{2,1,0:T(8,128)S(1)} custom-call(s32[6,16]{1,0:T(8,128)S(4)} %get-tuple-element.68.table, f32[5,16,2048]{2,1,0:T(8,128)S(1)} %get-tuple-element.116.field, f32[5,16,2048]{2,1,0:T(8,128)S(1)} %get-tuple-element.71.goal, f32[5,5,6,2048]{3,2,1,0:T(8,128)S(1)} %get-tuple-element.72.jacobian, ...), custom_call_target="tpu_custom_call" | custom-call | flops 1 | bytes 1 | tf_op jit(solution)/shard_map/own_part/pallas_call | solution.py:35
  50.7 0.7 collective-permute-start.22
  51.9 2.9 %collective-permute-done.20.tail = f32[5,2,3072]{2,1,0:T(2,128)S(1)} collective-permute-done((f32[5,2,3072]{2,1,0:T(2,128)S(1)}, f32[5,2,3072]{2,1,0:T(2,128)S(1)}, u32[]{:S(2)}, u32[]{:S(2)}) %collective-permute-start.20) | collective-permute-done | bytes 122912 | tf_op jit(solution)/shard_map/ppermute | solution.py:560
  55.3 1.4 %collective-permute-start.23 = (f32[5,2,3072]{2,1,0:T(2,128)S(1)}, f32[5,2,3072]{2,1,0:T(2,128)S(1)}, u32[]{:S(2)}, u32[]{:S(2)}) collective-permute-start(f32[5,2,3072]{2,1,0:T(2,128)S(1)} %get-tuple-element.127), channel_id=1, source_target_pairs={{0,8},{8,16},{16,24},{24,0},{1,9},{9,17},{17,25},{25,1},{2,10},{10... | collective-permute-start | bytes 368648 | tf_op jit(solution)/shard_map/ppermute | solution.py:560
  56.6 1.5 %own_part.13.part = f32[5,16,2048]{2,1,0:T(8,128)S(1)} custom-call(s32[6,16]{1,0:T(8,128)S(4)} %get-tuple-element.68.table, f32[5,16,2048]{2,1,0:T(8,128)S(1)} %get-tuple-element.122.field, f32[5,16,2048]{2,1,0:T(8,128)S(1)} %get-tuple-element.71.goal, f32[5,5,6,2048]{3,2,1,0:T(8,128)S(1)} %get-tuple-element.72.jacobian, ...), custom_call_target="tpu_custom_call" | custom-call | flops 1 | bytes 1 | tf_op jit(solution)/shard_map/own_part/pallas_call | solution.py:35
  59.6 2.1 %collective-permute-done.23.tail = f32[5,2,3072]{2,1,0:T(2,128)S(1)} collective-permute-done((f32[5,2,3072]{2,1,0:T(2,128)S(1)}, f32[5,2,3072]{2,1,0:T(2,128)S(1)}, u32[]{:S(2)}, u32[]{:S(2)}) %collective-permute-start.23) | collective-permute-done | bytes 122912 | tf_op jit(solution)/shard_map/ppermute | solution.py:560
  62.4 1.0 %collective-permute-start.26 = (f32[5,2,3072]{2,1,0:T(2,128)S(1)}, f32[5,2,3072]{2,1,0:T(2,128)S(1)}, u32[]{:S(2)}, u32[]{:S(2)}) collective-permute-start(f32[5,2,3072]{2,1,0:T(2,128)S(1)} %get-tuple-element.133), channel_id=1, source_target_pairs={{0,8},{8,16},{16,24},{24,0},{1,9},{9,17},{17,25},{25,1},{2,10},{10... | collective-permute-start | bytes 368648 | tf_op jit(solution)/shard_map/ppermute | solution.py:560
  63.4 1.5 %last_own_part.1 = (f32[5,16,2048]{2,1,0:T(8,128)S(1)}, f32[5,16,2048]{2,1,0:T(8,128)}) custom-call(s32[6,16]{1,0:T(8,128)S(4)} %get-tuple-element.68.table, f32[5,16,2048]{2,1,0:T(8,128)S(1)} %get-tuple-element.128.field, f32[5,16,2048]{2,1,0:T(8,128)S(1)} %get-tuple-element.71.goal, f32[5,5,6,2048]{3,2,1,0:T(8,128)S(1)} %get-tuple-element.72.jacobian, ...), custom_call_target="tpu_custom_call" | custom-call | flops 1 | bytes 1 | tf_op jit(solution)/shard_map/last_own_part/pallas_call | solution.py:35
  65.1 3.6 %collective-permute-done.26.tail = f32[5,2,3072]{2,1,0:T(2,128)S(1)} collective-permute-done((f32[5,2,3072]{2,1,0:T(2,128)S(1)}, f32[5,2,3072]{2,1,0:T(2,128)S(1)}, u32[]{:S(2)}, u32[]{:S(2)}) %collective-permute-start.26) | collective-permute-done | bytes 122912 | tf_op jit(solution)/shard_map/ppermute | solution.py:560
  68.9 1.1 %residual.1 = f32[5,16,2048]{2,1,0:T(8,128)} custom-call(s32[6,16]{1,0:T(8,128)S(4)} %get-tuple-element.68.table, f32[5,16,2048]{2,1,0:T(8,128)S(1)} %beside_part.1.part, f32[8,5,16,128]{3,2,1,0:T(8,128)S(1)} %rim.5, f32[5,2,3072]{2,1,0:T(2,128)S(1)} %collective-permute-done.26.tail, f32[2,5,5,2048]{3,2,1,0:T(8,128)S(1)} %get-tuple-element.76.rim_jacobian), custom_call_target="tpu_custom_call" | custom-call | flops 1 | bytes 1 | tf_op jit(solution)/shard_map/residual/pallas_call | solution.py:35
  (69 shorter events, 15.4 us)
Async XLA Ops:
  2.6 5.4 %collective-permute-start = (f32[8,5,16,128]{3,2,1,0:T(8,128)S(1)}, f32[8,5,16,128]{3,2,1,0:T(8,128)S(1)}, u32[]{:S(2)}, u32[]{:S(2)}) collective-permute-start(f32[8,5,16,128]{3,2,1,0:T(8,128)S(1)} %get-tuple-element.75.faces), channel_id=1, source_target_pairs={{0,1},{2,3},{4,5},{6,7},{1,0},{3,2},{5,4},{7,6},{8,9},{10,11},{12,... | collective-permute-start | bytes 983048 | tf_op jit(solution)/shard_map/ppermute | solution.py:555
  3.1 7.5 %collective-permute-start.2 = (f32[8,5,16,128]{3,2,1,0:T(8,128)S(1)}, f32[8,5,16,128]{3,2,1,0:T(8,128)S(1)}, u32[]{:S(2)}, u32[]{:S(2)}) collective-permute-start(f32[8,5,16,128]{3,2,1,0:T(8,128)S(1)} %get-tuple-element.75.faces), channel_id=1, source_target_pairs={{1,2},{3,4},{5,6},{2,1},{4,3},{6,5},{9,10},{11,12},{13,14},{10,9},... | collective-permute-start | bytes 983048 | tf_op jit(solution)/shard_map/ppermute | solution.py:551
  3.8 6.8 %collective-permute-start.1 = (f32[5,2,4096]{2,1,0:T(2,128)S(1)}, f32[5,2,4096]{2,1,0:T(2,128)S(1)}, u32[]{:S(2)}, u32[]{:S(2)}) collective-permute-start(f32[5,2,4096]{2,1,0:T(2,128)S(1)} %tail.1), channel_id=1, source_target_pairs={{0,8},{8,16},{16,24},{24,0},{1,9},{9,17},{17,25},{25,1},{2,10},{10... | collective-permute-start | bytes 491528 | tf_op jit(solution)/shard_map/ppermute | solution.py:560
  8.4 10.0 %collective-permute-start.4 = (f32[8,120,128]{2,1,0:T(8,128)S(1)}, f32[8,120,128]{2,1,0:T(8,128)S(1)}, u32[]{:S(2)}, u32[]{:S(2)}) collective-permute-start(f32[8,120,128]{2,1,0:T(8,128)S(1)} %get-tuple-element.84), channel_id=1, source_target_pairs={{1,2},{3,4},{5,6},{2,1},{4,3},{6,5},{9,10},{11,12},{13,14},{10,9},... | collective-permute-start | bytes 1474568 | tf_op jit(solution)/shard_map/ppermute | solution.py:551
  11.1 6.2 %collective-permute-start.3 = (f32[8,5,16,128]{3,2,1,0:T(8,128)S(1)}, f32[8,5,16,128]{3,2,1,0:T(8,128)S(1)}, u32[]{:S(2)}, u32[]{:S(2)}) collective-permute-start(f32[8,5,16,128]{3,2,1,0:T(8,128)S(1)} %get-tuple-element.82.faces), channel_id=1, source_target_pairs={{0,1},{2,3},{4,5},{6,7},{1,0},{3,2},{5,4},{7,6},{8,9},{10,11},{12,... | collective-permute-start | bytes 983048 | tf_op jit(solution)/shard_map/ppermute | solution.py:555
  14.3 6.2 %collective-permute-start.5 = (f32[5,2,3072]{2,1,0:T(2,128)S(1)}, f32[5,2,3072]{2,1,0:T(2,128)S(1)}, u32[]{:S(2)}, u32[]{:S(2)}) collective-permute-start(f32[5,2,3072]{2,1,0:T(2,128)S(1)} %get-tuple-element.87), channel_id=1, source_target_pairs={{0,8},{8,16},{16,24},{24,0},{1,9},{9,17},{17,25},{25,1},{2,10},{10... | collective-permute-start | bytes 368648 | tf_op jit(solution)/shard_map/ppermute | solution.py:560
  17.7 9.0 %collective-permute-start.7 = (f32[8,5,6,128]{3,2,1,0:T(8,128)S(1)}, f32[8,5,6,128]{3,2,1,0:T(8,128)S(1)}, u32[]{:S(2)}, u32[]{:S(2)}) collective-permute-start(f32[8,5,6,128]{3,2,1,0:T(8,128)S(1)} %get-tuple-element.85.next_message), channel_id=1, source_target_pairs={{1,2},{3,4},{5,6},{2,1},{4,3},{6,5},{9,10},{11,12},{13,14},{10,9},... | collective-permute-start | bytes 368648 | tf_op jit(solution)/shard_map/ppermute | solution.py:551
  20.9 4.9 %collective-permute-start.6 = (f32[8,5,4,128]{3,2,1,0:T(4,128)S(1)}, f32[8,5,4,128]{3,2,1,0:T(4,128)S(1)}, u32[]{:S(2)}, u32[]{:S(2)}) collective-permute-start(f32[8,5,4,128]{3,2,1,0:T(4,128)S(1)} %get-tuple-element.90.faces), channel_id=1, source_target_pairs={{0,1},{2,3},{4,5},{6,7},{1,0},{3,2},{5,4},{7,6},{8,9},{10,11},{12,... | collective-permute-start | bytes 245768 | tf_op jit(solution)/shard_map/ppermute | solution.py:555
  22.4 6.2 %collective-permute-start.8 = (f32[5,2,3072]{2,1,0:T(2,128)S(1)}, f32[5,2,3072]{2,1,0:T(2,128)S(1)}, u32[]{:S(2)}, u32[]{:S(2)}) collective-permute-start(f32[5,2,3072]{2,1,0:T(2,128)S(1)} %get-tuple-element.96), channel_id=1, source_target_pairs={{0,8},{8,16},{16,24},{24,0},{1,9},{9,17},{17,25},{25,1},{2,10},{10... | collective-permute-start | bytes 368648 | tf_op jit(solution)/shard_map/ppermute | solution.py:560
  26.0 6.8 %collective-permute-start.10 = (f32[16,5,4,128]{3,2,1,0:T(4,128)S(1)}, f32[16,5,4,128]{3,2,1,0:T(4,128)S(1)}, u32[]{:S(2)}, u32[]{:S(2)}) collective-permute-start(f32[16,5,4,128]{3,2,1,0:T(4,128)S(1)} %get-tuple-element.101), channel_id=1, source_target_pairs={{1,2},{3,4},{5,6},{2,1},{4,3},{6,5},{9,10},{11,12},{13,14},{10,9},... | collective-permute-start | bytes 491528 | tf_op jit(solution)/shard_map/ppermute | solution.py:551
  27.1 6.0 %collective-permute-start.11 = (f32[5,2,3072]{2,1,0:T(2,128)S(1)}, f32[5,2,3072]{2,1,0:T(2,128)S(1)}, u32[]{:S(2)}, u32[]{:S(2)}) collective-permute-start(f32[5,2,3072]{2,1,0:T(2,128)S(1)} %get-tuple-element.103), channel_id=1, source_target_pairs={{0,8},{8,16},{16,24},{24,0},{1,9},{9,17},{17,25},{25,1},{2,10},{10... | collective-permute-start | bytes 368648 | tf_op jit(solution)/shard_map/ppermute | solution.py:560
  28.9 3.0 %collective-permute-start.9 = (f32[8,5,4,128]{3,2,1,0:T(4,128)S(1)}, f32[8,5,4,128]{3,2,1,0:T(4,128)S(1)}, u32[]{:S(2)}, u32[]{:S(2)}) collective-permute-start(f32[8,5,4,128]{3,2,1,0:T(4,128)S(1)} %get-tuple-element.99.faces), channel_id=1, source_target_pairs={{0,1},{2,3},{4,5},{6,7},{1,0},{3,2},{5,4},{7,6},{8,9},{10,11},{12,... | collective-permute-start | bytes 245768 | tf_op jit(solution)/shard_map/ppermute | solution.py:555
  32.0 6.2 %collective-permute-start.13 = (f32[16,5,4,128]{3,2,1,0:T(4,128)S(1)}, f32[16,5,4,128]{3,2,1,0:T(4,128)S(1)}, u32[]{:S(2)}, u32[]{:S(2)}) collective-permute-start(f32[16,5,4,128]{3,2,1,0:T(4,128)S(1)} %get-tuple-element.107), channel_id=1, source_target_pairs={{1,2},{3,4},{5,6},{2,1},{4,3},{6,5},{9,10},{11,12},{13,14},{10,9},... | collective-permute-start | bytes 491528 | tf_op jit(solution)/shard_map/ppermute | solution.py:551
  33.3 4.1 %collective-permute-start.12 = (f32[8,5,4,128]{3,2,1,0:T(4,128)S(1)}, f32[8,5,4,128]{3,2,1,0:T(4,128)S(1)}, u32[]{:S(2)}, u32[]{:S(2)}) collective-permute-start(f32[8,5,4,128]{3,2,1,0:T(4,128)S(1)} %get-tuple-element.105.faces), channel_id=1, source_target_pairs={{0,1},{2,3},{4,5},{6,7},{1,0},{3,2},{5,4},{7,6},{8,9},{10,11},{12,... | collective-permute-start | bytes 245768 | tf_op jit(solution)/shard_map/ppermute | solution.py:555
  36.3 6.2 %collective-permute-start.14 = (f32[5,2,3072]{2,1,0:T(2,128)S(1)}, f32[5,2,3072]{2,1,0:T(2,128)S(1)}, u32[]{:S(2)}, u32[]{:S(2)}) collective-permute-start(f32[5,2,3072]{2,1,0:T(2,128)S(1)} %get-tuple-element.109), channel_id=1, source_target_pairs={{0,8},{8,16},{16,24},{24,0},{1,9},{9,17},{17,25},{25,1},{2,10},{10... | collective-permute-start | bytes 368648 | tf_op jit(solution)/shard_map/ppermute | solution.py:560
  37.6 7.4 %collective-permute-start.16 = (f32[16,5,4,128]{3,2,1,0:T(4,128)S(1)}, f32[16,5,4,128]{3,2,1,0:T(4,128)S(1)}, u32[]{:S(2)}, u32[]{:S(2)}) collective-permute-start(f32[16,5,4,128]{3,2,1,0:T(4,128)S(1)} %get-tuple-element.113), channel_id=1, source_target_pairs={{1,2},{3,4},{5,6},{2,1},{4,3},{6,5},{9,10},{11,12},{13,14},{10,9},... | collective-permute-start | bytes 491528 | tf_op jit(solution)/shard_map/ppermute | solution.py:551
  38.6 6.9 %collective-permute-start.17 = (f32[5,2,3072]{2,1,0:T(2,128)S(1)}, f32[5,2,3072]{2,1,0:T(2,128)S(1)}, u32[]{:S(2)}, u32[]{:S(2)}) collective-permute-start(f32[5,2,3072]{2,1,0:T(2,128)S(1)} %get-tuple-element.115), channel_id=1, source_target_pairs={{0,8},{8,16},{16,24},{24,0},{1,9},{9,17},{17,25},{25,1},{2,10},{10... | collective-permute-start | bytes 368648 | tf_op jit(solution)/shard_map/ppermute | solution.py:560
  42.7 1.3 %collective-permute-start.15 = (f32[8,5,4,128]{3,2,1,0:T(4,128)S(1)}, f32[8,5,4,128]{3,2,1,0:T(4,128)S(1)}, u32[]{:S(2)}, u32[]{:S(2)}) collective-permute-start(f32[8,5,4,128]{3,2,1,0:T(4,128)S(1)} %get-tuple-element.111.faces), channel_id=1, source_target_pairs={{0,1},{2,3},{4,5},{6,7},{1,0},{3,2},{5,4},{7,6},{8,9},{10,11},{12,... | collective-permute-start | bytes 245768 | tf_op jit(solution)/shard_map/ppermute | solution.py:555
  44.3 7.1 %collective-permute-start.19 = (f32[9,5,16,128]{3,2,1,0:T(8,128)S(1)}, f32[9,5,16,128]{3,2,1,0:T(8,128)S(1)}, u32[]{:S(2)}, u32[]{:S(2)}) collective-permute-start(f32[9,5,16,128]{3,2,1,0:T(8,128)S(1)} %get-tuple-element.119), channel_id=1, source_target_pairs={{1,2},{3,4},{5,6},{2,1},{4,3},{6,5},{9,10},{11,12},{13,14},{10,9},... | collective-permute-start | bytes 1105928 | tf_op jit(solution)/shard_map/ppermute | solution.py:551
  45.7 4.6 %collective-permute-start.18 = (f32[8,5,16,128]{3,2,1,0:T(8,128)S(1)}, f32[8,5,16,128]{3,2,1,0:T(8,128)S(1)}, u32[]{:S(2)}, u32[]{:S(2)}) collective-permute-start(f32[8,5,16,128]{3,2,1,0:T(8,128)S(1)} %get-tuple-element.117.faces), channel_id=1, source_target_pairs={{0,1},{2,3},{4,5},{6,7},{1,0},{3,2},{5,4},{7,6},{8,9},{10,11},{12,... | collective-permute-start | bytes 983048 | tf_op jit(solution)/shard_map/ppermute | solution.py:555
  48.4 6.4 %collective-permute-start.20 = (f32[5,2,3072]{2,1,0:T(2,128)S(1)}, f32[5,2,3072]{2,1,0:T(2,128)S(1)}, u32[]{:S(2)}, u32[]{:S(2)}) collective-permute-start(f32[5,2,3072]{2,1,0:T(2,128)S(1)} %get-tuple-element.121), channel_id=1, source_target_pairs={{0,8},{8,16},{16,24},{24,0},{1,9},{9,17},{17,25},{25,1},{2,10},{10... | collective-permute-start | bytes 368648 | tf_op jit(solution)/shard_map/ppermute | solution.py:560
  50.7 8.5 %collective-permute-start.22 = (f32[9,5,16,128]{3,2,1,0:T(8,128)S(1)}, f32[9,5,16,128]{3,2,1,0:T(8,128)S(1)}, u32[]{:S(2)}, u32[]{:S(2)}) collective-permute-start(f32[9,5,16,128]{3,2,1,0:T(8,128)S(1)} %get-tuple-element.125), channel_id=1, source_target_pairs={{1,2},{3,4},{5,6},{2,1},{4,3},{6,5},{9,10},{11,12},{13,14},{10,9},... | collective-permute-start | bytes 1105928 | tf_op jit(solution)/shard_map/ppermute | solution.py:551
  55.0 3.0 %collective-permute-start.21 = (f32[8,5,16,128]{3,2,1,0:T(8,128)S(1)}, f32[8,5,16,128]{3,2,1,0:T(8,128)S(1)}, u32[]{:S(2)}, u32[]{:S(2)}) collective-permute-start(f32[8,5,16,128]{3,2,1,0:T(8,128)S(1)} %get-tuple-element.123.faces), channel_id=1, source_target_pairs={{0,1},{2,3},{4,5},{6,7},{1,0},{3,2},{5,4},{7,6},{8,9},{10,11},{12,... | collective-permute-start | bytes 983048 | tf_op jit(solution)/shard_map/ppermute | solution.py:555
  55.3 6.5 %collective-permute-start.23 = (f32[5,2,3072]{2,1,0:T(2,128)S(1)}, f32[5,2,3072]{2,1,0:T(2,128)S(1)}, u32[]{:S(2)}, u32[]{:S(2)}) collective-permute-start(f32[5,2,3072]{2,1,0:T(2,128)S(1)} %get-tuple-element.127), channel_id=1, source_target_pairs={{0,8},{8,16},{16,24},{24,0},{1,9},{9,17},{17,25},{25,1},{2,10},{10... | collective-permute-start | bytes 368648 | tf_op jit(solution)/shard_map/ppermute | solution.py:560
  58.4 10.2 %collective-permute-start.25 = (f32[9,5,16,128]{3,2,1,0:T(8,128)S(1)}, f32[9,5,16,128]{3,2,1,0:T(8,128)S(1)}, u32[]{:S(2)}, u32[]{:S(2)}) collective-permute-start(f32[9,5,16,128]{3,2,1,0:T(8,128)S(1)} %get-tuple-element.132), channel_id=1, source_target_pairs={{1,2},{3,4},{5,6},{2,1},{4,3},{6,5},{9,10},{11,12},{13,14},{10,9},... | collective-permute-start | bytes 1105928 | tf_op jit(solution)/shard_map/ppermute | solution.py:551
  62.0 2.9 %collective-permute-start.24 = (f32[8,5,16,128]{3,2,1,0:T(8,128)S(1)}, f32[8,5,16,128]{3,2,1,0:T(8,128)S(1)}, u32[]{:S(2)}, u32[]{:S(2)}) collective-permute-start(f32[8,5,16,128]{3,2,1,0:T(8,128)S(1)} %get-tuple-element.131), channel_id=1, source_target_pairs={{0,1},{2,3},{4,5},{6,7},{1,0},{3,2},{5,4},{7,6},{8,9},{10,11},{12,... | collective-permute-start | bytes 983048 | tf_op jit(solution)/shard_map/ppermute | solution.py:555
  62.4 6.3 %collective-permute-start.26 = (f32[5,2,3072]{2,1,0:T(2,128)S(1)}, f32[5,2,3072]{2,1,0:T(2,128)S(1)}, u32[]{:S(2)}, u32[]{:S(2)}) collective-permute-start(f32[5,2,3072]{2,1,0:T(2,128)S(1)} %get-tuple-element.133), channel_id=1, source_target_pairs={{0,8},{8,16},{16,24},{24,0},{1,9},{9,17},{17,25},{25,1},{2,10},{10... | collective-permute-start | bytes 368648 | tf_op jit(solution)/shard_map/ppermute | solution.py:560
